TPU v7x, 256 devices: a whole 4x4x8 slice. The times are simulated.
256 devices in a mesh: sx: 8 (over y, x_hi), sy: 2 (over x_lo), snap: 16 (over z, core).
Axes of the slice: x: 4 (x_hi: 2, x_lo: 2; x = x_hi * 2 + x_lo), y: 4, z: 8, core: 2. Of those that a mesh axis runs over, the one named last changes fastest.
Arguments:
- snapshots: float32 [32, 8, 64, 4096], P('sx', 'sy', None, 'snap'), may hold values from -6 to 6
- links: int32 [32, 8, 9], P('sx', 'sy'), may hold values from 0 to 8, each once within a row
- mass: float32 [32, 8, 9, 4096], P('sx', 'sy'), may hold values from -0.25 to 0.25
Outputs:
- weighted: float32 [32, 8, 64, 4096], P('sx', 'sy', None, 'snap')
- gram: float32 [4096, 4096], P('snap', ('sx', 'sy'))
All inputs are finite; a program needn't handle non-finite values.
Results may differ from a plain program's by a relative error of at most 0.0001.
Values sent between devices are 32-bit elements; how exact they have to be, the bound alone decides.
No kernel may reach another device: no remote copies, remote signals or barrier semaphores. Data moves between devices by JAX's collectives and lax.ppermute only.
A program may use at most 128 MiB of HBM per device.

v0:
```python
import jax
import jax.numpy as jnp
from jax import lax
from jax.sharding import PartitionSpec as P

NEIGH = 9


def extended(cells, sides, width):
    for axis, dim in sides:
        count = lax.axis_size(axis)
        ends = count - 1
        head = lax.slice_in_dim(cells, 0, width, axis=dim)
        tail = lax.slice_in_dim(cells, cells.shape[dim] - width, cells.shape[dim], axis=dim)
        cells = jnp.concatenate(
            [
                lax.ppermute(tail, axis, [(i, (i + 1) % count) for i in range(ends)]),
                cells,
                lax.ppermute(head, axis, [((i + 1) % count, i) for i in range(ends)]),
            ],
            axis=dim,
        )
    return cells


def pair_tile(left, right):
    return lax.dot_general(
        left,
        right,
        (((0,), (0,)), ((), ())),
        precision=lax.Precision.HIGHEST,
        preferred_element_type=jnp.float32,
    )


def body(snapshots, links, mass):
    grid_x, grid_y, block_len, snap_cols = snapshots.shape
    blocks = mass.reshape(grid_x, grid_y, NEIGH, block_len, block_len)
    padded = extended(snapshots, (("sx", 0), ("sy", 1)), 1)
    weighted = jnp.zeros(snapshots.shape, jnp.float32)
    for offset in range(NEIGH):
        shift_x = offset // 3 - 1
        shift_y = offset % 3 - 1
        view = padded[1 + shift_x : 1 + shift_x + grid_x, 1 + shift_y : 1 + shift_y + grid_y]
        chosen = jnp.sum(
            jnp.where((links == offset)[:, :, :, None, None], blocks, jnp.float32(0.0)), axis=2
        )
        weighted = weighted + jnp.einsum(
            "abij,abjs->abis", chosen, view, precision=lax.Precision.HIGHEST
        )
    flattened = weighted.reshape(grid_x * grid_y * block_len, snap_cols)
    nodes_all = grid_x * grid_y * block_len * lax.axis_size("sx") * lax.axis_size("sy")
    row_sums = pair_tile(flattened, lax.all_gather(flattened, "snap", axis=1, tiled=True))
    gram = lax.psum_scatter(row_sums, ("sx", "sy"), scatter_dimension=1, tiled=True) / jnp.float32(
        nodes_all
    )
    return (weighted, gram)


def solution(mesh):
    placed = (P("sx", "sy", None, "snap"), P("sx", "sy", None), P("sx", "sy", None, None))
    return jax.shard_map(
        body,
        mesh=mesh,
        in_specs=placed,
        out_specs=(P("sx", "sy", None, "snap"), P("snap", ("sx", "sy"))),
        check_vma=False,
    )
```

profile of v0, /device:TPU:2, one launch (start us, length us, event | category | flops | bytes accessed | tf_op | source)
XLA Modules:
  0.0 270.1 jit_solution(13958149347179629260)
XLA Ops:
  7.2 0.0 all-gather.2.cloned.1.call-start
  7.2 1.9 fusion.33
  9.1 1.3 collective-permute-start.1
  10.4 6.8 %collective-permute-start = (f32[1,4,64,256]{3,2,1,0:T(8,128)}, f32[1,4,64,256]{3,2,1,0:T(8,128)}, u32[]{:S(2)}, u32[]{:S(2)}) collective-permute-start(f32[1,4,64,256]{3,2,1,0:T(8,128)} %get-tuple-element.14), channel_id=1, source_target_pairs={{0,32},{32,64},{64,96},{96,128},{128,160},{160,192},{192,224},{1,3... | collective-permute-start | bytes 786440 | tf_op jit(solution)/shard_map/ppermute | solution.py:17
  17.1 0.7 broadcast_compare_fusion.1
  17.9 0.1 copy.12
  18.0 0.1 copy.11
  18.1 0.1 copy.10
  18.3 0.1 copy.9
  18.4 0.1 copy.8
  18.5 0.1 copy.7
  18.6 0.1 copy.6
  18.8 0.1 copy.5
  18.9 0.1 copy.13
  19.0 0.0 copy-start
  19.0 8.6 %select_reduce_fusion.3 = (f32[4,4,4096]{2,1,0:T(4,128)}, f32[4,4,4096]{2,1,0:T(4,128)S(1)}, f32[4,4,4096]{2,1,0:T(4,128)S(1)}, f32[4,4,4096]{2,1,0:T(4,128)S(1)...) fusion(f32[4,4,9,4096]{3,1,2,0:T(4,128)} %param.5, ...), kind=kLoop, calls=%fused_computation.7 | loop fusion | flops 10027008 | bytes 4719888 | tf_op jit(solution)/shard_map/reduce_sum | solution.py:45
  27.6 0.3 reduce_sum.108
  27.9 0.0 copy-done
  27.9 1.0 fusion.34
  29.0 2.0 reduce_sum.110
  31.0 0.3 reduce_sum.112
  31.3 1.1 reduce_sum.106
  32.4 1.2 reduce_sum.104
  33.6 2.1 reduce_sum.102
  35.7 2.1 reduce_sum.100
  37.7 2.0 reduce_sum.116
  39.8 1.1 reduce_sum.114
  40.9 0.0 collective-permute-done
  40.9 1.0 constant_dynamic-update-slice_fusion.2
  41.8 0.0 copy-start.3
  41.9 0.1 constant_dynamic-update-slice_fusion.1
  41.9 0.0 collective-permute-done.1
  41.9 1.0 constant_dynamic-update-slice_fusion
  43.0 0.0 copy-start.4
  43.0 0.1 fusion.32
  43.0 1.4 collective-permute-start.2
  44.5 4.8 %collective-permute-start.3 = (f32[6,1,64,256]{3,2,1,0:T(8,128)S(1)}, f32[6,1,64,256]{3,2,1,0:T(8,128)S(1)}, u32[]{:S(2)}, u32[]{:S(2)}) collective-permute-start(f32[6,1,64,256]{3,2,1,0:T(8,128)S(1)} %get-tuple-element.12), channel_id=1, source_target_pairs={{16,0},{17,1},{18,2},{19,3},{20,4},{21,5},{22,6},{23,7},{24,8},{25... | collective-permute-start | bytes 1179656 | tf_op jit(solution)/shard_map/ppermute | solution.py:19
  49.3 0.0 copy-done.3
  49.3 2.0 fusion.22
  51.2 0.0 copy-done.4
  51.2 2.0 fusion.18
  53.2 0.0 copy-start.1
  53.2 2.1 collective-permute-done.2
  55.4 1.0 fusion.20
  56.4 0.0 copy-done.1
  56.4 1.0 fusion.12
  57.4 0.0 copy-start.2
  57.5 0.0 collective-permute-done.3
  57.5 1.0 fusion.9
  58.5 0.0 copy-done.2
  58.5 0.0 copy-start.6
  58.5 1.0 fusion.16
  59.6 0.0 copy-done.6
  59.6 0.0 copy-start.5
  59.6 1.3 fusion.5
  60.9 0.0 copy-done.5
  60.9 2.2 fusion.2
  63.1 0.0 all-gather.2.cloned.1.call-update
  63.1 0.3 reduce-scatter.2.cloned.1.call-start
  63.4 99.1 %all-gather.2.cloned.1.call-done = f32[1024,4096]{1,0:T(8,128)} async-done(((f32[1024,256]{1,0:T(8,128)}), f32[1024,4096]{1,0:T(8,128)}) %all-gather.2.cloned.1.call-update) | async-done | bytes 16777232 | tf_op jit(solution)/shard_map/all_gather | solution.py:53
  162.5 18.0 %fusion.35 = f32[256,4096]{1,0:T(8,128)} fusion(f32[1024,256]{1,0:T(8,128)} %bitcast.14, f32[1024,4096]{1,0:T(8,128)} %all-gather.2.cloned.1.call-done), kind=kOutput, calls=%fused_computation.67 | convolution fusion | flops 12884901888 | bytes 22020096 | tf_op jit(solution)/shard_map/dot_general | solution.py:27
  180.5 0.0 reduce-scatter.2.cloned.1.call-update
  180.5 81.1 %reduce-scatter.2.cloned.1.call-done = f32[256,256]{1,0:T(8,128)} async-done(((f32[256,4096]{1,0:T(8,128)}), f32[256,256]{1,0:T(8,128)}) %reduce-scatter.2.cloned.1.call-update) | async-done | bytes 262160 | tf_op jit(solution)/shard_map/reduce_scatter | solution.py:54
  261.6 1.7 broadcast_multiply_fusion
Async XLA Ops:
  7.2 155.4 %all-gather.2.cloned.1.call-start = ((), (), s32[]{:S(2)}) async-start(), calls=%async_computation.1 | async-start | bytes 17825792 | tf_op jit(solution)/shard_map/all_gather | solution.py:53
  9.1 32.9 %collective-permute-start.1 = (f32[1,4,64,256]{3,2,1,0:T(8,128)}, f32[1,4,64,256]{3,2,1,0:T(8,128)}, u32[]{:S(2)}, u32[]{:S(2)}) collective-permute-start(f32[1,4,64,256]{3,2,1,0:T(8,128)} %get-tuple-element.13), channel_id=1, source_target_pairs={{32,0},{64,32},{96,64},{128,96},{160,128},{192,160},{224,192},{33,... | collective-permute-start | bytes 786440 | tf_op jit(solution)/shard_map/ppermute | solution.py:19
  10.4 30.5 %collective-permute-start = (f32[1,4,64,256]{3,2,1,0:T(8,128)}, f32[1,4,64,256]{3,2,1,0:T(8,128)}, u32[]{:S(2)}, u32[]{:S(2)}) collective-permute-start(f32[1,4,64,256]{3,2,1,0:T(8,128)} %get-tuple-element.14), channel_id=1, source_target_pairs={{0,32},{32,64},{64,96},{96,128},{128,160},{160,192},{192,224},{1,3... | collective-permute-start | bytes 786440 | tf_op jit(solution)/shard_map/ppermute | solution.py:17
  19.0 8.9 %copy-start = (f32[4,4,64,256]{3,2,1,0:T(8,128)S(1)}, f32[4,4,64,256]{3,2,1,0:T(8,128)}, u32[]{:S(2)}) copy-start(f32[4,4,64,256]{3,2,1,0:T(8,128)} %param.3) | copy-start | bytes 3145732
  41.8 7.4 %copy-start.3 = (f32[4,4,64,64]{3,2,1,0:T(8,128)S(1)}, f32[4,4,64,64]{3,2,1,0:T(8,128)}, u32[]{:S(2)}) copy-start(f32[4,4,64,64]{3,2,1,0:T(8,128)} %reduce_sum.102) | copy-start | bytes 786436
  43.0 8.3 %copy-start.4 = (f32[4,4,64,64]{3,2,1,0:T(8,128)S(1)}, f32[4,4,64,64]{3,2,1,0:T(8,128)}, u32[]{:S(2)}) copy-start(f32[4,4,64,64]{3,2,1,0:T(8,128)} %reduce_sum.114) | copy-start | bytes 786436
  43.0 12.3 %collective-permute-start.2 = (f32[6,1,64,256]{3,2,1,0:T(8,128)S(1)}, f32[6,1,64,256]{3,2,1,0:T(8,128)S(1)}, u32[]{:S(2)}, u32[]{:S(2)}) collective-permute-start(f32[6,1,64,256]{3,2,1,0:T(8,128)S(1)} %get-tuple-element.11), channel_id=1, source_target_pairs={{0,16},{1,17},{2,18},{3,19},{4,20},{5,21},{6,22},{7,23},{8,24},{9,... | collective-permute-start | bytes 1179656 | tf_op jit(solution)/shard_map/ppermute | solution.py:17
  44.5 13.0 %collective-permute-start.3 = (f32[6,1,64,256]{3,2,1,0:T(8,128)S(1)}, f32[6,1,64,256]{3,2,1,0:T(8,128)S(1)}, u32[]{:S(2)}, u32[]{:S(2)}) collective-permute-start(f32[6,1,64,256]{3,2,1,0:T(8,128)S(1)} %get-tuple-element.12), channel_id=1, source_target_pairs={{16,0},{17,1},{18,2},{19,3},{20,4},{21,5},{22,6},{23,7},{24,8},{25... | collective-permute-start | bytes 1179656 | tf_op jit(solution)/shard_map/ppermute | solution.py:19
  53.2 3.2 %copy-start.1 = (f32[4,4,64,64]{3,2,1,0:T(8,128)S(1)}, f32[4,4,64,64]{3,2,1,0:T(8,128)}, u32[]{:S(2)}) copy-start(f32[4,4,64,64]{3,2,1,0:T(8,128)} %reduce_sum.106) | copy-start | bytes 786436
  57.4 1.1 copy-start.2
  58.5 1.0 copy-start.6
  59.6 1.3 copy-start.5
  63.1 198.5 %reduce-scatter.2.cloned.1.call-start = ((), (), s32[]{:S(2)}) async-start(), calls=%async_computation.2 | async-start | bytes 4456448 | tf_op jit(solution)/shard_map/reduce_scatter | solution.py:54
Sparse Core Ops, SparseCore 0:
  63.2 99.2 all-gather.1
  180.6 80.8 reduce-scatter.1
where the time goes:
time: 271 us; the launch traced here: 270 us
  waiting for transfers between devices  182 us (67%)
  matrix products  30.5 us (11%)
  local copies, waits for them, and re-layouts  17.4 us (6%)
  starting transfers between devices  14.5 us (5%)
  between operations  14.3 us (5%)
  other arithmetic  11 us (4%)
    all_gather x1, waiting for transfers between devices, body(): lax.all_gather(flattened, 'snap', axis=1, tiled=True)  99.1 us
    reduce_scatter x1, waiting for transfers between devices, body(): lax.psum_scatter(row_sums, ('sx', 'sy'), scatter_dimension=1, tiled=True)  81.1 us
    dot_general x1, matrix products, pair_tile(): lax.dot_general(left, right, (((0,), (0,)), ((), ())), precision=lax.Prec...  18 us
    dot_general x9, matrix products, body(): jnp.einsum('abij,abjs->abis', chosen, view, precision=lax.Precision.HIGHEST)  12.6 us
    reduce_sum x9, local copies, waits for them, and re-layouts, body(): jnp.sum(jnp.where((links == offset)[:, :, :, None, None], blocks, jnp.flo...  12.2 us
    reduce_sum x1, other arithmetic, body(): jnp.sum(jnp.where((links == offset)[:, :, :, None, None], blocks, jnp.flo...  8.59 us
    ppermute x2, starting transfers between devices, extended(): lax.ppermute(tail, axis, [(i, (i + 1) % count) for i in range(ends)])  8.19 us
    ppermute x2, starting transfers between devices, extended(): lax.ppermute(head, axis, [((i + 1) % count, i) for i in range(ends)])  6.05 us
  transfers between devices with their start and end apart: 6, of which 3 were waited for; matrix products, arithmetic and copies ran while one was open for 11% of the time, Pallas kernels for 0%

commit v1 on v0

v1 whole, which is shorter than its diff:
```python
import jax
import jax.numpy as jnp
from jax import lax
from jax.experimental import pallas as pl
from jax.experimental.pallas import tpu as pltpu
from jax.sharding import PartitionSpec as P

NEIGH = 9
BLK = 64
PLANE = ("y", "xh", "xl")
ALL = ("y", "xh", "xl", "z", "core")


def split(value):
    high = value.astype(jnp.bfloat16)
    return high, (value - high.astype(jnp.float32)).astype(jnp.bfloat16)


def weigh_kernel(
    links, side, own, x_low, x_high, y_side, corner_low, corner_high, mass, out, high, low, rhs_high, rhs_low, woven
):
    def put(place, value):
        high[place], low[place] = split(value)

    sy = side[0]
    for a in range(4):
        for b in range(4):
            put((a + 1) * 6 + b + 1, own[a * 4 + b])
    for b in range(4):
        put(b + 1, x_low[b])
        put(30 + b + 1, x_high[b])
    for column, owner in ((5, 0), (0, 1)):
        keep = (sy == owner).astype(jnp.float32)
        put(column, corner_low[...] * keep)
        put(30 + column, corner_high[...] * keep)
        for a in range(4):
            put((a + 1) * 6 + column, y_side[a] * keep)
    rhs_high[NEIGH * BLK :, :] = jnp.zeros((BLK, rhs_high.shape[1]), jnp.bfloat16)
    rhs_low[NEIGH * BLK :, :] = jnp.zeros((BLK, rhs_low.shape[1]), jnp.bfloat16)
    first = lax.broadcasted_iota(jnp.int32, (32, 128), 1) < BLK

    def block(index, carry):
        base = (index // 4) * 6 + index % 4
        evens, odds = [], []
        for k in range(NEIGH):
            code = links[index * NEIGH + k]
            source = base + (code // 3) * 6 + code % 3
            rhs_high[k * BLK : (k + 1) * BLK, :] = high[source]
            rhs_low[k * BLK : (k + 1) * BLK, :] = low[source]
        for k in range(0, NEIGH, 2):
            left = mass[index, k : k + 1, :].reshape(32, 128)
            if k + 1 < NEIGH:
                right = mass[index, k + 1 : k + 2, :].reshape(32, 128)
            else:
                right = jnp.zeros((32, 128), jnp.float32)
            evens.append(jnp.where(first, left, pltpu.roll(right, BLK, 1)))
            odds.append(jnp.where(first, pltpu.roll(left, BLK, 1), right))
        lhs = jnp.concatenate([jnp.concatenate(evens, 1), jnp.concatenate(odds, 1)], 0)
        lhs_high, lhs_low = split(lhs)
        both = jnp.dot(
            jnp.concatenate([lhs_high, lhs_low], 0), rhs_high[...], preferred_element_type=jnp.float32
        )
        total = both[:BLK] + (
            both[BLK:] + jnp.dot(lhs_high, rhs_low[...], preferred_element_type=jnp.float32)
        )
        for half in range(2):
            lanes = slice(half * 128, half * 128 + 128)
            woven[half, pl.ds(0, 32, stride=2), :] = total[:32, lanes]
            woven[half, pl.ds(1, 32, stride=2), :] = total[32:, lanes]
            out[index, :, lanes] = woven[half]
        return carry

    lax.fori_loop(0, 16, block, 0)


def weigh(snapshots, links, mass):
    sy = lax.axis_index("xl")
    edge = jnp.where(sy == 0, snapshots[:, 3], snapshots[:, 0])
    along = ("y", "xh")
    x_up = [(i, i + 1) for i in range(7)]
    x_down = [(i + 1, i) for i in range(7)]
    cross_up = [(2 * i + j, 2 * (i + 1) + 1 - j) for i in range(7) for j in range(2)]
    cross_down = [(2 * (i + 1) + j, 2 * i + 1 - j) for i in range(7) for j in range(2)]
    x_low = lax.ppermute(snapshots[3], along, x_up)
    x_high = lax.ppermute(snapshots[0], along, x_down)
    y_side = lax.ppermute(edge, "xl", [(0, 1), (1, 0)])
    corner_low = lax.ppermute(edge[3], PLANE, cross_up)
    corner_high = lax.ppermute(edge[0], PLANE, cross_down)
    cols = snapshots.shape[3]
    vmem = pl.BlockSpec(memory_space=pltpu.VMEM)
    smem = pl.BlockSpec(memory_space=pltpu.SMEM)
    out = pl.pallas_call(
        weigh_kernel,
        out_shape=jax.ShapeDtypeStruct((16, BLK, cols), jnp.float32),
        in_specs=[smem, smem] + [vmem] * 7,
        out_specs=vmem,
        scratch_shapes=[
            pltpu.VMEM((36, BLK, cols), jnp.bfloat16),
            pltpu.VMEM((36, BLK, cols), jnp.bfloat16),
            pltpu.VMEM(((NEIGH + 1) * BLK, cols), jnp.bfloat16),
            pltpu.VMEM(((NEIGH + 1) * BLK, cols), jnp.bfloat16),
            pltpu.VMEM((2, BLK, 128), jnp.float32),
        ],
        compiler_params=pltpu.CompilerParams(vmem_limit_bytes=40 * 1024 * 1024),
        cost_estimate=pl.CostEstimate(flops=10**9, bytes_accessed=6 * 10**6, transcendentals=0),
    )(
        links.reshape(-1),
        sy.reshape(1).astype(jnp.int32),
        snapshots.reshape(16, BLK, cols),
        x_low,
        x_high,
        y_side,
        corner_low,
        corner_high,
        mass.reshape(16, NEIGH, 4096),
    )
    return out


VMEM = pl.BlockSpec(memory_space=pltpu.VMEM)
SMEM = pl.BlockSpec(memory_space=pltpu.SMEM)


def dot(left, right):
    def one(a, b):
        return lax.dot_general(a, b, (((0,), (0,)), ((), ())), preferred_element_type=jnp.float32)

    return one(left[0], right[0]) + (one(left[0], right[1]) + one(left[1], right[0]))


def square_kernel(core, own, other, out):
    mine = core[0]
    parts = (split(own[...]), split(other[...]))
    sides = (mine, 1 - mine)
    for row in range(2):
        for column in range(2):
            block = dot(parts[row], parts[column])
            for i in range(2):
                for j in range(2):
                    out[4 * (2 * sides[row] + i) + 2 * sides[column] + j] = block[
                        i * 128 : i * 128 + 128, j * 128 : j * 128 + 128
                    ]


def near_kernel(core, held, last, own, other, out):
    mine = core[0]
    rights = (split(own[...]), split(other[...]))
    sides = (mine, 1 - mine)
    for index, left in enumerate((held, last)):
        left = split(left[...])
        slot = mine if index == 0 else 1 - mine
        for column in range(2):
            block = dot(left, rights[column])
            for i in range(2):
                for j in range(2):
                    out[slot, 4 * i + 2 * sides[column] + j] = block[
                        i * 128 : i * 128 + 128, j * 128 : j * 128 + 128
                    ]


def far_kernel(core, last, own, other, opposite, out):
    mine = core[0]
    rights = (split(own[...]), split(other[...]))
    sides = (mine, 1 - mine)
    left = split(last[...])
    for column in range(2):
        block = dot(left, rights[column])
        for i in range(2):
            for j in range(2):
                out[mine, 4 * i + 2 * sides[column] + j] = block[
                    i * 128 : i * 128 + 128, j * 128 : j * 128 + 128
                ]
    block = dot(left, split(opposite[...]))
    for i in range(2):
        for j in range(2):
            out[1 - mine, 4 * i + j] = block[i * 128 : i * 128 + 128, j * 128 : j * 128 + 128]
            out[1 - mine, 4 * i + 2 + j] = jnp.zeros((128, 128), jnp.float32)


def product(kernel, shape, core, *arrays):
    return pl.pallas_call(
        kernel,
        out_shape=jax.ShapeDtypeStruct(shape + (128, 128), jnp.float32),
        in_specs=[SMEM] + [VMEM] * len(arrays),
        out_specs=VMEM,
        compiler_params=pltpu.CompilerParams(vmem_limit_bytes=48 * 1024 * 1024),
        cost_estimate=pl.CostEstimate(flops=2 * 10**9, bytes_accessed=5 * 2**20, transcendentals=0),
    )(core.reshape(1).astype(jnp.int32), *arrays)


def joined(blocks):
    return jnp.concatenate([blocks[0], lax.ppermute(blocks[1], "core", SWAP)], 0)


def scatter(blocks):
    return jnp.sum(lax.all_to_all(blocks, PLANE, 0, 0, tiled=True), 0)


SWAP = [(0, 1), (1, 0)]
FIRST = (1, 3, 0, 2)


def flat(z, core, column):
    return (column % 16) * 16 + 2 * (z % 8) + core


def crossed(z, core):
    return core if z % 8 < 4 else 1 - core


def routes(turn, far):
    pairs = []
    for i in range(4):
        for j in range(4):
            low, high = 2 * (i % 2) + j % 2, 2 * (j % 2) + i % 2
            for z in range(8):
                for core in range(2):
                    here = flat(z, core, 4 * i + j)
                    row = i // 2 if core == 0 else 1 - i // 2
                    column = j // 2
                    if not far:
                        a, b = (z, z + 1) if core == 0 else (z - 1, z + 1)
                    else:
                        a, b = (z - 2, z + 1) if core == 0 else (z - 2, z + 2)
                        if core == 1:
                            if j > 1:
                                continue
                            column = crossed(z, row)
                    if low == turn:
                        pairs.append((here, flat(a, row, 2 * b + column)))
                    if (high + 2) % 4 == turn:
                        pairs.append((here, flat(b, column, 2 * a + row)))
                    if FIRST[low] == turn and core == 1 and not far:
                        pairs.append((here, flat(z, i // 2, 2 * z + j // 2)))
    return pairs


def body(snapshots, links, mass):
    y, x = lax.axis_index("y"), 2 * lax.axis_index("xh") + lax.axis_index("xl")
    z, core = lax.axis_index("z"), lax.axis_index("core")
    up = [(i, (i + 1) % 8) for i in range(8)]
    down = [(i, (i - 1) % 8) for i in range(8)]
    down_crossed = [
        (2 * i + c, 2 * ((i - 1) % 8) + crossed(i - 1, c)) for i in range(8) for c in range(2)
    ]
    weighted = weigh(snapshots, links, mass)
    held = weighted.reshape(1024, weighted.shape[2])
    next_1 = lax.ppermute(held, "z", down)
    last_1 = lax.ppermute(held, "z", up)
    held_other = lax.ppermute(held, "core", SWAP)
    square = scatter(product(square_kernel, (16,), core, held, held_other))
    next_1, last_1, square = lax.optimization_barrier((next_1, last_1, square))
    next_2 = lax.ppermute(next_1, ("z", "core"), down_crossed)
    last_2 = lax.ppermute(last_1, "z", up)
    next_other = lax.ppermute(next_1, "core", SWAP)
    near = scatter(joined(product(near_kernel, (2, 8), core, held, last_1, next_1, next_other)))
    low = 2 * (y % 2) + x % 2
    high = 2 * (x % 2) + y % 2
    next_2, last_2, near = lax.optimization_barrier((next_2, last_2, near))
    near_turned = near.T
    got = []
    for turn in range(4):
        value = jnp.where(low == turn, near, jnp.where((high + 2) % 4 == turn, near_turned, square))
        got.append(lax.ppermute(value, ALL, routes(turn, False)))
    far = scatter(
        joined(product(far_kernel, (2, 8), core, last_2, next_1, next_other, next_2))
    )
    far_turned = far.T
    for turn in range(4):
        value = jnp.where(low == turn, far, far_turned)
        got[turn] = got[turn] + lax.ppermute(value, ALL, routes(turn, True))
    column = 4 * y + x
    apart = (column // 2 - z) % 8
    over = (z + 2) % 8
    straight = (column % 2) == jnp.where(over < 4, core, 1 - core)
    mirrored = (apart > 4) | ((apart == 4) & jnp.logical_not(straight))
    part = [
        jnp.where(apart == 0, got[FIRST[k]], jnp.where(mirrored, got[(k + 2) % 4], got[k]))
        for k in range(4)
    ]
    gram = jnp.concatenate(
        [jnp.concatenate(part[:2], 1), jnp.concatenate(part[2:], 1)], 0
    ) * jnp.float32(1.0 / 16384)
    return weighted.reshape(snapshots.shape), gram


def solution(mesh):
    parts = jax.sharding.Mesh(mesh.devices.reshape(4, 2, 2, 8, 2), ALL)
    along, side, snap = ("y", "xh"), "xl", ("z", "core")
    placed = (P(along, side, None, snap), P(along, side, None), P(along, side, None, None))
    return jax.shard_map(
        body,
        mesh=parts,
        in_specs=placed,
        out_specs=(P(along, side, None, snap), P(snap, PLANE)),
        check_vma=False,
    )
```

time: 271 us -> 153 us (0.56)
  the two profiles are of different devices: /device:TPU:2 before, /device:TPU:121 now
where the time goes in v1:
time: 153 us
  starting transfers between devices  56.8 us (37%)
  blocking collectives  39.2 us (26%)
  waiting for transfers between devices  26.6 us (17%)
  Pallas kernels  13.3 us (9%)
  local copies, waits for them, and re-layouts  8.81 us (6%)
  other arithmetic  6.73 us (4%)
    all_to_all x2, blocking collectives, scatter(): return jnp.sum(lax.all_to_all(blocks, PLANE, 0, 0, tiled=True), 0)  39.2 us
    ppermute x4, starting transfers between devices, body(): got[turn] = got[turn] + lax.ppermute(value, ALL, routes(turn, True))  17.5 us
    ppermute x4, starting transfers between devices, body(): got.append(lax.ppermute(value, ALL, routes(turn, False)))  8.7 us
    ppermute x4, waiting for transfers between devices, body(): got[turn] = got[turn] + lax.ppermute(value, ALL, routes(turn, True))  8.1 us
    all_to_all x1, waiting for transfers between devices, scatter(): return jnp.sum(lax.all_to_all(blocks, PLANE, 0, 0, tiled=True), 0)  7.07 us
    pallas_call x3, Pallas kernels, product(): pl.pallas_call(kernel, out_shape=jax.ShapeDtypeStruct(shape + (128, 128),...  6.68 us
    unnamed x15, local copies, waits for them, and re-layouts  6.6 us
    pallas_call x1, Pallas kernels, weigh(): pl.pallas_call(weigh_kernel, out_shape=jax.ShapeDtypeStruct((16, BLK, col...  6.59 us
  transfers between devices with their start and end apart: 22, of which 8 were waited for; matrix products, arithmetic and copies ran while one was open for 6% of the time, Pallas kernels for 1%

profile of v1, /device:TPU:121, one launch (start us, length us, event | category | flops | bytes accessed | tf_op | source)
XLA Modules:
  0.0 152.6 jit_solution(12809574311248079202)
XLA Ops:
  0.6 1.1 fusion.4
  1.7 0.0 copy-start
  1.7 1.3 collective-permute-start.2
  3.0 1.1 slice_bitcast_fusion.4
  4.1 4.5 %collective-permute-start.1 = (f32[4,64,256]{2,1,0:T(8,128)S(1)}, f32[4,64,256]{2,1,0:T(8,128)S(1)}, u32[]{:S(2)}, u32[]{:S(2)}) collective-permute-start(f32[4,64,256]{2,1,0:T(8,128)S(1)} %get-tuple-element.18), channel_id=1, source_target_pairs={{32,0},{64,32},{96,64},{128,96},{160,128},{192,160},{224,192},{33,... | collective-permute-start | bytes 786440 | tf_op jit(solution)/shard_map/ppermute | solution.py:85
  8.6 2.3 %collective-permute-start = (f32[4,64,256]{2,1,0:T(8,128)S(1)}, f32[4,64,256]{2,1,0:T(8,128)S(1)}, u32[]{:S(2)}, u32[]{:S(2)}) collective-permute-start(f32[4,64,256]{2,1,0:T(8,128)S(1)} %get-tuple-element.19), channel_id=1, source_target_pairs={{0,32},{32,64},{64,96},{96,128},{128,160},{160,192},{192,224},{1,3... | collective-permute-start | bytes 786440 | tf_op jit(solution)/shard_map/ppermute | solution.py:84
  10.9 1.1 slice_select_fusion
  12.0 4.8 %collective-permute-start.4 = (f32[64,256]{1,0:T(8,128)S(1)}, f32[64,256]{1,0:T(8,128)S(1)}, u32[]{:S(2)}, u32[]{:S(2)}) collective-permute-start(f32[64,256]{1,0:T(8,128)S(1)} %get-tuple-element.24), channel_id=1, source_target_pairs={{32,16},{48,0},{64,48},{80,32},{96,80},{112,64},{128,112},{144,96}... | collective-permute-start | bytes 196616 | tf_op jit(solution)/shard_map/ppermute | solution.py:88
  16.8 1.9 %collective-permute-start.3 = (f32[64,256]{1,0:T(8,128)S(1)}, f32[64,256]{1,0:T(8,128)S(1)}, u32[]{:S(2)}, u32[]{:S(2)}) collective-permute-start(f32[64,256]{1,0:T(8,128)S(1)} %get-tuple-element.25), channel_id=1, source_target_pairs={{0,48},{16,32},{32,80},{48,64},{64,112},{80,96},{96,144},{112,128}... | collective-permute-start | bytes 196616 | tf_op jit(solution)/shard_map/ppermute | solution.py:87
  18.7 0.8 reshape.33.links
  19.5 3.1 %copy.5 = f32[4,4,9,4096]{3,2,1,0:T(8,128)S(1)} copy(f32[4,4,9,4096]{3,1,2,0:T(4,128)} %param.5) | data formatting | bytes 4718592 | tf_op args[2]
  22.6 0.0 collective-permute-done.4.corner_high
  22.7 3.2 %collective-permute-done.3.corner_low = f32[64,256]{1,0:T(8,128)S(1)} collective-permute-done((f32[64,256]{1,0:T(8,128)S(1)}, f32[64,256]{1,0:T(8,128)S(1)}, u32[]{:S(2)}, u32[]{:S(2)}) %collective-permute-start.3) | collective-permute-done | bytes 65568 | tf_op jit(solution)/shard_map/ppermute | solution.py:87
  25.9 0.0 collective-permute-done.1.x_high
  25.9 0.0 collective-permute-done.x_low
  25.9 6.6 %shard_map.50 = f32[16,64,256]{2,1,0:T(8,128)} custom-call(s32[144]{0:T(256)S(1)} %reshape.33.links, s32[1]{0:T(128)} %bitcast.side, f32[16,64,256]{2,1,0:T(8,128)S(1)} %bitcast.43, f32[4,64,256]{2,1,0:T(8,128)S(1)} %collective-permute-done.x_low, f32[4,64,256]{2,1,0:T(8,128)S(1)} %collective-permute-done.1.x_high, ...), custom_call_target="tpu_custom_call" | custom-call | flops 1000000000 | bytes 6000000 | tf_op jit(solution)/shard_map/pallas_call | solution.py:92
  32.5 1.1 collective-permute-start.7
  33.6 2.8 %collective-permute-start.6 = (f32[1024,256]{1,0:T(8,128)}, f32[1024,256]{1,0:T(8,128)S(1)}, u32[]{:S(2)}, u32[]{:S(2)}) collective-permute-start(f32[1024,256]{1,0:T(8,128)} %bitcast.45), channel_id=1, source_target_pairs={{0,2},{2,4},{4,6},{6,8},{8,10},{10,12},{12,14},{14,0},{1,3},{3,5},... | collective-permute-start | bytes 3145736 | tf_op jit(solution)/shard_map/ppermute | solution.py:249
  36.4 0.0 collective-permute-start.5
  36.4 0.0 collective-permute-done.7.other
  36.4 1.0 copy-done.5
  37.4 1.2 copy-done.1
  38.7 1.2 copy-done.6
  39.9 1.8 %shard_map.51 = f32[16,128,128]{2,1,0:T(8,128)S(1)} custom-call(s32[1]{0:T(128)} %bitcast.10.core, f32[1024,256]{1,0:T(8,128)S(1)} %bitcast.48, f32[1024,256]{1,0:T(8,128)S(1)} %copy-done.6), custom_call_target="tpu_custom_call" | custom-call | flops 2000000000 | bytes 5242880 | tf_op jit(solution)/shard_map/pallas_call | solution.py:181
  41.7 19.4 %all_to_all.15 = f32[16,128,128]{2,1,0:T(8,128)} all-to-all(f32[16,128,128]{2,1,0:T(8,128)S(1)} %shard_map.51), channel_id=1, replica_groups=mesh['y'=4,'xh'=2,'xl'=2,'z'=8,'core'=2] {'y','xh','xl'}, dimensions={0} | all-to-all | bytes 2097152 | tf_op jit(solution)/shard_map/all_to_all | solution.py:196
  61.1 1.3 reduce_sum.27
  62.4 0.0 collective-permute-done.6.last
  62.4 1.8 %collective-permute-start.10 = (f32[1024,256]{1,0:T(8,128)S(1)}, f32[1024,256]{1,0:T(8,128)S(1)}, u32[]{:S(2)}, u32[]{:S(2)}) collective-permute-start(f32[1024,256]{1,0:T(8,128)S(1)} %collective-permute-done.5.own), channel_id=1, source_target_pairs={{0,1},{1,0},{2,3},{3,2},{4,5},{5,4},{6,7},{7,6},{8,9},{9,8},{10,11... | collective-permute-start | bytes 3145736 | tf_op jit(solution)/shard_map/ppermute | solution.py:255
  64.2 2.3 %collective-permute-done.10.other = f32[1024,256]{1,0:T(8,128)S(1)} collective-permute-done((f32[1024,256]{1,0:T(8,128)S(1)}, f32[1024,256]{1,0:T(8,128)S(1)}, u32[]{:S(2)}, u32[]{:S(2)}) %collective-permute-start.10) | collective-permute-done | bytes 1048608 | tf_op jit(solution)/shard_map/ppermute | solution.py:255
  66.5 1.9 %shard_map.52 = f32[2,8,128,128]{3,2,1,0:T(8,128)S(1)} custom-call(s32[1]{0:T(128)} %bitcast.10.core, f32[1024,256]{1,0:T(8,128)S(1)} %bitcast.49, f32[1024,256]{1,0:T(8,128)S(1)} %collective-permute-done.6.last, f32[1024,256]{1,0:T(8,128)S(1)} %collective-permute-done.5.own, f32[1024,256]{1,0:T(8,128)S(1)} %collective-permute-done.10.other), custom_call_target="tpu_custom_call" | custom-call | flops 2000000000 | bytes 5242880 | tf_op jit(solution)/shard_map/pallas_call | solution.py:181
  68.4 0.1 slice_bitcast_fusion.3
  68.5 0.5 collective-permute-start.11
  68.9 2.7 %collective-permute-start.9 = (f32[1024,256]{1,0:T(8,128)S(1)}, f32[1024,256]{1,0:T(8,128)}, u32[]{:S(2)}, u32[]{:S(2)}) collective-permute-start(f32[1024,256]{1,0:T(8,128)S(1)} %collective-permute-done.6.last), channel_id=1, source_target_pairs={{0,2},{2,4},{4,6},{6,8},{8,10},{10,12},{12,14},{14,0},{1,3},{3,5},... | collective-permute-start | bytes 3145736 | tf_op jit(solution)/shard_map/ppermute | solution.py:254
  71.6 0.0 collective-permute-done.11
  71.6 0.1 pad_maximum_fusion
  71.7 19.8 %all_to_all.16 = f32[16,128,128]{2,1,0:T(8,128)} all-to-all(f32[16,128,128]{2,1,0:T(8,128)S(1)} %pad_maximum_fusion), channel_id=1, replica_groups=mesh['y'=4,'xh'=2,'xl'=2,'z'=8,'core'=2] {'y','xh','xl'}, dimensions={0} | all-to-all | bytes 2097152 | tf_op jit(solution)/shard_map/all_to_all | solution.py:196
  91.5 1.3 reduce_sum.28
  92.8 1.2 collective-permute-done.9.last
  94.0 3.2 %collective-permute-done.8.opposite = f32[1024,256]{1,0:T(8,128)} collective-permute-done((f32[1024,256]{1,0:T(8,128)S(1)}, f32[1024,256]{1,0:T(8,128)}, u32[]{:S(2)}, u32[]{:S(2)}) %collective-permute-start.8) | collective-permute-done | bytes 1048608 | tf_op jit(solution)/shard_map/ppermute | solution.py:253
  97.2 3.0 %shard_map.53 = f32[2,8,128,128]{3,2,1,0:T(8,128)S(1)} custom-call(s32[1]{0:T(128)} %bitcast.10.core, f32[1024,256]{1,0:T(8,128)} %collective-permute-done.9.last, f32[1024,256]{1,0:T(8,128)S(1)} %collective-permute-done.5.own, f32[1024,256]{1,0:T(8,128)S(1)} %copy-done.4, f32[1024,256]{1,0:T(8,128)} %collective-permute-done.8.opposite), custom_call_target="tpu_custom_call" | custom-call | flops 2000000000 | bytes 5242880 | tf_op jit(solution)/shard_map/pallas_call | solution.py:181
  100.2 0.1 slice_bitcast_fusion.1
  100.3 1.4 collective-permute-start.13
  101.7 1.5 %collective-permute-done.13 = f32[8,128,128]{2,1,0:T(8,128)S(1)} collective-permute-done((f32[8,128,128]{2,1,0:T(8,128)S(1)}, f32[8,128,128]{2,1,0:T(8,128)S(1)}, u32[]{:S(2)}, u32[]{:S(2)}) %collective-permute-start.13) | collective-permute-done | bytes 524320 | tf_op jit(solution)/shard_map/ppermute | solution.py:192
  103.2 1.1 pad_maximum_fusion.1
  104.3 5.6 %all-to-all-start.2 = ((f32[16,128,128]{2,1,0:T(8,128)}), f32[16,128,128]{2,1,0:T(8,128)S(1)}, u32[]{:S(2)}, u32[]{:S(2)}) async-start(f32[16,128,128]{2,1,0:T(8,128)} %pad_maximum_fusion.1), calls=%async_computation.2 | async-start | bytes 2097152 | tf_op jit(solution)/shard_map/all_to_all | solution.py:196
  109.9 0.1 copy.6
  110.0 5.5 %collective-permute-start.17 = (f32[128,128]{1,0:T(8,128)S(1)}, f32[128,128]{1,0:T(8,128)S(1)}, u32[]{:S(2)}, u32[]{:S(2)}) collective-permute-start(f32[128,128]{1,0:T(8,128)S(1)} %get-tuple-element.26), channel_id=1, source_target_pairs={{0,32},{1,47},{2,66},{3,65},{4,100},{5,99},{6,134},{7,133},{8,168}... | collective-permute-start | bytes 196616 | tf_op jit(solution)/shard_map/ppermute | solution.py:264
  115.5 1.3 collective-permute-start.19
  116.8 1.3 collective-permute-start.15
  118.1 0.7 collective-permute-start.12
  118.8 7.1 %all-to-all-done.2 = f32[16,128,128]{2,1,0:T(8,128)S(1)} async-done(((f32[16,128,128]{2,1,0:T(8,128)}), f32[16,128,128]{2,1,0:T(8,128)S(1)}, u32[]{:S(2)}, u32[]{:S(2)}) %all-to-all-start.2) | async-done | bytes 1048608 | tf_op jit(solution)/shard_map/all_to_all | solution.py:196
  125.8 0.1 reduce_sum.29
  125.9 0.1 copy.7
  126.0 1.3 collective-permute-start.18
  127.3 0.0 collective-permute-done.17
  127.3 13.0 %collective-permute-start.20 = (f32[128,128]{1,0:T(8,128)S(1)}, f32[128,128]{1,0:T(8,128)S(1)}, u32[]{:S(2)}, u32[]{:S(2)}) collective-permute-start(f32[128,128]{1,0:T(8,128)S(1)} %get-tuple-element.31), channel_id=1, source_target_pairs={{64,194},{65,213},{66,228},{67,247},{68,6},{69,25},{70,40},{71,59}... | collective-permute-start | bytes 196616 | tf_op jit(solution)/shard_map/ppermute | solution.py:271
  140.4 1.9 %collective-permute-start.16 = (f32[128,128]{1,0:T(8,128)S(1)}, f32[128,128]{1,0:T(8,128)S(1)}, u32[]{:S(2)}, u32[]{:S(2)}) collective-permute-start(f32[128,128]{1,0:T(8,128)S(1)} %get-tuple-element.32), channel_id=1, source_target_pairs={{0,194},{1,213},{2,228},{3,247},{4,6},{5,25},{6,40},{7,59},{8,74},... | collective-permute-start | bytes 196616 | tf_op jit(solution)/shard_map/ppermute | solution.py:271
  142.3 0.0 collective-permute-done.15
  142.3 1.3 collective-permute-start.14
  143.7 0.0 collective-permute-done.18
  143.7 0.0 collective-permute-done.20
  143.7 4.7 %collective-permute-done.16 = f32[128,128]{1,0:T(8,128)S(1)} collective-permute-done((f32[128,128]{1,0:T(8,128)S(1)}, f32[128,128]{1,0:T(8,128)S(1)}, u32[]{:S(2)}, u32[]{:S(2)}) %collective-permute-start.16) | collective-permute-done | bytes 65568 | tf_op jit(solution)/shard_map/ppermute | solution.py:271
  148.4 3.4 %collective-permute-done.14 = f32[128,128]{1,0:T(8,128)S(1)} collective-permute-done((f32[128,128]{1,0:T(8,128)S(1)}, f32[128,128]{1,0:T(8,128)S(1)}, u32[]{:S(2)}, u32[]{:S(2)}) %collective-permute-start.14) | collective-permute-done | bytes 65568 | tf_op jit(solution)/shard_map/ppermute | solution.py:271
  151.9 0.7 maximum_multiply_fusion
  (19 shorter events, 0.1 us)
Async XLA Ops:
  1.7 24.2 %copy-start = (f32[4,4,64,256]{3,2,1,0:T(8,128)S(1)}, f32[4,4,64,256]{3,2,1,0:T(8,128)}, u32[]{:S(2)}) copy-start(f32[4,4,64,256]{3,2,1,0:T(8,128)} %param.3) | copy-start | bytes 3145732
  1.7 24.2 %collective-permute-start.2 = (f32[4,64,256]{2,1,0:T(8,128)S(1)}, f32[4,64,256]{2,1,0:T(8,128)S(1)}, u32[]{:S(2)}, u32[]{:S(2)}) collective-permute-start(f32[4,64,256]{2,1,0:T(8,128)S(1)} %fusion.4), channel_id=1, source_target_pairs={{0,16},{16,0},{1,17},{17,1},{2,18},{18,2},{3,19},{19,3},{4,20},{20... | collective-permute-start | bytes 786440 | tf_op jit(solution)/shard_map/ppermute | solution.py:86
  4.1 21.8 %collective-permute-start.1 = (f32[4,64,256]{2,1,0:T(8,128)S(1)}, f32[4,64,256]{2,1,0:T(8,128)S(1)}, u32[]{:S(2)}, u32[]{:S(2)}) collective-permute-start(f32[4,64,256]{2,1,0:T(8,128)S(1)} %get-tuple-element.18), channel_id=1, source_target_pairs={{32,0},{64,32},{96,64},{128,96},{160,128},{192,160},{224,192},{33,... | collective-permute-start | bytes 786440 | tf_op jit(solution)/shard_map/ppermute | solution.py:85
  8.6 17.3 %collective-permute-start = (f32[4,64,256]{2,1,0:T(8,128)S(1)}, f32[4,64,256]{2,1,0:T(8,128)S(1)}, u32[]{:S(2)}, u32[]{:S(2)}) collective-permute-start(f32[4,64,256]{2,1,0:T(8,128)S(1)} %get-tuple-element.19), channel_id=1, source_target_pairs={{0,32},{32,64},{64,96},{96,128},{128,160},{160,192},{192,224},{1,3... | collective-permute-start | bytes 786440 | tf_op jit(solution)/shard_map/ppermute | solution.py:84
  12.0 10.7 %collective-permute-start.4 = (f32[64,256]{1,0:T(8,128)S(1)}, f32[64,256]{1,0:T(8,128)S(1)}, u32[]{:S(2)}, u32[]{:S(2)}) collective-permute-start(f32[64,256]{1,0:T(8,128)S(1)} %get-tuple-element.24), channel_id=1, source_target_pairs={{32,16},{48,0},{64,48},{80,32},{96,80},{112,64},{128,112},{144,96}... | collective-permute-start | bytes 196616 | tf_op jit(solution)/shard_map/ppermute | solution.py:88
  16.8 9.1 %collective-permute-start.3 = (f32[64,256]{1,0:T(8,128)S(1)}, f32[64,256]{1,0:T(8,128)S(1)}, u32[]{:S(2)}, u32[]{:S(2)}) collective-permute-start(f32[64,256]{1,0:T(8,128)S(1)} %get-tuple-element.25), channel_id=1, source_target_pairs={{0,48},{16,32},{32,80},{48,64},{64,112},{80,96},{96,144},{112,128}... | collective-permute-start | bytes 196616 | tf_op jit(solution)/shard_map/ppermute | solution.py:87
  32.5 3.9 %collective-permute-start.7 = (f32[1024,256]{1,0:T(8,128)}, f32[1024,256]{1,0:T(8,128)S(1)}, u32[]{:S(2)}, u32[]{:S(2)}) collective-permute-start(f32[1024,256]{1,0:T(8,128)} %bitcast.44), channel_id=1, source_target_pairs={{0,1},{1,0},{2,3},{3,2},{4,5},{5,4},{6,7},{7,6},{8,9},{9,8},{10,11... | collective-permute-start | bytes 3145736 | tf_op jit(solution)/shard_map/ppermute | solution.py:250
  33.6 28.9 %collective-permute-start.6 = (f32[1024,256]{1,0:T(8,128)}, f32[1024,256]{1,0:T(8,128)S(1)}, u32[]{:S(2)}, u32[]{:S(2)}) collective-permute-start(f32[1024,256]{1,0:T(8,128)} %bitcast.45), channel_id=1, source_target_pairs={{0,2},{2,4},{4,6},{6,8},{8,10},{10,12},{12,14},{14,0},{1,3},{3,5},... | collective-permute-start | bytes 3145736 | tf_op jit(solution)/shard_map/ppermute | solution.py:249
  36.4 26.0 %collective-permute-start.5 = (f32[1024,256]{1,0:T(8,128)}, f32[1024,256]{1,0:T(8,128)S(1)}, u32[]{:S(2)}, u32[]{:S(2)}) collective-permute-start(f32[1024,256]{1,0:T(8,128)} %bitcast.46), channel_id=1, source_target_pairs={{0,14},{2,0},{4,2},{6,4},{8,6},{10,8},{12,10},{14,12},{1,15},{3,1}... | collective-permute-start | bytes 3145736 | tf_op jit(solution)/shard_map/ppermute | solution.py:248
  36.4 1.0 copy-start.5
  37.4 1.2 copy-start.1
  38.7 1.2 copy-start.6
  39.9 26.6 %copy-start.2 = (f32[16,64,256]{2,1,0:T(8,128)S(1)}, f32[16,64,256]{2,1,0:T(8,128)}, u32[]{:S(2)}) copy-start(f32[16,64,256]{2,1,0:T(8,128)} %shard_map.50) | copy-start | bytes 3145732
  62.4 4.0 %collective-permute-start.10 = (f32[1024,256]{1,0:T(8,128)S(1)}, f32[1024,256]{1,0:T(8,128)S(1)}, u32[]{:S(2)}, u32[]{:S(2)}) collective-permute-start(f32[1024,256]{1,0:T(8,128)S(1)} %collective-permute-done.5.own), channel_id=1, source_target_pairs={{0,1},{1,0},{2,3},{3,2},{4,5},{5,4},{6,7},{7,6},{8,9},{9,8},{10,11... | collective-permute-start | bytes 3145736 | tf_op jit(solution)/shard_map/ppermute | solution.py:255
  66.5 2.0 %copy-start.3 = (f32[1024,256]{1,0:T(8,128)}, f32[1024,256]{1,0:T(8,128)S(1)}, u32[]{:S(2)}) copy-start(f32[1024,256]{1,0:T(8,128)S(1)} %collective-permute-done.10.other) | copy-start | bytes 3145732
  68.5 28.8 %copy-start.4 = (f32[1024,256]{1,0:T(8,128)S(1)}, f32[1024,256]{1,0:T(8,128)}, u32[]{:S(2)}) copy-start(f32[1024,256]{1,0:T(8,128)} %copy-done.3) | copy-start | bytes 3145732
  68.5 3.1 %collective-permute-start.11 = (f32[8,128,128]{2,1,0:T(8,128)S(1)}, f32[8,128,128]{2,1,0:T(8,128)S(1)}, u32[]{:S(2)}, u32[]{:S(2)}) collective-permute-start(f32[8,128,128]{2,1,0:T(8,128)S(1)} %get-tuple-element.17), channel_id=1, source_target_pairs={{0,1},{1,0},{2,3},{3,2},{4,5},{5,4},{6,7},{7,6},{8,9},{9,8},{10,11... | collective-permute-start | bytes 1572872 | tf_op jit(solution)/shard_map/ppermute | solution.py:192
  68.9 25.1 %collective-permute-start.9 = (f32[1024,256]{1,0:T(8,128)S(1)}, f32[1024,256]{1,0:T(8,128)}, u32[]{:S(2)}, u32[]{:S(2)}) collective-permute-start(f32[1024,256]{1,0:T(8,128)S(1)} %collective-permute-done.6.last), channel_id=1, source_target_pairs={{0,2},{2,4},{4,6},{6,8},{8,10},{10,12},{12,14},{14,0},{1,3},{3,5},... | collective-permute-start | bytes 3145736 | tf_op jit(solution)/shard_map/ppermute | solution.py:254
  71.6 25.6 %collective-permute-start.8 = (f32[1024,256]{1,0:T(8,128)S(1)}, f32[1024,256]{1,0:T(8,128)}, u32[]{:S(2)}, u32[]{:S(2)}) collective-permute-start(f32[1024,256]{1,0:T(8,128)S(1)} %collective-permute-done.5.own), channel_id=1, source_target_pairs={{0,15},{1,14},{2,0},{3,1},{4,2},{5,3},{6,4},{7,5},{8,6},{9,7},{10,... | collective-permute-start | bytes 3145736 | tf_op jit(solution)/shard_map/ppermute | solution.py:253
  100.3 2.9 %collective-permute-start.13 = (f32[8,128,128]{2,1,0:T(8,128)S(1)}, f32[8,128,128]{2,1,0:T(8,128)S(1)}, u32[]{:S(2)}, u32[]{:S(2)}) collective-permute-start(f32[8,128,128]{2,1,0:T(8,128)S(1)} %get-tuple-element.15), channel_id=1, source_target_pairs={{0,1},{1,0},{2,3},{3,2},{4,5},{5,4},{6,7},{7,6},{8,9},{9,8},{10,11... | collective-permute-start | bytes 1572872 | tf_op jit(solution)/shard_map/ppermute | solution.py:192
  104.3 21.6 %all-to-all-start.2 = ((f32[16,128,128]{2,1,0:T(8,128)}), f32[16,128,128]{2,1,0:T(8,128)S(1)}, u32[]{:S(2)}, u32[]{:S(2)}) async-start(f32[16,128,128]{2,1,0:T(8,128)} %pad_maximum_fusion.1), calls=%async_computation.2 | async-start | bytes 2097152 | tf_op jit(solution)/shard_map/all_to_all | solution.py:196
  110.0 17.3 %collective-permute-start.17 = (f32[128,128]{1,0:T(8,128)S(1)}, f32[128,128]{1,0:T(8,128)S(1)}, u32[]{:S(2)}, u32[]{:S(2)}) collective-permute-start(f32[128,128]{1,0:T(8,128)S(1)} %get-tuple-element.26), channel_id=1, source_target_pairs={{0,32},{1,47},{2,66},{3,65},{4,100},{5,99},{6,134},{7,133},{8,168}... | collective-permute-start | bytes 196616 | tf_op jit(solution)/shard_map/ppermute | solution.py:264
  115.5 24.9 %collective-permute-start.19 = (f32[128,128]{1,0:T(8,128)S(1)}, f32[128,128]{1,0:T(8,128)S(1)}, u32[]{:S(2)}, u32[]{:S(2)}) collective-permute-start(f32[128,128]{1,0:T(8,128)S(1)} %get-tuple-element.27), channel_id=1, source_target_pairs={{17,0},{19,34},{21,68},{23,102},{25,136},{27,170},{29,204},{31,238... | collective-permute-start | bytes 196616 | tf_op jit(solution)/shard_map/ppermute | solution.py:264
  116.8 25.5 %collective-permute-start.15 = (f32[128,128]{1,0:T(8,128)S(1)}, f32[128,128]{1,0:T(8,128)S(1)}, u32[]{:S(2)}, u32[]{:S(2)}) collective-permute-start(f32[128,128]{1,0:T(8,128)S(1)} %get-tuple-element.28), channel_id=1, source_target_pairs={{0,2},{1,242},{2,36},{3,20},{4,70},{5,54},{6,104},{7,88},{8,138},{... | collective-permute-start | bytes 196616 | tf_op jit(solution)/shard_map/ppermute | solution.py:264
  118.1 25.6 %collective-permute-start.12 = (f32[128,128]{1,0:T(8,128)S(1)}, f32[128,128]{1,0:T(8,128)S(1)}, u32[]{:S(2)}, u32[]{:S(2)}) collective-permute-start(f32[128,128]{1,0:T(8,128)S(1)} %get-tuple-element.29), channel_id=1, source_target_pairs={{1,0},{3,34},{5,68},{7,102},{9,136},{11,170},{13,204},{15,238},{16... | collective-permute-start | bytes 196616 | tf_op jit(solution)/shard_map/ppermute | solution.py:264
  126.0 17.7 %collective-permute-start.18 = (f32[128,128]{1,0:T(8,128)S(1)}, f32[128,128]{1,0:T(8,128)S(1)}, u32[]{:S(2)}, u32[]{:S(2)}) collective-permute-start(f32[128,128]{1,0:T(8,128)S(1)} %get-tuple-element.30), channel_id=1, source_target_pairs={{0,44},{1,93},{2,78},{3,127},{4,96},{5,145},{6,130},{7,179},{8,164... | collective-permute-start | bytes 196616 | tf_op jit(solution)/shard_map/ppermute | solution.py:271
  127.3 16.4 %collective-permute-start.20 = (f32[128,128]{1,0:T(8,128)S(1)}, f32[128,128]{1,0:T(8,128)S(1)}, u32[]{:S(2)}, u32[]{:S(2)}) collective-permute-start(f32[128,128]{1,0:T(8,128)S(1)} %get-tuple-element.31), channel_id=1, source_target_pairs={{64,194},{65,213},{66,228},{67,247},{68,6},{69,25},{70,40},{71,59}... | collective-permute-start | bytes 196616 | tf_op jit(solution)/shard_map/ppermute | solution.py:271
  140.4 8.0 %collective-permute-start.16 = (f32[128,128]{1,0:T(8,128)S(1)}, f32[128,128]{1,0:T(8,128)S(1)}, u32[]{:S(2)}, u32[]{:S(2)}) collective-permute-start(f32[128,128]{1,0:T(8,128)S(1)} %get-tuple-element.32), channel_id=1, source_target_pairs={{0,194},{1,213},{2,228},{3,247},{4,6},{5,25},{6,40},{7,59},{8,74},... | collective-permute-start | bytes 196616 | tf_op jit(solution)/shard_map/ppermute | solution.py:271
  142.3 9.5 %collective-permute-start.14 = (f32[128,128]{1,0:T(8,128)S(1)}, f32[128,128]{1,0:T(8,128)S(1)}, u32[]{:S(2)}, u32[]{:S(2)}) collective-permute-start(f32[128,128]{1,0:T(8,128)S(1)} %get-tuple-element.33), channel_id=1, source_target_pairs={{16,44},{17,93},{18,78},{19,127},{20,96},{21,145},{22,130},{23,179... | collective-permute-start | bytes 196616 | tf_op jit(solution)/shard_map/ppermute | solution.py:271

commit v2 on v0

v2 whole, which is shorter than its diff:
```python
import jax
import jax.numpy as jnp
from jax import lax
from jax.experimental import pallas as pl
from jax.experimental.pallas import tpu as pltpu
from jax.sharding import PartitionSpec as P

NEIGH = 9
BLK = 64
PLANE = ("y", "xh", "xl")
ALL = ("y", "xh", "xl", "z", "core")
SWAP = [(0, 1), (1, 0)]
UP = [(k, (k + 1) % 8) for k in range(8)]
DOWN = [(k, (k - 1) % 8) for k in range(8)]
VMEM = pl.BlockSpec(memory_space=pltpu.VMEM)
SMEM = pl.BlockSpec(memory_space=pltpu.SMEM)
CORE, SIDE, ROW, COLUMN, TURN, MIRROR, KEEP = range(7)


def split(value):
    high = value.astype(jnp.bfloat16)
    return high, (value - high.astype(jnp.float32)).astype(jnp.bfloat16)


def call(kernel, shape, scratch, scalars, *arrays, after=()):
    lead = len(scalars) + len(arrays)

    def ordered(*refs):
        kernel(*refs[:lead], *refs[lead + len(after) :])

    return pl.pallas_call(
        ordered,
        out_shape=shape,
        in_specs=[SMEM] * len(scalars)
        + [VMEM] * len(arrays)
        + [pl.BlockSpec(memory_space=pl.ANY)] * len(after),
        out_specs=jax.tree.map(lambda _: VMEM, shape),
        scratch_shapes=scratch,
        compiler_params=pltpu.CompilerParams(vmem_limit_bytes=40 * 1024 * 1024),
        cost_estimate=pl.CostEstimate(flops=1, bytes_accessed=1, transcendentals=0),
    )(*scalars, *arrays, *after)


def stencil(factors, highs, lows):
    first = lax.broadcasted_iota(jnp.int32, (32, 128), 1) < BLK
    highs, lows = list(highs), list(lows)
    evens, odds = [], []
    for k in range(0, len(factors), 2):
        left = factors[k]
        if k + 1 < len(factors):
            right = factors[k + 1]
        else:
            right = jnp.zeros((32, 128), jnp.float32)
            highs.append(highs[-1])
            lows.append(lows[-1])
        evens.append(jnp.where(first, left, pltpu.roll(right, BLK, 1)))
        odds.append(jnp.where(first, pltpu.roll(left, BLK, 1), right))
    lhs = jnp.concatenate([jnp.concatenate(evens, 1), jnp.concatenate(odds, 1)], 0)
    lhs_high, lhs_low = split(lhs)
    both = jnp.dot(
        jnp.concatenate([lhs_high, lhs_low], 0),
        jnp.concatenate(highs, 0),
        preferred_element_type=jnp.float32,
    )
    return both[:BLK] + (
        both[BLK:]
        + jnp.dot(lhs_high, jnp.concatenate(lows, 0), preferred_element_type=jnp.float32)
    )


def factor(mass, a, k, b):
    return mass[a, k, b : b + 1, :].reshape(32, 128)


def halves(count, cols):
    return [pltpu.VMEM((count, BLK, cols), jnp.bfloat16)] * 2


def weave(out, at, woven, value):
    for half in range(2):
        lanes = slice(half * 128, half * 128 + 128)
        woven[half, pl.ds(0, 32, stride=2), :] = value[:32, lanes]
        woven[half, pl.ds(1, 32, stride=2), :] = value[32:, lanes]
        out[at, :, lanes] = woven[half]


def side_terms(spot, places, mass, a, high, low):
    side = spot[SIDE]
    factors = []
    for shift in range(3):
        place = places[(a * 4 + 3 - 3 * side) * NEIGH + shift * 3 + 2 - 2 * side]
        factors.append(
            jnp.where(side == 0, factor(mass, a, place, 3), factor(mass, a, place, 0))
        )
    return stencil(
        factors, [high[a + shift] for shift in range(3)], [low[a + shift] for shift in range(3)]
    )


def weigh_mid(spot, places, own, y_side, mass, mid, outer, total, high, low, y_high, y_low, woven):
    for block in range(16):
        high[block], low[block] = split(own[block])
    for a in range(4):
        y_high[1 + a], y_low[1 + a] = split(y_side[a])
    for a in range(4):
        for b in range(4):
            factors, highs, lows = [], [], []
            for code in range(NEIGH):
                row, column = a + code // 3 - 1, b + code % 3 - 1
                if 0 <= row < 4 and 0 <= column < 4:
                    factors.append(factor(mass, a, places[(a * 4 + b) * NEIGH + code], b))
                    highs.append(high[row * 4 + column])
                    lows.append(low[row * 4 + column])
            value = stencil(factors, highs, lows)
            if a in (1, 2):
                total[a * 4 - 4 + b] = value
            else:
                outer[a // 3 * 4 + b] = value
    b = 3 - 3 * spot[SIDE]
    for a in (1, 2):
        at = a * 4 - 4 + b
        total[at] = total[at] + side_terms(spot, places, mass, a, y_high, y_low)
    for block in range(8):
        weave(mid, block, woven, total[block])


def weigh_outer(
    spot, places, part, x_low, x_high, y_side, corners, mass, mid, outer, out, total, high, low, y_high, y_low, woven
):
    for b in range(4):
        high[b], low[b] = split(x_low[b])
        high[4 + b], low[4 + b] = split(x_high[b])
        y_high[1 + b], y_low[1 + b] = split(y_side[b])
    y_high[0], y_low[0] = split(corners[0])
    y_high[5], y_low[5] = split(corners[1])
    for a, code_at, halo in ((0, 0, 0), (3, 6, 4)):
        for b in range(4):
            factors, highs, lows = [], [], []
            for shift in range(3):
                column = b + shift - 1
                if 0 <= column < 4:
                    place = places[(a * 4 + b) * NEIGH + code_at + shift]
                    factors.append(factor(mass, a, place, b))
                    highs.append(high[halo + column])
                    lows.append(low[halo + column])
            total[halo + b] = part[halo + b] + stencil(factors, highs, lows)
        at = halo + 3 - 3 * spot[SIDE]
        total[at] = total[at] + side_terms(spot, places, mass, a, y_high, y_low)
    for block in range(8):
        weave(outer, block, woven, total[block])
    out[:4] = outer[:4]
    out[4:12] = mid[...]
    out[12:] = outer[4:]


def weigh(spot, snapshots, links, mass):
    side = lax.axis_index("xl")
    edge = jnp.where(side == 0, snapshots[:, 3], snapshots[:, 0])
    along = ("y", "xh")
    y_side = lax.ppermute(edge, "xl", SWAP)
    x_low = lax.ppermute(snapshots[3], along, [(i, i + 1) for i in range(7)])
    x_high = lax.ppermute(snapshots[0], along, [(i + 1, i) for i in range(7)])
    cols = snapshots.shape[3]
    codes = jnp.arange(NEIGH, dtype=jnp.int32)
    places = jnp.sum(
        jnp.where(links.reshape(16, NEIGH, 1) == codes, codes[:, None], 0), axis=1
    ).reshape(-1)
    mass = mass.transpose(0, 2, 1, 3)

    def blocks(count):
        return jax.ShapeDtypeStruct((count, BLK, cols), jnp.float32)

    total, woven = pltpu.VMEM((8, BLK, cols), jnp.float32), pltpu.VMEM((2, BLK, 128), jnp.float32)
    mid, part = call(
        weigh_mid,
        [blocks(8)] * 2,
        [total] + halves(16, cols) + halves(6, cols) + [woven],
        [spot, places],
        snapshots.reshape(16, BLK, cols),
        y_side,
        mass,
    )
    flat = mid.reshape(8 * BLK, cols)
    early = [lax.ppermute(flat, "z", UP), lax.ppermute(flat, "z", DOWN)]
    x_low, x_high, mid = lax.optimization_barrier((x_low, x_high, mid))
    corners = jnp.where(
        side == 0, jnp.stack([x_low[3], x_high[3]]), jnp.stack([x_low[0], x_high[0]])
    )
    corners = lax.ppermute(corners, "xl", SWAP)
    outer, weighted = call(
        weigh_outer,
        [blocks(8), blocks(16)],
        [total] + halves(8, cols) + halves(6, cols) + [woven],
        [spot, places],
        part,
        x_low,
        x_high,
        y_side,
        corners,
        mass,
        mid,
        after=early,
    )
    return flat, outer.reshape(8 * BLK, cols), weighted, early


def dot(left, right):
    def one(a, b):
        return lax.dot_general(a, b, (((0,), (0,)), ((), ())), preferred_element_type=jnp.float32)

    return one(left[0], right[0]) + (one(left[0], right[1]) + one(left[1], right[0]))


def whole(pair):
    parts = [split(ref[...]) for ref in pair]
    return tuple(jnp.concatenate([parts[0][k], parts[1][k]], 0) for k in range(2))


def columns(value, start, stop):
    return tuple(part[:, start:stop] for part in value)


def lay(out, at, block):
    for i in range(2):
        for j in range(2):
            out[at + 4 * i + j, :128, :] = block[i * 128 : i * 128 + 128, j * 128 : j * 128 + 128]


def near_kernel(spot, *refs):
    *arrays, out, square, relay_a, relay_b = refs
    mine = spot[CORE]
    for relay, own, other in zip((relay_a, relay_b), arrays[4:6], arrays[6:8]):
        relay[...] = jnp.where(spot[KEEP] == 1, own[...], other[...])
    held, last, own, other = [whole(arrays[k : k + 2]) for k in range(0, 8, 2)]
    for side, right in ((mine, own), (1 - mine, other)):
        lay(out, 2 * side, dot(held, right))
        lay(out, 8 + 2 * side, dot(last, right))
    first = mine == 0
    left = tuple(
        jnp.where(first, a, b) for a, b in zip(columns(own, 0, 128), columns(other, 128, 256))
    )
    right = tuple(jnp.where(first, a, b) for a, b in zip(other, own))
    cross = dot(left, right)
    square[...] = jnp.zeros(square.shape, jnp.float32)
    square[0, :128, :] = cross[:, :128]
    square[1, :128, :] = cross[:, 128:]
    diagonal = dot(own, own)
    row = lax.broadcasted_iota(jnp.int32, (128, 128), 0)
    column = lax.broadcasted_iota(jnp.int32, (128, 128), 1)
    low_end = diagonal[128:, 128:]
    square[2, :128, :] = jnp.where(row <= column, diagonal[:128, :128], low_end)
    square[2, 128:129, :] = jnp.sum(jnp.where(row == column, low_end, 0.0), 0, keepdims=True)
    square[3, :128, :] = diagonal[:128, 128:]


def far_kernel(spot, *refs):
    *arrays, square, out = refs
    mine = spot[CORE]
    last, own, other, opposite = [whole(arrays[k : k + 2]) for k in range(0, 8, 2)]
    out[:, 128:, :] = jnp.zeros((16, 8, 128), jnp.float32)
    for side, right in ((mine, own), (1 - mine, other)):
        lay(out, 2 * side, dot(last, right))
    lay(out, 8, dot(last, opposite))
    out[10:12] = square[:2]
    out[14:16] = square[2:]


def add_kernel(blocks, out):
    total = blocks[0]
    for piece in range(1, 16):
        total = total + blocks[piece]
    out[...] = total


def send_kernel(spot, far, far_beside, near, near_beside, *outs):
    y, x, core = spot[ROW], spot[COLUMN], spot[CORE]
    beside = x % 2
    even = jnp.where(beside == 0, far[...], far_beside[...])
    odd = jnp.where(beside == 0, far_beside[...], far[...])[:128]
    row = lax.broadcasted_iota(jnp.int32, (128, 128), 0)
    column = lax.broadcasted_iota(jnp.int32, (128, 128), 1)
    packed = even[:128]
    upper = jnp.where(row <= column, packed, 0.0)
    upper = upper + jnp.where(row < column, packed, 0.0).T
    lower = jnp.where(row > column, packed, 0.0)
    lower = lower + lower.T + jnp.where(row == column, even[128:129], 0.0)
    diagonal = (y == 3) & (x >= 2)
    lefts = jnp.where(diagonal, jnp.where(beside == 0, upper, odd.T), packed)
    rights = jnp.where(diagonal & (beside == 1), lower, odd)
    near_left = jnp.where(beside == 0, near[...], near_beside[...])
    near_right = jnp.where(beside == 0, near_beside[...], near[...])
    late = (y + beside + core) % 2
    for turn in range(2):
        outs[turn][:, :128] = jnp.where(late == turn, lefts, near_left)
        outs[turn][:, 128:] = jnp.where(late == turn, rights, near_right)


def place_kernel(spot, first, second, out):
    block = jnp.concatenate([first[...], second[...]], 0)
    swapped = jnp.concatenate([second[...], first[...]], 0)
    block = jnp.where(spot[TURN] == 0, block, swapped) * (1.0 / 16384)
    out[...] = jnp.where(spot[MIRROR] == 0, block, block.T)


def array(*shape):
    return jax.ShapeDtypeStruct(shape, jnp.float32)


def exchange(blocks):
    return lax.all_to_all(blocks, PLANE, 0, 0, tiled=True)


def gathered(blocks):
    total = call(add_kernel, array(*blocks.shape[1:]), [], [], blocks)
    return total, lax.ppermute(total, "xl", SWAP)


def crossed(z, core):
    return core if z % 8 < 4 else 1 - core


def routes(turn):
    pairs = []

    def flat(z, core, column):
        return (column % 16) * 16 + 2 * (z % 8) + core

    for i in range(4):
        for j in range(4):
            for z in range(8):
                for core in range(2):
                    late = turn == (i + j + core) % 2
                    mirror = j % 2 == 1
                    here = flat(z, core, 4 * i + j)
                    column = j // 2
                    if i < 2:
                        a, b = (z - 2, z + 1) if late else (z, z + 1)
                    elif not late:
                        a, b = z - 1, z + 1
                    elif j < 2:
                        a, b, column = z - 2, z + 2, crossed(z, core)
                    else:
                        row = 0 if i == 2 else core
                        column = 1 if i == 2 else core
                        if i == 3:
                            mirror = False
                        a = b = z + 1
                        pairs.append(
                            (here, flat(b, column, 2 * a + row) if mirror else flat(a, row, 2 * b + column))
                        )
                        continue
                    pairs.append(
                        (here, flat(b, column, 2 * a + core) if mirror else flat(a, core, 2 * b + column))
                    )
    return pairs


def body(snapshots, links, mass):
    y, x = lax.axis_index("y"), 2 * lax.axis_index("xh") + lax.axis_index("xl")
    z, core = lax.axis_index("z"), lax.axis_index("core")
    other = x % 2
    apart = ((4 * y + x) // 2 - z) % 8
    straight = other == jnp.where((z + 2) % 8 < 4, core, 1 - core)
    mirror = (apart > 4) | ((apart == 4) & jnp.logical_not(straight))
    mirror = mirror | ((apart == 0) & (core == 1) & (other == 0))
    turn = jnp.where(mirror, 1 - other, core)
    turn = jnp.where((apart == 1) | (apart == 2) | ((apart == 0) & (core == other)), 1 - core, turn)
    turn = jnp.where(apart > 5, other, turn)
    turn = jnp.where((apart == 0) & (core != other), core, turn)
    keep = (z + 7) % 8 < 4
    spot = [core, lax.axis_index("xl"), y, x, turn, mirror, keep]
    spot = jnp.stack([jnp.asarray(value).astype(jnp.int32) for value in spot])
    *held, weighted, early = weigh(spot, snapshots, links, mass)
    next_1 = [early[1], lax.ppermute(held[1], "z", DOWN)]
    last_1 = [early[0], lax.ppermute(held[1], "z", UP)]
    last_2 = [lax.ppermute(half, "z", UP) for half in last_1]
    next_other = [lax.ppermute(half, "core", SWAP) for half in next_1]
    near, square, *relay = call(
        near_kernel,
        [array(16, 128, 128), array(4, 136, 128)] + [array(*held[0].shape)] * 2,
        [],
        [spot],
        *held,
        *last_1,
        *next_1,
        *next_other,
    )
    next_2 = [lax.ppermute(half, "z", DOWN) for half in relay]
    near = lax.cond(links[0, 0, 0] >= 0, exchange, lambda blocks: blocks, near)
    near, near_beside = gathered(near)
    *late, near, near_beside = lax.optimization_barrier((*next_2, *last_2, near, near_beside))
    next_2, last_2 = late[:2], late[2:]
    far = call(
        far_kernel,
        array(16, 136, 128),
        [],
        [spot],
        *last_2,
        *next_1,
        *next_other,
        *next_2,
        square,
    )
    far, far_beside = gathered(exchange(far))
    sent = call(
        send_kernel, [array(128, 256)] * 2, [], [spot], far, far_beside, near, near_beside
    )
    got = [lax.ppermute(sent[k], ALL, routes(k)) for k in range(2)]
    gram = call(place_kernel, array(256, 256), [], [spot], *got)
    return weighted.reshape(snapshots.shape), gram


def solution(mesh):
    parts = jax.sharding.Mesh(mesh.devices.reshape(4, 2, 2, 8, 2), ALL)
    along, side, snap = ("y", "xh"), "xl", ("z", "core")
    placed = (P(along, side, None, snap), P(along, side, None), P(along, side, None, None))
    return jax.shard_map(
        body,
        mesh=parts,
        in_specs=placed,
        out_specs=(P(along, side, None, snap), P(snap, PLANE)),
        check_vma=False,
    )
```

time: 271 us -> 136 us (0.50)
  waiting for transfers between devices: 182 us -> 37 us
  blocking collectives: 0 us -> 42.9 us
  matrix products: 30.5 us -> 0 us
  starting transfers between devices: 14.5 us -> 32.6 us
  Pallas kernels: 0 us -> 15.4 us
  between operations: 14.3 us -> 1.58 us
  local copies, waits for them, and re-layouts: 17.4 us -> 4.74 us
  other arithmetic: 11 us -> 1.26 us
    all_gather x1 -> x0, waiting for transfers between devices: 99.1 us -> none  [body(): lax.all_gather(flattened, 'snap', axis=1, tiled=True)]
    reduce_scatter x1 -> x0, waiting for transfers between devices: 81.1 us -> none  [body(): lax.psum_scatter(row_sums, ('sx', 'sy'), scatter_dimension=1, tiled=True)]
    all_to_all x0 -> x2, blocking collectives: none -> 42.9 us  [exchange(): return lax.all_to_all(blocks, PLANE, 0, 0, tiled=True)]
    ppermute x4 -> x18, waiting for transfers between devices: 2.14 us -> 37 us  [the longest x1 9.6 us: body(): next_1 = [early[1], lax.ppermute(held[1], 'z', DOWN)]]
    dot_general x10 -> x0, matrix products: 30.5 us -> none  [the longest x1 18 us: pair_tile(): lax.dot_general(left, right, (((0,), (0,)), ((), ())), precision=lax.Prec...]
    ppermute x4 -> x18, starting transfers between devices: 14.2 us -> 32.6 us  [the longest x2 8.58 us: body(): got = [lax.ppermute(sent[k], ALL, routes(k)) for k in range(2)]]
    pallas_call x0 -> x8, Pallas kernels: none -> 15.4 us  [call(): pl.pallas_call(ordered, out_shape=shape, in_specs=[SMEM] * len(scalars) +...]
    reduce_sum x9 -> x0, local copies, waits for them, and re-layouts: 12.2 us -> none  [body(): jnp.sum(jnp.where((links == offset)[:, :, :, None, None], blocks, jnp.flo...]
  transfers between devices with their start and end apart: 6 -> 18, of which waited for: 3 -> 10; matrix products, arithmetic and copies ran while one was open for 11% -> 1% of each run, Pallas kernels for 0% -> 6%
where the time goes in v2:
time: 136 us; the launch traced here: 135 us
  blocking collectives  42.9 us (32%)
  waiting for transfers between devices  37 us (27%)
  starting transfers between devices  32.6 us (24%)
  Pallas kernels  15.4 us (11%)
  local copies, waits for them, and re-layouts  4.74 us (3%)
  between operations  1.58 us (1%)
    all_to_all x2, blocking collectives, exchange(): return lax.all_to_all(blocks, PLANE, 0, 0, tiled=True)  42.9 us
    pallas_call x8, Pallas kernels, call(): pl.pallas_call(ordered, out_shape=shape, in_specs=[SMEM] * len(scalars) +...  15.4 us
    ppermute x1, waiting for transfers between devices, body(): next_1 = [early[1], lax.ppermute(held[1], 'z', DOWN)]  9.6 us
    ppermute x2, waiting for transfers between devices, weigh(): early = [lax.ppermute(flat, 'z', UP), lax.ppermute(flat, 'z', DOWN)]  8.63 us
    ppermute x2, starting transfers between devices, body(): got = [lax.ppermute(sent[k], ALL, routes(k)) for k in range(2)]  8.58 us
    ppermute x2, waiting for transfers between devices, body(): got = [lax.ppermute(sent[k], ALL, routes(k)) for k in range(2)]  7.75 us
    ppermute x1, starting transfers between devices, weigh(): x_low = lax.ppermute(snapshots[3], along, [(i, i + 1) for i in range(7)])  6.07 us
    ppermute x2, waiting for transfers between devices, gathered(): return (total, lax.ppermute(total, 'xl', SWAP))  5.89 us
  transfers between devices with their start and end apart: 18, of which 10 were waited for; matrix products, arithmetic and copies ran while one was open for 1% of the time, Pallas kernels for 6%

profile of v2, /device:TPU:2, one launch (start us, length us, event | category | flops | bytes accessed | tf_op | source)
XLA Modules:
  0.0 135.4 jit_solution(13503072377970334615)
XLA Ops:
  0.6 0.0 copy-start.2
  0.6 0.0 copy-start.4
  0.7 1.2 fusion
  1.8 2.4 %collective-permute-start = (f32[4,64,256]{2,1,0:T(8,128)S(1)}, f32[4,64,256]{2,1,0:T(8,128)S(1)}, u32[]{:S(2)}, u32[]{:S(2)}) collective-permute-start(f32[4,64,256]{2,1,0:T(8,128)S(1)} %fusion), channel_id=1, source_target_pairs={{0,16},{16,0},{1,17},{17,1},{2,18},{18,2},{3,19},{19,3},{4,20},{20... | collective-permute-start | bytes 786440 | tf_op jit(solution)/shard_map/ppermute | solution.py:160
  4.2 1.1 slice_bitcast_fusion
  5.2 1.3 collective-permute-start.2
  6.5 6.1 %collective-permute-start.1 = (f32[4,64,256]{2,1,0:T(8,128)S(1)}, f32[4,64,256]{2,1,0:T(8,128)S(1)}, u32[]{:S(2)}, u32[]{:S(2)}) collective-permute-start(f32[4,64,256]{2,1,0:T(8,128)S(1)} %get-tuple-element.46), channel_id=1, source_target_pairs={{0,32},{32,64},{64,96},{96,128},{128,160},{160,192},{192,224},{1,3... | collective-permute-start | bytes 786440 | tf_op jit(solution)/shard_map/ppermute | solution.py:161
  12.7 0.0 copy-done.4
  12.7 0.1 copy.7
  12.8 0.1 select_reduce_fusion
  12.9 0.1 reshape.27.refs_1_
  13.0 0.1 stack.45.refs_0_
  13.1 0.0 collective-permute-done.refs_3_.refs_5_
  13.1 0.0 copy-done.2
  13.1 0.0 copy-start
  13.1 1.7 %copy-done = f32[4,4,9,4096]{3,1,2,0:T(4,128)S(1)} copy-done((f32[4,4,9,4096]{3,1,2,0:T(4,128)S(1)}, f32[4,4,9,4096]{3,1,2,0:T(4,128)}, u32[]{:S(2)}) %copy-start) | copy-done | bytes 2359320
  14.8 0.0 copy-start.1
  14.8 2.0 %shard_map.50 = (f32[8,64,256]{2,1,0:T(8,128)S(1)}, f32[8,64,256]{2,1,0:T(8,128)S(1)}) custom-call(s32[7]{0:T(128)S(1)} %stack.45.refs_0_, s32[144]{0:T(256)S(1)} %reshape.27.refs_1_, f32[16,64,256]{2,1,0:T(8,128)S(1)} %bitcast.28, f32[4,64,256]{2,1,0:T(8,128)S(1)} %collective-permute-done.refs_3_.refs_5_, f32[4,9,4,4096]{3,2,1,0:T(4,128)S(1)} %bitcast.26), custom_call_target="tpu_custom_call" | custom-call | flops 1 | bytes 1 | tf_op jit(solution)/shard_map/pallas_call | solution.py:31
  16.8 4.2 %collective-permute-start.5 = (f32[512,256]{1,0:T(8,128)S(1)}, f32[512,256]{1,0:T(8,128)S(1)}, u32[]{:S(2)}, u32[]{:S(2)}) collective-permute-start(f32[512,256]{1,0:T(8,128)S(1)} %bitcast.29), channel_id=1, source_target_pairs={{0,14},{2,0},{4,2},{6,4},{8,6},{10,8},{12,10},{14,12},{1,15},{3,1}... | collective-permute-start | bytes 1572872 | tf_op jit(solution)/shard_map/ppermute | solution.py:184
  21.0 0.0 collective-permute-start.4
  21.0 0.0 collective-permute-done.2.refs_4_
  21.0 0.0 collective-permute-done.1.refs_3_
  21.1 1.6 %collective-permute-start.3 = (f32[2,64,256]{2,1,0:T(8,128)S(1)}, f32[2,64,256]{2,1,0:T(8,128)S(1)}, u32[]{:S(2)}, u32[]{:S(2)}) collective-permute-start(f32[2,64,256]{2,1,0:T(8,128)S(1)} %maximum_select_fusion), channel_id=1, source_target_pairs={{0,16},{16,0},{1,17},{17,1},{2,18},{18,2},{3,19},{19,3},{4,20},{20... | collective-permute-start | bytes 393224 | tf_op jit(solution)/shard_map/ppermute | solution.py:189
  22.7 3.5 %collective-permute-done.3.refs_6_ = f32[2,64,256]{2,1,0:T(8,128)S(1)} collective-permute-done((f32[2,64,256]{2,1,0:T(8,128)S(1)}, f32[2,64,256]{2,1,0:T(8,128)S(1)}, u32[]{:S(2)}, u32[]{:S(2)}) %collective-permute-start.3) | collective-permute-done | bytes 131104 | tf_op jit(solution)/shard_map/ppermute | solution.py:189
  26.2 5.2 %collective-permute-done.5.refs_10_.refs_5_.refs_3_ = f32[512,256]{1,0:T(8,128)S(1)} collective-permute-done((f32[512,256]{1,0:T(8,128)S(1)}, f32[512,256]{1,0:T(8,128)S(1)}, u32[]{:S(2)}, u32[]{:S(2)}) %collective-permute-start.5) | collective-permute-done | bytes 524320 | tf_op jit(solution)/shard_map/ppermute | solution.py:184
  31.4 3.4 %collective-permute-done.4.refs_9_.refs_3_ = f32[512,256]{1,0:T(8,128)S(1)} collective-permute-done((f32[512,256]{1,0:T(8,128)S(1)}, f32[512,256]{1,0:T(8,128)S(1)}, u32[]{:S(2)}, u32[]{:S(2)}) %collective-permute-start.4) | collective-permute-done | bytes 524320 | tf_op jit(solution)/shard_map/ppermute | solution.py:184
  34.8 0.0 copy-done.1
  34.8 2.2 %shard_map.51 = (f32[8,64,256]{2,1,0:T(8,128)S(1)}, f32[16,64,256]{2,1,0:T(8,128)}) custom-call(s32[7]{0:T(128)S(1)} %stack.45.refs_0_, s32[144]{0:T(256)S(1)} %reshape.27.refs_1_, f32[8,64,256]{2,1,0:T(8,128)S(1)} %get-tuple-element.26.refs_2_, f32[4,64,256]{2,1,0:T(8,128)S(1)} %collective-permute-done.1.refs_3_, ...), custom_call_target="tpu_custom_call" | custom-call | flops 1 | bytes 1 | tf_op jit(solution)/shard_map/pallas_call | solution.py:31
  37.0 0.3 collective-permute-start.7
  37.3 1.7 %collective-permute-start.6 = (f32[512,256]{1,0:T(8,128)S(1)}, f32[512,256]{1,0:T(8,128)}, u32[]{:S(2)}, u32[]{:S(2)}) collective-permute-start(f32[512,256]{1,0:T(8,128)S(1)} %bitcast.33), channel_id=1, source_target_pairs={{0,2},{2,4},{4,6},{6,8},{8,10},{10,12},{12,14},{14,0},{1,3},{3,5},... | collective-permute-start | bytes 1572872 | tf_op jit(solution)/shard_map/ppermute | solution.py:375
  39.0 0.0 collective-permute-start.8
  39.1 9.6 %collective-permute-done.7.refs_6_.refs_4_ = f32[512,256]{1,0:T(8,128)S(1)} collective-permute-done((f32[512,256]{1,0:T(8,128)S(1)}, f32[512,256]{1,0:T(8,128)S(1)}, u32[]{:S(2)}, u32[]{:S(2)}) %collective-permute-start.7) | collective-permute-done | bytes 524320 | tf_op jit(solution)/shard_map/ppermute | solution.py:374
  48.6 0.0 collective-permute-start.9
  48.7 0.0 collective-permute-start.12
  48.7 1.6 %collective-permute-done.6.refs_4_ = f32[512,256]{1,0:T(8,128)} collective-permute-done((f32[512,256]{1,0:T(8,128)S(1)}, f32[512,256]{1,0:T(8,128)}, u32[]{:S(2)}, u32[]{:S(2)}) %collective-permute-start.6) | collective-permute-done | bytes 524320 | tf_op jit(solution)/shard_map/ppermute | solution.py:375
  50.3 0.2 collective-permute-start.13
  50.5 0.0 collective-permute-done.8.refs_7_.refs_5_
  50.5 0.1 collective-permute-done.9.refs_8_.refs_6_
  50.6 4.9 %shard_map.52 = (f32[16,128,128]{2,1,0:T(8,128)}, f32[4,136,128]{2,1,0:T(8,128)S(1)}, f32[512,256]{1,0:T(8,128)}, f32[512,256]{1,0:T(8,128)}) custom-call(s32[7]{0:T(128)S(1)} %stack.45.refs_0_, f32[512,256]{1,0:T(8,128)S(1)} %bitcast.31, f32[512,256]{1,0:T(8,128)S(1)} %bitcast.34, f32[512,256]{1,0:T(8,128)S(1)} %collective-permute-done.4.refs_9_.refs_3_, ...), custom_call_target="tpu_custom_call" | custom-call | flops 1 | bytes 1 | tf_op jit(solution)/shard_map/pallas_call | solution.py:31
  55.4 2.9 %collective-permute-start.10 = (f32[512,256]{1,0:T(8,128)}, f32[512,256]{1,0:T(8,128)}, u32[]{:S(2)}, u32[]{:S(2)}) collective-permute-start(f32[512,256]{1,0:T(8,128)} %get-tuple-element.33), channel_id=1, source_target_pairs={{0,14},{2,0},{4,2},{6,4},{8,6},{10,8},{12,10},{14,12},{1,15},{3,1}... | collective-permute-start | bytes 1572872 | tf_op jit(solution)/shard_map/ppermute | solution.py:388
  58.4 0.4 collective-permute-start.11
  58.8 0.5 slice.35
  60.0 25.5 %conditional.1 = (f32[16,128,128]{2,1,0:T(8,128)}) conditional(s32[]{:T(128)} %bitcast.16, f32[16,128,128]{2,1,0:T(8,128)} %get-tuple-element.35, f32[16,128,128]{2,1,0:T(8,128)} %get-tuple-element.35), branch_computations={%region_1.2_spmd, %region_2.3_spmd} | conditional | bytes 6291492 | solution.py:389
  60.0 0.0 copy-start.3
  60.0 1.2 copy-done.3
  61.2 24.3 %all_to_all.9 = f32[16,128,128]{2,1,0:T(8,128)} all-to-all(f32[16,128,128]{2,1,0:T(8,128)S(1)} %copy-done.3), channel_id=1, replica_groups=mesh['y'=4,'xh'=2,'xl'=2,'z'=8,'core'=2] {'y','xh','xl'}, dimensions={0} | all-to-all | bytes 2097152 | tf_op jit(solution)/shard_map/cond/branch_1_fun/all_to_all | solution.py:310
  85.5 1.3 shard_map.53.refs_3_
  86.8 1.5 %collective-permute-start.14 = (f32[128,128]{1,0:T(8,128)S(1)}, f32[128,128]{1,0:T(8,128)S(1)}, u32[]{:S(2)}, u32[]{:S(2)}) collective-permute-start(f32[128,128]{1,0:T(8,128)S(1)} %shard_map.53.refs_3_), channel_id=1, source_target_pairs={{0,16},{16,0},{1,17},{17,1},{2,18},{18,2},{3,19},{19,3},{4,20},{20... | collective-permute-start | bytes 196616 | tf_op jit(solution)/shard_map/ppermute | solution.py:315
  88.3 0.0 collective-permute-done.12.refs_1_
  88.3 0.0 collective-permute-done.13.refs_2_
  88.3 2.8 %collective-permute-done.14.refs_4_ = f32[128,128]{1,0:T(8,128)S(1)} collective-permute-done((f32[128,128]{1,0:T(8,128)S(1)}, f32[128,128]{1,0:T(8,128)S(1)}, u32[]{:S(2)}, u32[]{:S(2)}) %collective-permute-start.14) | collective-permute-done | bytes 65568 | tf_op jit(solution)/shard_map/ppermute | solution.py:315
  91.1 0.0 collective-permute-done.10.refs_7_
  91.1 0.0 collective-permute-done.11.refs_8_
  91.1 2.8 %shard_map.54 = f32[16,136,128]{2,1,0:T(8,128)S(1)} custom-call(s32[7]{0:T(128)S(1)} %stack.45.refs_0_, f32[512,256]{1,0:T(8,128)S(1)} %collective-permute-done.12.refs_1_, f32[512,256]{1,0:T(8,128)} %collective-permute-done.13.refs_2_, f32[512,256]{1,0:T(8,128)S(1)} %collective-permute-done.5.refs_10_.refs_5_.refs_3_, ...), custom_call_target="tpu_custom_call" | custom-call | flops 1 | bytes 1 | tf_op jit(solution)/shard_map/pallas_call | solution.py:31
  94.0 18.6 %all_to_all.10.refs_0_ = f32[16,136,128]{2,1,0:T(8,128)S(1)} all-to-all(f32[16,136,128]{2,1,0:T(8,128)S(1)} %shard_map.54), channel_id=1, replica_groups=mesh['y'=4,'xh'=2,'xl'=2,'z'=8,'core'=2] {'y','xh','xl'}, dimensions={0} | all-to-all | bytes 2228224 | tf_op jit(solution)/shard_map/all_to_all | solution.py:310
  112.6 0.1 shard_map.55.refs_1_
  112.6 1.3 collective-permute-start.15
  114.0 3.1 %collective-permute-done.15.refs_2_ = f32[136,128]{1,0:T(8,128)S(1)} collective-permute-done((f32[136,128]{1,0:T(8,128)S(1)}, f32[136,128]{1,0:T(8,128)S(1)}, u32[]{:S(2)}, u32[]{:S(2)}) %collective-permute-start.15) | collective-permute-done | bytes 69664 | tf_op jit(solution)/shard_map/ppermute | solution.py:315
  117.0 0.7 shard_map.56
  117.7 3.3 %collective-permute-start.16 = (f32[128,256]{1,0:T(8,128)S(1)}, f32[128,256]{1,0:T(8,128)S(1)}, u32[]{:S(2)}, u32[]{:S(2)}) collective-permute-start(f32[128,256]{1,0:T(8,128)S(1)} %get-tuple-element.43), channel_id=1, source_target_pairs={{0,44},{1,33},{2,78},{3,67},{4,96},{5,101},{6,130},{7,135},{8,164}... | collective-permute-start | bytes 393224 | tf_op jit(solution)/shard_map/ppermute | solution.py:408
  121.0 5.3 %collective-permute-start.17 = (f32[128,256]{1,0:T(8,128)S(1)}, f32[128,256]{1,0:T(8,128)S(1)}, u32[]{:S(2)}, u32[]{:S(2)}) collective-permute-start(f32[128,256]{1,0:T(8,128)S(1)} %get-tuple-element.44), channel_id=1, source_target_pairs={{0,32},{1,45},{2,66},{3,79},{4,100},{5,97},{6,134},{7,131},{8,168}... | collective-permute-start | bytes 393224 | tf_op jit(solution)/shard_map/ppermute | solution.py:408
  126.3 2.8 %collective-permute-done.16.refs_1_ = f32[128,256]{1,0:T(8,128)S(1)} collective-permute-done((f32[128,256]{1,0:T(8,128)S(1)}, f32[128,256]{1,0:T(8,128)S(1)}, u32[]{:S(2)}, u32[]{:S(2)}) %collective-permute-start.16) | collective-permute-done | bytes 131104 | tf_op jit(solution)/shard_map/ppermute | solution.py:408
  129.1 5.0 %collective-permute-done.17.refs_2_ = f32[128,256]{1,0:T(8,128)S(1)} collective-permute-done((f32[128,256]{1,0:T(8,128)S(1)}, f32[128,256]{1,0:T(8,128)S(1)}, u32[]{:S(2)}, u32[]{:S(2)}) %collective-permute-start.17) | collective-permute-done | bytes 131104 | tf_op jit(solution)/shard_map/ppermute | solution.py:408
  134.1 1.4 %shard_map.57 = f32[256,256]{1,0:T(8,128)} custom-call(s32[7]{0:T(128)S(1)} %stack.45.refs_0_, f32[128,256]{1,0:T(8,128)S(1)} %collective-permute-done.16.refs_1_, f32[128,256]{1,0:T(8,128)S(1)} %collective-permute-done.17.refs_2_), custom_call_target="tpu_custom_call" | custom-call | flops 1 | bytes 1 | tf_op jit(solution)/shard_map/pallas_call | solution.py:31
  (2 shorter events, 0.0 us)
Async XLA Ops:
  0.6 12.5 %copy-start.2 = (f32[4,4,64,256]{3,2,1,0:T(8,128)S(1)}, f32[4,4,64,256]{3,2,1,0:T(8,128)}, u32[]{:S(2)}) copy-start(f32[4,4,64,256]{3,2,1,0:T(8,128)} %param.5) | copy-start | bytes 3145732
  0.6 12.1 %copy-start.4 = (s32[4,4,9]{2,1,0:T(4,128)S(1)}, s32[4,4,9]{2,1,0:T(4,128)}, u32[]{:S(2)}) copy-start(s32[4,4,9]{2,1,0:T(4,128)} %param.6) | copy-start | bytes 1732
  1.8 11.3 %collective-permute-start = (f32[4,64,256]{2,1,0:T(8,128)S(1)}, f32[4,64,256]{2,1,0:T(8,128)S(1)}, u32[]{:S(2)}, u32[]{:S(2)}) collective-permute-start(f32[4,64,256]{2,1,0:T(8,128)S(1)} %fusion), channel_id=1, source_target_pairs={{0,16},{16,0},{1,17},{17,1},{2,18},{18,2},{3,19},{19,3},{4,20},{20... | collective-permute-start | bytes 786440 | tf_op jit(solution)/shard_map/ppermute | solution.py:160
  5.2 15.8 %collective-permute-start.2 = (f32[4,64,256]{2,1,0:T(8,128)S(1)}, f32[4,64,256]{2,1,0:T(8,128)S(1)}, u32[]{:S(2)}, u32[]{:S(2)}) collective-permute-start(f32[4,64,256]{2,1,0:T(8,128)S(1)} %get-tuple-element.45), channel_id=1, source_target_pairs={{32,0},{64,32},{96,64},{128,96},{160,128},{192,160},{224,192},{33,... | collective-permute-start | bytes 786440 | tf_op jit(solution)/shard_map/ppermute | solution.py:162
  6.5 14.5 %collective-permute-start.1 = (f32[4,64,256]{2,1,0:T(8,128)S(1)}, f32[4,64,256]{2,1,0:T(8,128)S(1)}, u32[]{:S(2)}, u32[]{:S(2)}) collective-permute-start(f32[4,64,256]{2,1,0:T(8,128)S(1)} %get-tuple-element.46), channel_id=1, source_target_pairs={{0,32},{32,64},{64,96},{96,128},{128,160},{160,192},{192,224},{1,3... | collective-permute-start | bytes 786440 | tf_op jit(solution)/shard_map/ppermute | solution.py:161
  13.1 1.7 %copy-start = (f32[4,4,9,4096]{3,1,2,0:T(4,128)S(1)}, f32[4,4,9,4096]{3,1,2,0:T(4,128)}, u32[]{:S(2)}) copy-start(f32[4,4,9,4096]{3,1,2,0:T(4,128)} %param.7) | copy-start | bytes 7077892
  14.8 20.0 %copy-start.1 = (f32[4,4,9,4096]{3,1,2,0:T(4,128)S(1)}, f32[4,4,9,4096]{3,1,2,0:T(4,128)}, u32[]{:S(2)}) copy-start(f32[4,4,9,4096]{3,1,2,0:T(4,128)} %param.7) | copy-start | bytes 7077892
  16.8 14.6 %collective-permute-start.5 = (f32[512,256]{1,0:T(8,128)S(1)}, f32[512,256]{1,0:T(8,128)S(1)}, u32[]{:S(2)}, u32[]{:S(2)}) collective-permute-start(f32[512,256]{1,0:T(8,128)S(1)} %bitcast.29), channel_id=1, source_target_pairs={{0,14},{2,0},{4,2},{6,4},{8,6},{10,8},{12,10},{14,12},{1,15},{3,1}... | collective-permute-start | bytes 1572872 | tf_op jit(solution)/shard_map/ppermute | solution.py:184
  21.0 13.8 %collective-permute-start.4 = (f32[512,256]{1,0:T(8,128)S(1)}, f32[512,256]{1,0:T(8,128)S(1)}, u32[]{:S(2)}, u32[]{:S(2)}) collective-permute-start(f32[512,256]{1,0:T(8,128)S(1)} %bitcast.30), channel_id=1, source_target_pairs={{0,2},{2,4},{4,6},{6,8},{8,10},{10,12},{12,14},{14,0},{1,3},{3,5},... | collective-permute-start | bytes 1572872 | tf_op jit(solution)/shard_map/ppermute | solution.py:184
  21.1 5.1 %collective-permute-start.3 = (f32[2,64,256]{2,1,0:T(8,128)S(1)}, f32[2,64,256]{2,1,0:T(8,128)S(1)}, u32[]{:S(2)}, u32[]{:S(2)}) collective-permute-start(f32[2,64,256]{2,1,0:T(8,128)S(1)} %maximum_select_fusion), channel_id=1, source_target_pairs={{0,16},{16,0},{1,17},{17,1},{2,18},{18,2},{3,19},{19,3},{4,20},{20... | collective-permute-start | bytes 393224 | tf_op jit(solution)/shard_map/ppermute | solution.py:189
  37.0 11.6 %collective-permute-start.7 = (f32[512,256]{1,0:T(8,128)S(1)}, f32[512,256]{1,0:T(8,128)S(1)}, u32[]{:S(2)}, u32[]{:S(2)}) collective-permute-start(f32[512,256]{1,0:T(8,128)S(1)} %bitcast.32), channel_id=1, source_target_pairs={{0,14},{2,0},{4,2},{6,4},{8,6},{10,8},{12,10},{14,12},{1,15},{3,1}... | collective-permute-start | bytes 1572872 | tf_op jit(solution)/shard_map/ppermute | solution.py:374
  37.3 12.9 %collective-permute-start.6 = (f32[512,256]{1,0:T(8,128)S(1)}, f32[512,256]{1,0:T(8,128)}, u32[]{:S(2)}, u32[]{:S(2)}) collective-permute-start(f32[512,256]{1,0:T(8,128)S(1)} %bitcast.33), channel_id=1, source_target_pairs={{0,2},{2,4},{4,6},{6,8},{8,10},{10,12},{12,14},{14,0},{1,3},{3,5},... | collective-permute-start | bytes 1572872 | tf_op jit(solution)/shard_map/ppermute | solution.py:375
  39.0 11.5 %collective-permute-start.8 = (f32[512,256]{1,0:T(8,128)S(1)}, f32[512,256]{1,0:T(8,128)S(1)}, u32[]{:S(2)}, u32[]{:S(2)}) collective-permute-start(f32[512,256]{1,0:T(8,128)S(1)} %collective-permute-done.5.refs_10_.refs_5_.refs_3_), channel_id=1, source_target_pairs={{0,1},{1,0},{2,3},{3,2},{4,5},{5,4},{6,7},{7,6},{8,9},{9,8},{10,11... | collective-permute-start | bytes 1572872 | tf_op jit(solution)/shard_map/ppermute | solution.py:377
  48.6 1.9 %collective-permute-start.9 = (f32[512,256]{1,0:T(8,128)S(1)}, f32[512,256]{1,0:T(8,128)S(1)}, u32[]{:S(2)}, u32[]{:S(2)}) collective-permute-start(f32[512,256]{1,0:T(8,128)S(1)} %collective-permute-done.7.refs_6_.refs_4_), channel_id=1, source_target_pairs={{0,1},{1,0},{2,3},{3,2},{4,5},{5,4},{6,7},{7,6},{8,9},{9,8},{10,11... | collective-permute-start | bytes 1572872 | tf_op jit(solution)/shard_map/ppermute | solution.py:377
  48.7 39.6 %collective-permute-start.12 = (f32[512,256]{1,0:T(8,128)S(1)}, f32[512,256]{1,0:T(8,128)S(1)}, u32[]{:S(2)}, u32[]{:S(2)}) collective-permute-start(f32[512,256]{1,0:T(8,128)S(1)} %collective-permute-done.4.refs_9_.refs_3_), channel_id=1, source_target_pairs={{0,2},{2,4},{4,6},{6,8},{8,10},{10,12},{12,14},{14,0},{1,3},{3,5},... | collective-permute-start | bytes 1572872 | tf_op jit(solution)/shard_map/ppermute | solution.py:376
  50.3 38.0 %collective-permute-start.13 = (f32[512,256]{1,0:T(8,128)}, f32[512,256]{1,0:T(8,128)}, u32[]{:S(2)}, u32[]{:S(2)}) collective-permute-start(f32[512,256]{1,0:T(8,128)} %collective-permute-done.6.refs_4_), channel_id=1, source_target_pairs={{0,2},{2,4},{4,6},{6,8},{8,10},{10,12},{12,14},{14,0},{1,3},{3,5},... | collective-permute-start | bytes 1572872 | tf_op jit(solution)/shard_map/ppermute | solution.py:376
  55.4 35.7 %collective-permute-start.10 = (f32[512,256]{1,0:T(8,128)}, f32[512,256]{1,0:T(8,128)}, u32[]{:S(2)}, u32[]{:S(2)}) collective-permute-start(f32[512,256]{1,0:T(8,128)} %get-tuple-element.33), channel_id=1, source_target_pairs={{0,14},{2,0},{4,2},{6,4},{8,6},{10,8},{12,10},{14,12},{1,15},{3,1}... | collective-permute-start | bytes 1572872 | tf_op jit(solution)/shard_map/ppermute | solution.py:388
  58.4 32.7 %collective-permute-start.11 = (f32[512,256]{1,0:T(8,128)}, f32[512,256]{1,0:T(8,128)}, u32[]{:S(2)}, u32[]{:S(2)}) collective-permute-start(f32[512,256]{1,0:T(8,128)} %get-tuple-element.34), channel_id=1, source_target_pairs={{0,14},{2,0},{4,2},{6,4},{8,6},{10,8},{12,10},{14,12},{1,15},{3,1}... | collective-permute-start | bytes 1572872 | tf_op jit(solution)/shard_map/ppermute | solution.py:388
  60.0 1.2 copy-start.3
  86.8 4.4 %collective-permute-start.14 = (f32[128,128]{1,0:T(8,128)S(1)}, f32[128,128]{1,0:T(8,128)S(1)}, u32[]{:S(2)}, u32[]{:S(2)}) collective-permute-start(f32[128,128]{1,0:T(8,128)S(1)} %shard_map.53.refs_3_), channel_id=1, source_target_pairs={{0,16},{16,0},{1,17},{17,1},{2,18},{18,2},{3,19},{19,3},{4,20},{20... | collective-permute-start | bytes 196616 | tf_op jit(solution)/shard_map/ppermute | solution.py:315
  112.6 4.4 %collective-permute-start.15 = (f32[136,128]{1,0:T(8,128)S(1)}, f32[136,128]{1,0:T(8,128)S(1)}, u32[]{:S(2)}, u32[]{:S(2)}) collective-permute-start(f32[136,128]{1,0:T(8,128)S(1)} %shard_map.55.refs_1_), channel_id=1, source_target_pairs={{0,16},{16,0},{1,17},{17,1},{2,18},{18,2},{3,19},{19,3},{4,20},{20... | collective-permute-start | bytes 208904 | tf_op jit(solution)/shard_map/ppermute | solution.py:315
  117.7 11.4 %collective-permute-start.16 = (f32[128,256]{1,0:T(8,128)S(1)}, f32[128,256]{1,0:T(8,128)S(1)}, u32[]{:S(2)}, u32[]{:S(2)}) collective-permute-start(f32[128,256]{1,0:T(8,128)S(1)} %get-tuple-element.43), channel_id=1, source_target_pairs={{0,44},{1,33},{2,78},{3,67},{4,96},{5,101},{6,130},{7,135},{8,164}... | collective-permute-start | bytes 393224 | tf_op jit(solution)/shard_map/ppermute | solution.py:408
  121.0 13.1 %collective-permute-start.17 = (f32[128,256]{1,0:T(8,128)S(1)}, f32[128,256]{1,0:T(8,128)S(1)}, u32[]{:S(2)}, u32[]{:S(2)}) collective-permute-start(f32[128,256]{1,0:T(8,128)S(1)} %get-tuple-element.44), channel_id=1, source_target_pairs={{0,32},{1,45},{2,66},{3,79},{4,100},{5,97},{6,134},{7,131},{8,168}... | collective-permute-start | bytes 393224 | tf_op jit(solution)/shard_map/ppermute | solution.py:408

commit v3 on v2

--- a/solution.py
+++ b/solution.py
@@ -12,9 +12,18 @@
 SWAP = [(0, 1), (1, 0)]
 UP = [(k, (k + 1) % 8) for k in range(8)]
 DOWN = [(k, (k - 1) % 8) for k in range(8)]
+
+
+def turned(z):
+    return (z + 3) % 8 // 4 ^ 1
+
+
+DOWN_TURNED = [
+    (2 * k + c, 2 * ((k - 1) % 8) + (c ^ turned(k - 1))) for k in range(8) for c in range(2)
+]
 VMEM = pl.BlockSpec(memory_space=pltpu.VMEM)
 SMEM = pl.BlockSpec(memory_space=pltpu.SMEM)
-CORE, SIDE, ROW, COLUMN, TURN, MIRROR, KEEP = range(7)
+CORE, SIDE, ROW, COLUMN, TURN, MIRROR, OWN = range(7)
 
 
 def split(value):
@@ -181,7 +190,7 @@
         mass,
     )
     flat = mid.reshape(8 * BLK, cols)
-    early = [lax.ppermute(flat, "z", UP), lax.ppermute(flat, "z", DOWN)]
+    early = [lax.ppermute(flat, "z", UP), lax.ppermute(flat, ("z", "core"), DOWN_TURNED)]
     x_low, x_high, mid = lax.optimization_barrier((x_low, x_high, mid))
     corners = jnp.where(
         side == 0, jnp.stack([x_low[3], x_high[3]]), jnp.stack([x_low[0], x_high[0]])
@@ -199,7 +208,7 @@
         corners,
         mass,
         mid,
-        after=early,
+        after=early[:1],
     )
     return flat, outer.reshape(8 * BLK, cols), weighted, early
 
@@ -226,16 +235,10 @@
             out[at + 4 * i + j, :128, :] = block[i * 128 : i * 128 + 128, j * 128 : j * 128 + 128]
 
 
-def near_kernel(spot, *refs):
-    *arrays, out, square, relay_a, relay_b = refs
-    mine = spot[CORE]
-    for relay, own, other in zip((relay_a, relay_b), arrays[4:6], arrays[6:8]):
-        relay[...] = jnp.where(spot[KEEP] == 1, own[...], other[...])
-    held, last, own, other = [whole(arrays[k : k + 2]) for k in range(0, 8, 2)]
-    for side, right in ((mine, own), (1 - mine, other)):
-        lay(out, 2 * side, dot(held, right))
-        lay(out, 8 + 2 * side, dot(last, right))
-    first = mine == 0
+def square_kernel(spot, *refs):
+    *arrays, square = refs
+    own, other = whole(arrays[:2]), whole(arrays[2:])
+    first = spot[CORE] == 0
     left = tuple(
         jnp.where(first, a, b) for a, b in zip(columns(own, 0, 128), columns(other, 128, 256))
     )
@@ -253,16 +256,26 @@
     square[3, :128, :] = diagonal[:128, 128:]
 
 
-def far_kernel(spot, *refs):
+def near_kernel(spot, *refs):
     *arrays, square, out = refs
     mine = spot[CORE]
-    last, own, other, opposite = [whole(arrays[k : k + 2]) for k in range(0, 8, 2)]
+    held, beside, last, own = [whole(arrays[k : k + 2]) for k in range(0, 8, 2)]
     out[:, 128:, :] = jnp.zeros((16, 8, 128), jnp.float32)
-    for side, right in ((mine, own), (1 - mine, other)):
-        lay(out, 2 * side, dot(last, right))
-    lay(out, 8, dot(last, opposite))
+    lay(out, 2 * mine, dot(own, held))
+    lay(out, 2 * (1 - mine), dot(own, beside))
+    lay(out, 8, dot(last, own))
     out[10:12] = square[:2]
     out[14:16] = square[2:]
+
+
+def far_kernel(spot, *refs):
+    *arrays, out = refs
+    mine = spot[OWN]
+    last_2, own, other, opposite, last_1 = [whole(arrays[k : k + 2]) for k in range(0, 10, 2)]
+    lay(out, 2 * mine, dot(last_2, own))
+    lay(out, 2 * (1 - mine), dot(last_2, other))
+    lay(out, 8, dot(last_2, opposite))
+    lay(out, 10, dot(last_1, other))
 
 
 def add_kernel(blocks, out):
@@ -275,8 +288,8 @@
 def send_kernel(spot, far, far_beside, near, near_beside, *outs):
     y, x, core = spot[ROW], spot[COLUMN], spot[CORE]
     beside = x % 2
-    even = jnp.where(beside == 0, far[...], far_beside[...])
-    odd = jnp.where(beside == 0, far_beside[...], far[...])[:128]
+    even = jnp.where(beside == 0, near[...], near_beside[...])
+    odd = jnp.where(beside == 0, near_beside[...], near[...])[:128]
     row = lax.broadcasted_iota(jnp.int32, (128, 128), 0)
     column = lax.broadcasted_iota(jnp.int32, (128, 128), 1)
     packed = even[:128]
@@ -287,12 +300,12 @@
     diagonal = (y == 3) & (x >= 2)
     lefts = jnp.where(diagonal, jnp.where(beside == 0, upper, odd.T), packed)
     rights = jnp.where(diagonal & (beside == 1), lower, odd)
-    near_left = jnp.where(beside == 0, near[...], near_beside[...])
-    near_right = jnp.where(beside == 0, near_beside[...], near[...])
+    far_left = jnp.where(beside == 0, far[...], far_beside[...])
+    far_right = jnp.where(beside == 0, far_beside[...], far[...])
     late = (y + beside + core) % 2
     for turn in range(2):
-        outs[turn][:, :128] = jnp.where(late == turn, lefts, near_left)
-        outs[turn][:, 128:] = jnp.where(late == turn, rights, near_right)
+        outs[turn][:, :128] = jnp.where(late == turn, far_left, lefts)
+        outs[turn][:, 128:] = jnp.where(late == turn, far_right, rights)
 
 
 def place_kernel(spot, first, second, out):
@@ -333,25 +346,20 @@
                     mirror = j % 2 == 1
                     here = flat(z, core, 4 * i + j)
                     column = j // 2
+                    row = core
                     if i < 2:
-                        a, b = (z - 2, z + 1) if late else (z, z + 1)
-                    elif not late:
-                        a, b = z - 1, z + 1
-                    elif j < 2:
+                        a, b = (z - 2, z + 1) if late else (z + 1, z)
+                        row = core if late else core ^ turned(z)
+                    elif j < 2 and late:
                         a, b, column = z - 2, z + 2, crossed(z, core)
+                    elif j < 2 or late:
+                        a, b, column = z - 1, z + 1, core ^ turned(z) ^ late
                     else:
-                        row = 0 if i == 2 else core
-                        column = 1 if i == 2 else core
-                        if i == 3:
-                            mirror = False
-                        a = b = z + 1
-                        pairs.append(
-                            (here, flat(b, column, 2 * a + row) if mirror else flat(a, row, 2 * b + column))
-                        )
-                        continue
-                    pairs.append(
-                        (here, flat(b, column, 2 * a + core) if mirror else flat(a, core, 2 * b + column))
-                    )
+                        a = b = z
+                        row, column = (0, 1) if i == 2 else (core, core)
+                        mirror = mirror and i == 2
+                    there = flat(b, column, 2 * a + row) if mirror else flat(a, row, 2 * b + column)
+                    pairs.append((here, there))
     return pairs
 
 
@@ -361,46 +369,59 @@
     other = x % 2
     apart = ((4 * y + x) // 2 - z) % 8
     straight = other == jnp.where((z + 2) % 8 < 4, core, 1 - core)
-    mirror = (apart > 4) | ((apart == 4) & jnp.logical_not(straight))
+    same = core == other
+    after_same = other == core ^ turned(z + 1)
+    before_same = core == other ^ turned(z + 7)
+    mirror = (apart == 1) | (apart == 5) | (apart == 6)
+    mirror = mirror | ((apart == 4) & jnp.logical_not(straight))
     mirror = mirror | ((apart == 0) & (core == 1) & (other == 0))
-    turn = jnp.where(mirror, 1 - other, core)
-    turn = jnp.where((apart == 1) | (apart == 2) | ((apart == 0) & (core == other)), 1 - core, turn)
-    turn = jnp.where(apart > 5, other, turn)
-    turn = jnp.where((apart == 0) & (core != other), core, turn)
-    keep = (z + 7) % 8 < 4
-    spot = [core, lax.axis_index("xl"), y, x, turn, mirror, keep]
+    turns = (
+        jnp.where(same, core, 1 - core),
+        other ^ turned(z),
+        jnp.where(after_same, 1 - core, core),
+        core,
+        jnp.where(straight, core, 1 - other),
+        1 - other,
+        jnp.where(before_same, other, 1 - other),
+        1 - core ^ turned(z + 7),
+    )
+    turn = sum(jnp.where(apart == k, value, 0) for k, value in enumerate(turns))
+    spot = [core, lax.axis_index("xl"), y, x, turn, mirror, core ^ turned(z)]
     spot = jnp.stack([jnp.asarray(value).astype(jnp.int32) for value in spot])
     *held, weighted, early = weigh(spot, snapshots, links, mass)
-    next_1 = [early[1], lax.ppermute(held[1], "z", DOWN)]
+    next_1 = [early[1], lax.ppermute(held[1], ("z", "core"), DOWN_TURNED)]
     last_1 = [early[0], lax.ppermute(held[1], "z", UP)]
+    held_other = [lax.ppermute(half, "core", SWAP) for half in held]
+    square = call(square_kernel, array(4, 136, 128), [], [spot], *held, *held_other)
+    next_1[1], last_1[1], square = lax.optimization_barrier((next_1[1], last_1[1], square))
     last_2 = [lax.ppermute(half, "z", UP) for half in last_1]
     next_other = [lax.ppermute(half, "core", SWAP) for half in next_1]
-    near, square, *relay = call(
+    near = call(
         near_kernel,
-        [array(16, 128, 128), array(4, 136, 128)] + [array(*held[0].shape)] * 2,
+        array(16, 136, 128),
         [],
         [spot],
         *held,
+        *held_other,
         *last_1,
         *next_1,
-        *next_other,
-    )
-    next_2 = [lax.ppermute(half, "z", DOWN) for half in relay]
+        square,
+    )
+    next_2 = [lax.ppermute(half, "z", DOWN) for half in next_1]
     near = lax.cond(links[0, 0, 0] >= 0, exchange, lambda blocks: blocks, near)
-    near, near_beside = gathered(near)
-    *late, near, near_beside = lax.optimization_barrier((*next_2, *last_2, near, near_beside))
-    next_2, last_2 = late[:2], late[2:]
     far = call(
         far_kernel,
-        array(16, 136, 128),
+        array(16, 128, 128),
         [],
         [spot],
         *last_2,
         *next_1,
         *next_other,
         *next_2,
-        square,
-    )
+        *last_1,
+        after=(near,),
+    )
+    near, near_beside = gathered(near)
     far, far_beside = gathered(exchange(far))
     sent = call(
         send_kernel, [array(128, 256)] * 2, [], [spot], far, far_beside, near, near_beside

time: 136 us -> 132 us (0.971); the launches traced: 135 us -> 130 us
  blocking collectives: 42.9 us -> 25.9 us
  waiting for transfers between devices: 37 us -> 46.5 us
  starting transfers between devices: 32.6 us -> 34.3 us
    all_to_all x2 -> x1, blocking collectives: 42.9 us -> 25.9 us  [exchange(): return lax.all_to_all(blocks, PLANE, 0, 0, tiled=True)]
    all_to_all x0 -> x1, waiting for transfers between devices: none -> 15.5 us  [exchange(): return lax.all_to_all(blocks, PLANE, 0, 0, tiled=True)]
    ppermute x5 -> x7, waiting for transfers between devices: 18.2 us -> 11.1 us  [the longest x1 7.52 us: body(): next_1 = [early[1], lax.ppermute(held[1], ('z', 'core'), DOWN_TURNED)]]
    ppermute x5 -> x7, starting transfers between devices: 7.88 us -> 13.5 us  [the longest x2 6.53 us: body(): next_2 = [lax.ppermute(half, 'z', DOWN) for half in next_1]]
    all_to_all x0 -> x1, starting transfers between devices: none -> 5.03 us  [exchange(): return lax.all_to_all(blocks, PLANE, 0, 0, tiled=True)]
    ppermute x1, waiting for transfers between devices: 0.01 us -> 3.69 us  [weigh(): x_high = lax.ppermute(snapshots[0], along, [(i + 1, i) for i in range(7)])]
    ppermute x1, starting transfers between devices: 6.07 us -> 2.6 us  [weigh(): x_low = lax.ppermute(snapshots[3], along, [(i, i + 1) for i in range(7)])]
    ppermute x2, waiting for transfers between devices: 5.89 us -> 2.81 us  [gathered(): return (total, lax.ppermute(total, 'xl', SWAP))]
  transfers between devices with their start and end apart: 18 -> 21, of which waited for: 10 -> 10; matrix products, arithmetic and copies ran while one was open for 1% -> 2% of each run, Pallas kernels for 6% -> 7%
where the time goes in v3:
time: 132 us; the launch traced here: 130 us
  waiting for transfers between devices  46.5 us (35%)
  starting transfers between devices  34.3 us (26%)
  blocking collectives  25.9 us (20%)
  Pallas kernels  15.3 us (12%)
  local copies, waits for them, and re-layouts  4.78 us (4%)
  between operations  1.73 us (1%)
    all_to_all x1, blocking collectives, exchange(): return lax.all_to_all(blocks, PLANE, 0, 0, tiled=True)  25.9 us
    all_to_all x1, waiting for transfers between devices, exchange(): return lax.all_to_all(blocks, PLANE, 0, 0, tiled=True)  15.5 us
    pallas_call x9, Pallas kernels, call(): pl.pallas_call(ordered, out_shape=shape, in_specs=[SMEM] * len(scalars) +...  15.3 us
    ppermute x1, waiting for transfers between devices, body(): next_1 = [early[1], lax.ppermute(held[1], ('z', 'core'), DOWN_TURNED)]  7.52 us
    ppermute x2, starting transfers between devices, body(): next_2 = [lax.ppermute(half, 'z', DOWN) for half in next_1]  6.53 us
    ppermute x2, waiting for transfers between devices, body(): got = [lax.ppermute(sent[k], ALL, routes(k)) for k in range(2)]  6.17 us
    ppermute x2, starting transfers between devices, body(): got = [lax.ppermute(sent[k], ALL, routes(k)) for k in range(2)]  5.73 us
    all_to_all x1, starting transfers between devices, exchange(): return lax.all_to_all(blocks, PLANE, 0, 0, tiled=True)  5.03 us
  transfers between devices with their start and end apart: 21, of which 10 were waited for; matrix products, arithmetic and copies ran while one was open for 2% of the time, Pallas kernels for 7%

profile of v3, /device:TPU:2, one launch (start us, length us, event | category | flops | bytes accessed | tf_op | source)
XLA Modules:
  0.0 129.7 jit_solution(6853215011425196370)
XLA Ops:
  0.6 0.0 copy-start.5
  0.6 0.0 copy-start.2
  0.7 1.2 fusion
  1.8 2.4 %collective-permute-start = (f32[4,64,256]{2,1,0:T(8,128)S(1)}, f32[4,64,256]{2,1,0:T(8,128)S(1)}, u32[]{:S(2)}, u32[]{:S(2)}) collective-permute-start(f32[4,64,256]{2,1,0:T(8,128)S(1)} %fusion), channel_id=1, source_target_pairs={{0,16},{16,0},{1,17},{17,1},{2,18},{18,2},{3,19},{19,3},{4,20},{20... | collective-permute-start | bytes 786440 | tf_op jit(solution)/shard_map/ppermute | solution.py:169
  4.2 1.1 slice_bitcast_fusion
  5.3 2.6 %collective-permute-start.1 = (f32[4,64,256]{2,1,0:T(8,128)S(1)}, f32[4,64,256]{2,1,0:T(8,128)S(1)}, u32[]{:S(2)}, u32[]{:S(2)}) collective-permute-start(f32[4,64,256]{2,1,0:T(8,128)S(1)} %get-tuple-element.32), channel_id=1, source_target_pairs={{0,32},{32,64},{64,96},{96,128},{128,160},{160,192},{192,224},{1,3... | collective-permute-start | bytes 786440 | tf_op jit(solution)/shard_map/ppermute | solution.py:170
  7.9 1.3 collective-permute-start.2
  9.4 0.1 copy.7
  9.5 0.1 select_reduce_fusion
  9.6 0.1 reshape.27.refs_1_
  9.7 0.1 stack.41.refs_0_
  9.8 0.3 collective-permute-done.refs_3_.refs_5_
  10.1 1.7 %copy-done = f32[4,4,9,4096]{3,1,2,0:T(4,128)S(1)} copy-done((f32[4,4,9,4096]{3,1,2,0:T(4,128)S(1)}, f32[4,4,9,4096]{3,1,2,0:T(4,128)}, u32[]{:S(2)}) %copy-start) | copy-done | bytes 2359320
  11.8 2.0 %shard_map.50 = (f32[8,64,256]{2,1,0:T(8,128)S(1)}, f32[8,64,256]{2,1,0:T(8,128)S(1)}) custom-call(s32[7]{0:T(128)S(1)} %stack.41.refs_0_, s32[144]{0:T(256)S(1)} %reshape.27.refs_1_, f32[16,64,256]{2,1,0:T(8,128)S(1)} %bitcast.33, f32[4,64,256]{2,1,0:T(8,128)S(1)} %collective-permute-done.refs_3_.refs_5_, f32[4,9,4,4096]{3,2,1,0:T(4,128)S(1)} %bitcast.26), custom_call_target="tpu_custom_call" | custom-call | flops 1 | bytes 1 | tf_op jit(solution)/shard_map/pallas_call | solution.py:40
  13.8 2.0 %collective-permute-start.4 = (f32[512,256]{1,0:T(8,128)S(1)}, f32[512,256]{1,0:T(8,128)S(1)}, u32[]{:S(2)}, u32[]{:S(2)}) collective-permute-start(f32[512,256]{1,0:T(8,128)S(1)} %bitcast.28), channel_id=1, source_target_pairs={{0,2},{2,4},{4,6},{6,8},{8,10},{10,12},{12,14},{14,0},{1,3},{3,5},... | collective-permute-start | bytes 1572872 | tf_op jit(solution)/shard_map/ppermute | solution.py:193
  15.8 2.6 %collective-permute-start.11 = (f32[512,256]{1,0:T(8,128)S(1)}, f32[512,256]{1,0:T(8,128)S(1)}, u32[]{:S(2)}, u32[]{:S(2)}) collective-permute-start(f32[512,256]{1,0:T(8,128)S(1)} %bitcast.29), channel_id=1, source_target_pairs={{0,15},{1,14},{2,1},{3,0},{4,2},{5,3},{6,4},{7,5},{8,6},{9,7},{10,... | collective-permute-start | bytes 1572872 | tf_op jit(solution)/shard_map/ppermute | solution.py:193
  18.4 0.0 collective-permute-done.1.refs_3_
  18.4 3.7 %collective-permute-done.2.refs_4_ = f32[4,64,256]{2,1,0:T(8,128)S(1)} collective-permute-done((f32[4,64,256]{2,1,0:T(8,128)S(1)}, f32[4,64,256]{2,1,0:T(8,128)S(1)}, u32[]{:S(2)}, u32[]{:S(2)}) %collective-permute-start.2) | collective-permute-done | bytes 262176 | tf_op jit(solution)/shard_map/ppermute | solution.py:171
  22.2 1.9 %collective-permute-start.3 = (f32[2,64,256]{2,1,0:T(8,128)S(1)}, f32[2,64,256]{2,1,0:T(8,128)S(1)}, u32[]{:S(2)}, u32[]{:S(2)}) collective-permute-start(f32[2,64,256]{2,1,0:T(8,128)S(1)} %maximum_select_fusion), channel_id=1, source_target_pairs={{0,16},{16,0},{1,17},{17,1},{2,18},{18,2},{3,19},{19,3},{4,20},{20... | collective-permute-start | bytes 393224 | tf_op jit(solution)/shard_map/ppermute | solution.py:198
  24.1 0.0 collective-permute-start.8
  24.1 3.2 %collective-permute-done.3.refs_6_ = f32[2,64,256]{2,1,0:T(8,128)S(1)} collective-permute-done((f32[2,64,256]{2,1,0:T(8,128)S(1)}, f32[2,64,256]{2,1,0:T(8,128)S(1)}, u32[]{:S(2)}, u32[]{:S(2)}) %collective-permute-start.3) | collective-permute-done | bytes 131104 | tf_op jit(solution)/shard_map/ppermute | solution.py:198
  27.2 3.6 %collective-permute-done.4.refs_9_.refs_5_ = f32[512,256]{1,0:T(8,128)S(1)} collective-permute-done((f32[512,256]{1,0:T(8,128)S(1)}, f32[512,256]{1,0:T(8,128)S(1)}, u32[]{:S(2)}, u32[]{:S(2)}) %collective-permute-start.4) | collective-permute-done | bytes 524320 | tf_op jit(solution)/shard_map/ppermute | solution.py:193
  30.8 2.2 %shard_map.51 = (f32[8,64,256]{2,1,0:T(8,128)S(1)}, f32[16,64,256]{2,1,0:T(8,128)}) custom-call(s32[7]{0:T(128)S(1)} %stack.41.refs_0_, s32[144]{0:T(256)S(1)} %reshape.27.refs_1_, f32[8,64,256]{2,1,0:T(8,128)S(1)} %get-tuple-element.19.refs_2_, f32[4,64,256]{2,1,0:T(8,128)S(1)} %collective-permute-done.1.refs_3_, ...), custom_call_target="tpu_custom_call" | custom-call | flops 1 | bytes 1 | tf_op jit(solution)/shard_map/pallas_call | solution.py:40
  33.0 0.0 collective-permute-start.9
  33.0 2.4 %collective-permute-start.6 = (f32[512,256]{1,0:T(8,128)S(1)}, f32[512,256]{1,0:T(8,128)S(1)}, u32[]{:S(2)}, u32[]{:S(2)}) collective-permute-start(f32[512,256]{1,0:T(8,128)S(1)} %bitcast.35), channel_id=1, source_target_pairs={{0,15},{1,14},{2,1},{3,0},{4,2},{5,3},{6,4},{7,5},{8,6},{9,7},{10,... | collective-permute-start | bytes 1572872 | tf_op jit(solution)/shard_map/ppermute | solution.py:392
  35.4 0.0 collective-permute-start.7
  35.4 0.0 collective-permute-done.11.refs_7_.refs_3_
  35.4 0.0 collective-permute-start.12
  35.4 0.0 collective-permute-done.8.refs_3_
  35.4 3.3 %collective-permute-start.14 = (f32[512,256]{1,0:T(8,128)S(1)}, f32[512,256]{1,0:T(8,128)S(1)}, u32[]{:S(2)}, u32[]{:S(2)}) collective-permute-start(f32[512,256]{1,0:T(8,128)S(1)} %collective-permute-done.11.refs_7_.refs_3_), channel_id=1, source_target_pairs={{0,14},{2,0},{4,2},{6,4},{8,6},{10,8},{12,10},{14,12},{1,15},{3,1}... | collective-permute-start | bytes 1572872 | tf_op jit(solution)/shard_map/ppermute | solution.py:410
  38.7 0.0 collective-permute-done.9.refs_4_
  38.7 0.0 collective-permute-start.5
  38.7 1.4 %shard_map.52.refs_9_ = f32[4,136,128]{2,1,0:T(8,128)S(1)} custom-call(s32[7]{0:T(128)S(1)} %stack.41.refs_0_, f32[512,256]{1,0:T(8,128)S(1)} %bitcast.31, f32[512,256]{1,0:T(8,128)S(1)} %bitcast.37, f32[512,256]{1,0:T(8,128)S(1)} %collective-permute-done.8.refs_3_, f32[512,256]{1,0:T(8,128)S(1)} %collective-permute-done.9.refs_4_), custom_call_target="tpu_custom_call" | custom-call | flops 1 | bytes 1 | tf_op jit(solution)/shard_map/pallas_call | solution.py:40
  40.2 7.5 %collective-permute-done.6.refs_8_.refs_4_ = f32[512,256]{1,0:T(8,128)S(1)} collective-permute-done((f32[512,256]{1,0:T(8,128)S(1)}, f32[512,256]{1,0:T(8,128)S(1)}, u32[]{:S(2)}, u32[]{:S(2)}) %collective-permute-start.6) | collective-permute-done | bytes 524320 | tf_op jit(solution)/shard_map/ppermute | solution.py:392
  47.7 3.7 %collective-permute-done.7.refs_6_.refs_10_ = f32[512,256]{1,0:T(8,128)S(1)} collective-permute-done((f32[512,256]{1,0:T(8,128)S(1)}, f32[512,256]{1,0:T(8,128)S(1)}, u32[]{:S(2)}, u32[]{:S(2)}) %collective-permute-start.7) | collective-permute-done | bytes 524320 | tf_op jit(solution)/shard_map/ppermute | solution.py:393
  51.4 0.0 collective-permute-start.10
  51.4 0.0 collective-permute-start.13
  51.4 0.0 collective-permute-done.12.refs_5_
  51.4 3.2 %collective-permute-start.15 = (f32[512,256]{1,0:T(8,128)S(1)}, f32[512,256]{1,0:T(8,128)}, u32[]{:S(2)}, u32[]{:S(2)}) collective-permute-start(f32[512,256]{1,0:T(8,128)S(1)} %collective-permute-done.6.refs_8_.refs_4_), channel_id=1, source_target_pairs={{0,14},{2,0},{4,2},{6,4},{8,6},{10,8},{12,10},{14,12},{1,15},{3,1}... | collective-permute-start | bytes 1572872 | tf_op jit(solution)/shard_map/ppermute | solution.py:410
  54.7 0.5 slice.35
  55.8 3.0 %shard_map.53 = f32[16,136,128]{2,1,0:T(8,128)} custom-call(s32[7]{0:T(128)S(1)} %stack.41.refs_0_, f32[512,256]{1,0:T(8,128)S(1)} %bitcast.32, f32[512,256]{1,0:T(8,128)S(1)} %bitcast.38, f32[512,256]{1,0:T(8,128)S(1)} %collective-permute-done.8.refs_3_, f32[512,256]{1,0:T(8,128)S(1)} %collective-permute-done.9.refs_4_, ...), custom_call_target="tpu_custom_call" | custom-call | flops 1 | bytes 1 | tf_op jit(solution)/shard_map/pallas_call | solution.py:40
  58.8 27.1 %conditional.1 = (f32[16,136,128]{2,1,0:T(8,128)}) conditional(s32[]{:T(128)} %bitcast.16, f32[16,136,128]{2,1,0:T(8,128)} %shard_map.53, f32[16,136,128]{2,1,0:T(8,128)} %shard_map.53), branch_computations={%region_1.2_spmd, %region_2.3_spmd} | conditional | bytes 6684708 | solution.py:411
  58.8 1.2 copy-done.4
  60.1 25.9 %all_to_all.9 = f32[16,136,128]{2,1,0:T(8,128)} all-to-all(f32[16,136,128]{2,1,0:T(8,128)S(1)} %copy-done.4), channel_id=1, replica_groups=mesh['y'=4,'xh'=2,'xl'=2,'z'=8,'core'=2] {'y','xh','xl'}, dimensions={0} | all-to-all | bytes 2228224 | tf_op jit(solution)/shard_map/cond/branch_1_fun/all_to_all | solution.py:323
  85.9 0.0 collective-permute-done.14.refs_7_
  85.9 0.0 collective-permute-done.5.refs_1_
  86.0 0.0 collective-permute-done.10.refs_2_
  86.0 0.0 collective-permute-done.13.refs_6_
  86.0 0.0 collective-permute-done.15.refs_8_
  86.0 4.5 %shard_map.54 = f32[16,128,128]{2,1,0:T(8,128)} custom-call(s32[7]{0:T(128)S(1)} %stack.41.refs_0_, f32[512,256]{1,0:T(8,128)} %collective-permute-done.5.refs_1_, f32[512,256]{1,0:T(8,128)} %collective-permute-done.10.refs_2_, f32[512,256]{1,0:T(8,128)S(1)} %collective-permute-done.11.refs_7_.refs_3_, ...), custom_call_target="tpu_custom_call" | custom-call | flops 1 | bytes 1 | tf_op jit(solution)/shard_map/pallas_call | solution.py:40
  90.4 5.0 %all-to-all-start.1 = ((f32[16,128,128]{2,1,0:T(8,128)}), f32[16,128,128]{2,1,0:T(8,128)S(1)}, u32[]{:S(2)}, u32[]{:S(2)}) async-start(f32[16,128,128]{2,1,0:T(8,128)} %shard_map.54), calls=%async_computation.1 | async-start | bytes 2097152 | tf_op jit(solution)/shard_map/all_to_all | solution.py:323
  95.5 0.1 shard_map.56.refs_3_
  95.5 0.3 collective-permute-start.17
  95.8 15.5 %all-to-all-done.1.refs_0_ = f32[16,128,128]{2,1,0:T(8,128)S(1)} async-done(((f32[16,128,128]{2,1,0:T(8,128)}), f32[16,128,128]{2,1,0:T(8,128)S(1)}, u32[]{:S(2)}, u32[]{:S(2)}) %all-to-all-start.1) | async-done | bytes 1048608 | tf_op jit(solution)/shard_map/all_to_all | solution.py:323
  111.4 0.1 shard_map.55.refs_1_
  111.4 1.5 %collective-permute-start.16 = (f32[128,128]{1,0:T(8,128)S(1)}, f32[128,128]{1,0:T(8,128)S(1)}, u32[]{:S(2)}, u32[]{:S(2)}) collective-permute-start(f32[128,128]{1,0:T(8,128)S(1)} %shard_map.55.refs_1_), channel_id=1, source_target_pairs={{0,16},{16,0},{1,17},{17,1},{2,18},{18,2},{3,19},{19,3},{4,20},{20... | collective-permute-start | bytes 196616 | tf_op jit(solution)/shard_map/ppermute | solution.py:328
  113.0 0.0 collective-permute-done.17.refs_4_
  113.0 2.8 %collective-permute-done.16.refs_2_ = f32[128,128]{1,0:T(8,128)S(1)} collective-permute-done((f32[128,128]{1,0:T(8,128)S(1)}, f32[128,128]{1,0:T(8,128)S(1)}, u32[]{:S(2)}, u32[]{:S(2)}) %collective-permute-start.16) | collective-permute-done | bytes 65568 | tf_op jit(solution)/shard_map/ppermute | solution.py:328
  115.8 0.7 shard_map.57
  116.5 1.9 %collective-permute-start.18 = (f32[128,256]{1,0:T(8,128)S(1)}, f32[128,256]{1,0:T(8,128)S(1)}, u32[]{:S(2)}, u32[]{:S(2)}) collective-permute-start(f32[128,256]{1,0:T(8,128)S(1)} %get-tuple-element.29), channel_id=1, source_target_pairs={{0,44},{1,2},{2,78},{3,37},{4,96},{5,71},{6,130},{7,105},{8,164},{... | collective-permute-start | bytes 393224 | tf_op jit(solution)/shard_map/ppermute | solution.py:429
  118.4 3.8 %collective-permute-start.19 = (f32[128,256]{1,0:T(8,128)S(1)}, f32[128,256]{1,0:T(8,128)S(1)}, u32[]{:S(2)}, u32[]{:S(2)}) collective-permute-start(f32[128,256]{1,0:T(8,128)S(1)} %get-tuple-element.30), channel_id=1, source_target_pairs={{0,3},{1,45},{2,36},{3,79},{4,70},{5,97},{6,104},{7,131},{8,138},{... | collective-permute-start | bytes 393224 | tf_op jit(solution)/shard_map/ppermute | solution.py:429
  122.2 6.1 %collective-permute-done.18.refs_1_ = f32[128,256]{1,0:T(8,128)S(1)} collective-permute-done((f32[128,256]{1,0:T(8,128)S(1)}, f32[128,256]{1,0:T(8,128)S(1)}, u32[]{:S(2)}, u32[]{:S(2)}) %collective-permute-start.18) | collective-permute-done | bytes 131104 | tf_op jit(solution)/shard_map/ppermute | solution.py:429
  128.3 0.1 collective-permute-done.19.refs_2_
  128.4 1.4 %shard_map.58 = f32[256,256]{1,0:T(8,128)} custom-call(s32[7]{0:T(128)S(1)} %stack.41.refs_0_, f32[128,256]{1,0:T(8,128)S(1)} %collective-permute-done.18.refs_1_, f32[128,256]{1,0:T(8,128)S(1)} %collective-permute-done.19.refs_2_), custom_call_target="tpu_custom_call" | custom-call | flops 1 | bytes 1 | tf_op jit(solution)/shard_map/pallas_call | solution.py:40
  (10 shorter events, 0.1 us)
Async XLA Ops:
  0.6 8.8 %copy-start.5 = (s32[4,4,9]{2,1,0:T(4,128)S(1)}, s32[4,4,9]{2,1,0:T(4,128)}, u32[]{:S(2)}) copy-start(s32[4,4,9]{2,1,0:T(4,128)} %param.6) | copy-start | bytes 1732
  0.6 9.4 %copy-start.2 = (f32[4,4,64,256]{3,2,1,0:T(8,128)S(1)}, f32[4,4,64,256]{3,2,1,0:T(8,128)}, u32[]{:S(2)}) copy-start(f32[4,4,64,256]{3,2,1,0:T(8,128)} %param.5) | copy-start | bytes 3145732
  1.8 8.3 %collective-permute-start = (f32[4,64,256]{2,1,0:T(8,128)S(1)}, f32[4,64,256]{2,1,0:T(8,128)S(1)}, u32[]{:S(2)}, u32[]{:S(2)}) collective-permute-start(f32[4,64,256]{2,1,0:T(8,128)S(1)} %fusion), channel_id=1, source_target_pairs={{0,16},{16,0},{1,17},{17,1},{2,18},{18,2},{3,19},{19,3},{4,20},{20... | collective-permute-start | bytes 786440 | tf_op jit(solution)/shard_map/ppermute | solution.py:169
  5.3 13.2 %collective-permute-start.1 = (f32[4,64,256]{2,1,0:T(8,128)S(1)}, f32[4,64,256]{2,1,0:T(8,128)S(1)}, u32[]{:S(2)}, u32[]{:S(2)}) collective-permute-start(f32[4,64,256]{2,1,0:T(8,128)S(1)} %get-tuple-element.32), channel_id=1, source_target_pairs={{0,32},{32,64},{64,96},{96,128},{128,160},{160,192},{192,224},{1,3... | collective-permute-start | bytes 786440 | tf_op jit(solution)/shard_map/ppermute | solution.py:170
  7.9 14.2 %collective-permute-start.2 = (f32[4,64,256]{2,1,0:T(8,128)S(1)}, f32[4,64,256]{2,1,0:T(8,128)S(1)}, u32[]{:S(2)}, u32[]{:S(2)}) collective-permute-start(f32[4,64,256]{2,1,0:T(8,128)S(1)} %get-tuple-element.31), channel_id=1, source_target_pairs={{32,0},{64,32},{96,64},{128,96},{160,128},{192,160},{224,192},{33,... | collective-permute-start | bytes 786440 | tf_op jit(solution)/shard_map/ppermute | solution.py:171
  10.1 1.7 %copy-start = (f32[4,4,9,4096]{3,1,2,0:T(4,128)S(1)}, f32[4,4,9,4096]{3,1,2,0:T(4,128)}, u32[]{:S(2)}) copy-start(f32[4,4,9,4096]{3,1,2,0:T(4,128)} %param.7) | copy-start | bytes 7077892
  11.7 19.1 %copy-start.1 = (f32[4,4,9,4096]{3,1,2,0:T(4,128)S(1)}, f32[4,4,9,4096]{3,1,2,0:T(4,128)}, u32[]{:S(2)}) copy-start(f32[4,4,9,4096]{3,1,2,0:T(4,128)} %param.7) | copy-start | bytes 7077892
  13.8 17.0 %collective-permute-start.4 = (f32[512,256]{1,0:T(8,128)S(1)}, f32[512,256]{1,0:T(8,128)S(1)}, u32[]{:S(2)}, u32[]{:S(2)}) collective-permute-start(f32[512,256]{1,0:T(8,128)S(1)} %bitcast.28), channel_id=1, source_target_pairs={{0,2},{2,4},{4,6},{6,8},{8,10},{10,12},{12,14},{14,0},{1,3},{3,5},... | collective-permute-start | bytes 1572872 | tf_op jit(solution)/shard_map/ppermute | solution.py:193
  15.8 19.6 %collective-permute-start.11 = (f32[512,256]{1,0:T(8,128)S(1)}, f32[512,256]{1,0:T(8,128)S(1)}, u32[]{:S(2)}, u32[]{:S(2)}) collective-permute-start(f32[512,256]{1,0:T(8,128)S(1)} %bitcast.29), channel_id=1, source_target_pairs={{0,15},{1,14},{2,1},{3,0},{4,2},{5,3},{6,4},{7,5},{8,6},{9,7},{10,... | collective-permute-start | bytes 1572872 | tf_op jit(solution)/shard_map/ppermute | solution.py:193
  22.2 5.1 %collective-permute-start.3 = (f32[2,64,256]{2,1,0:T(8,128)S(1)}, f32[2,64,256]{2,1,0:T(8,128)S(1)}, u32[]{:S(2)}, u32[]{:S(2)}) collective-permute-start(f32[2,64,256]{2,1,0:T(8,128)S(1)} %maximum_select_fusion), channel_id=1, source_target_pairs={{0,16},{16,0},{1,17},{17,1},{2,18},{18,2},{3,19},{19,3},{4,20},{20... | collective-permute-start | bytes 393224 | tf_op jit(solution)/shard_map/ppermute | solution.py:198
  24.1 11.4 %collective-permute-start.8 = (f32[512,256]{1,0:T(8,128)S(1)}, f32[512,256]{1,0:T(8,128)S(1)}, u32[]{:S(2)}, u32[]{:S(2)}) collective-permute-start(f32[512,256]{1,0:T(8,128)S(1)} %bitcast.30), channel_id=1, source_target_pairs={{0,1},{1,0},{2,3},{3,2},{4,5},{5,4},{6,7},{7,6},{8,9},{9,8},{10,11... | collective-permute-start | bytes 1572872 | tf_op jit(solution)/shard_map/ppermute | solution.py:394
  33.0 5.7 %collective-permute-start.9 = (f32[512,256]{1,0:T(8,128)S(1)}, f32[512,256]{1,0:T(8,128)S(1)}, u32[]{:S(2)}, u32[]{:S(2)}) collective-permute-start(f32[512,256]{1,0:T(8,128)S(1)} %bitcast.34), channel_id=1, source_target_pairs={{0,1},{1,0},{2,3},{3,2},{4,5},{5,4},{6,7},{7,6},{8,9},{9,8},{10,11... | collective-permute-start | bytes 1572872 | tf_op jit(solution)/shard_map/ppermute | solution.py:394
  33.0 14.6 %collective-permute-start.6 = (f32[512,256]{1,0:T(8,128)S(1)}, f32[512,256]{1,0:T(8,128)S(1)}, u32[]{:S(2)}, u32[]{:S(2)}) collective-permute-start(f32[512,256]{1,0:T(8,128)S(1)} %bitcast.35), channel_id=1, source_target_pairs={{0,15},{1,14},{2,1},{3,0},{4,2},{5,3},{6,4},{7,5},{8,6},{9,7},{10,... | collective-permute-start | bytes 1572872 | tf_op jit(solution)/shard_map/ppermute | solution.py:392
  35.4 16.0 %collective-permute-start.7 = (f32[512,256]{1,0:T(8,128)S(1)}, f32[512,256]{1,0:T(8,128)S(1)}, u32[]{:S(2)}, u32[]{:S(2)}) collective-permute-start(f32[512,256]{1,0:T(8,128)S(1)} %bitcast.36), channel_id=1, source_target_pairs={{0,2},{2,4},{4,6},{6,8},{8,10},{10,12},{12,14},{14,0},{1,3},{3,5},... | collective-permute-start | bytes 1572872 | tf_op jit(solution)/shard_map/ppermute | solution.py:393
  35.4 16.0 %collective-permute-start.12 = (f32[512,256]{1,0:T(8,128)S(1)}, f32[512,256]{1,0:T(8,128)S(1)}, u32[]{:S(2)}, u32[]{:S(2)}) collective-permute-start(f32[512,256]{1,0:T(8,128)S(1)} %collective-permute-done.11.refs_7_.refs_3_), channel_id=1, source_target_pairs={{0,1},{1,0},{2,3},{3,2},{4,5},{5,4},{6,7},{7,6},{8,9},{9,8},{10,11... | collective-permute-start | bytes 1572872 | tf_op jit(solution)/shard_map/ppermute | solution.py:398
  35.4 50.5 %collective-permute-start.14 = (f32[512,256]{1,0:T(8,128)S(1)}, f32[512,256]{1,0:T(8,128)S(1)}, u32[]{:S(2)}, u32[]{:S(2)}) collective-permute-start(f32[512,256]{1,0:T(8,128)S(1)} %collective-permute-done.11.refs_7_.refs_3_), channel_id=1, source_target_pairs={{0,14},{2,0},{4,2},{6,4},{8,6},{10,8},{12,10},{14,12},{1,15},{3,1}... | collective-permute-start | bytes 1572872 | tf_op jit(solution)/shard_map/ppermute | solution.py:410
  38.7 47.2 %collective-permute-start.5 = (f32[512,256]{1,0:T(8,128)S(1)}, f32[512,256]{1,0:T(8,128)}, u32[]{:S(2)}, u32[]{:S(2)}) collective-permute-start(f32[512,256]{1,0:T(8,128)S(1)} %collective-permute-done.4.refs_9_.refs_5_), channel_id=1, source_target_pairs={{0,2},{2,4},{4,6},{6,8},{8,10},{10,12},{12,14},{14,0},{1,3},{3,5},... | collective-permute-start | bytes 1572872 | tf_op jit(solution)/shard_map/ppermute | solution.py:397
  51.4 34.5 %collective-permute-start.10 = (f32[512,256]{1,0:T(8,128)S(1)}, f32[512,256]{1,0:T(8,128)}, u32[]{:S(2)}, u32[]{:S(2)}) collective-permute-start(f32[512,256]{1,0:T(8,128)S(1)} %collective-permute-done.7.refs_6_.refs_10_), channel_id=1, source_target_pairs={{0,2},{2,4},{4,6},{6,8},{8,10},{10,12},{12,14},{14,0},{1,3},{3,5},... | collective-permute-start | bytes 1572872 | tf_op jit(solution)/shard_map/ppermute | solution.py:397
  51.4 34.5 %collective-permute-start.13 = (f32[512,256]{1,0:T(8,128)S(1)}, f32[512,256]{1,0:T(8,128)}, u32[]{:S(2)}, u32[]{:S(2)}) collective-permute-start(f32[512,256]{1,0:T(8,128)S(1)} %collective-permute-done.6.refs_8_.refs_4_), channel_id=1, source_target_pairs={{0,1},{1,0},{2,3},{3,2},{4,5},{5,4},{6,7},{7,6},{8,9},{9,8},{10,11... | collective-permute-start | bytes 1572872 | tf_op jit(solution)/shard_map/ppermute | solution.py:398
  51.4 34.5 %collective-permute-start.15 = (f32[512,256]{1,0:T(8,128)S(1)}, f32[512,256]{1,0:T(8,128)}, u32[]{:S(2)}, u32[]{:S(2)}) collective-permute-start(f32[512,256]{1,0:T(8,128)S(1)} %collective-permute-done.6.refs_8_.refs_4_), channel_id=1, source_target_pairs={{0,14},{2,0},{4,2},{6,4},{8,6},{10,8},{12,10},{14,12},{1,15},{3,1}... | collective-permute-start | bytes 1572872 | tf_op jit(solution)/shard_map/ppermute | solution.py:410
  58.8 1.2 copy-start.4
  90.4 5.0 %copy-start.3 = (f32[16,136,128]{2,1,0:T(8,128)S(1)}, f32[16,136,128]{2,1,0:T(8,128)}, u32[]{:S(2)}) copy-start(f32[16,136,128]{2,1,0:T(8,128)} %get-tuple-element.39.refs_11_.refs_0_) | copy-start | bytes 3342340
  90.4 20.9 %all-to-all-start.1 = ((f32[16,128,128]{2,1,0:T(8,128)}), f32[16,128,128]{2,1,0:T(8,128)S(1)}, u32[]{:S(2)}, u32[]{:S(2)}) async-start(f32[16,128,128]{2,1,0:T(8,128)} %shard_map.54), calls=%async_computation.1 | async-start | bytes 2097152 | tf_op jit(solution)/shard_map/all_to_all | solution.py:323
  95.5 17.4 %collective-permute-start.17 = (f32[136,128]{1,0:T(8,128)S(1)}, f32[136,128]{1,0:T(8,128)S(1)}, u32[]{:S(2)}, u32[]{:S(2)}) collective-permute-start(f32[136,128]{1,0:T(8,128)S(1)} %shard_map.56.refs_3_), channel_id=1, source_target_pairs={{0,16},{16,0},{1,17},{17,1},{2,18},{18,2},{3,19},{19,3},{4,20},{20... | collective-permute-start | bytes 208904 | tf_op jit(solution)/shard_map/ppermute | solution.py:328
  111.4 4.4 %collective-permute-start.16 = (f32[128,128]{1,0:T(8,128)S(1)}, f32[128,128]{1,0:T(8,128)S(1)}, u32[]{:S(2)}, u32[]{:S(2)}) collective-permute-start(f32[128,128]{1,0:T(8,128)S(1)} %shard_map.55.refs_1_), channel_id=1, source_target_pairs={{0,16},{16,0},{1,17},{17,1},{2,18},{18,2},{3,19},{19,3},{4,20},{20... | collective-permute-start | bytes 196616 | tf_op jit(solution)/shard_map/ppermute | solution.py:328
  116.5 11.8 %collective-permute-start.18 = (f32[128,256]{1,0:T(8,128)S(1)}, f32[128,256]{1,0:T(8,128)S(1)}, u32[]{:S(2)}, u32[]{:S(2)}) collective-permute-start(f32[128,256]{1,0:T(8,128)S(1)} %get-tuple-element.29), channel_id=1, source_target_pairs={{0,44},{1,2},{2,78},{3,37},{4,96},{5,71},{6,130},{7,105},{8,164},{... | collective-permute-start | bytes 393224 | tf_op jit(solution)/shard_map/ppermute | solution.py:429
  118.4 9.9 %collective-permute-start.19 = (f32[128,256]{1,0:T(8,128)S(1)}, f32[128,256]{1,0:T(8,128)S(1)}, u32[]{:S(2)}, u32[]{:S(2)}) collective-permute-start(f32[128,256]{1,0:T(8,128)S(1)} %get-tuple-element.30), channel_id=1, source_target_pairs={{0,3},{1,45},{2,36},{3,79},{4,70},{5,97},{6,104},{7,131},{8,138},{... | collective-permute-start | bytes 393224 | tf_op jit(solution)/shard_map/ppermute | solution.py:429

commit v4 on v3

--- a/solution.py
+++ b/solution.py
@@ -23,7 +23,7 @@
 ]
 VMEM = pl.BlockSpec(memory_space=pltpu.VMEM)
 SMEM = pl.BlockSpec(memory_space=pltpu.SMEM)
-CORE, SIDE, ROW, COLUMN, TURN, MIRROR, OWN = range(7)
+CORE, SIDE, ROW, COLUMN, OWN = range(5)
 
 
 def split(value):
@@ -208,8 +208,8 @@
         corners,
         mass,
         mid,
-        after=early[:1],
-    )
+    )
+    outer, *early = lax.optimization_barrier((outer, *early))
     return flat, outer.reshape(8 * BLK, cols), weighted, early
 
 
@@ -303,29 +303,23 @@
     far_left = jnp.where(beside == 0, far[...], far_beside[...])
     far_right = jnp.where(beside == 0, far_beside[...], far[...])
     late = (y + beside + core) % 2
+    turned = (beside == 1) & jnp.logical_not(diagonal)
+    lefts, rights = jnp.where(turned, lefts.T, lefts), jnp.where(turned, rights.T, rights)
+    turned = beside == 1
+    far_left = jnp.where(turned, far_left.T, far_left)
+    far_right = jnp.where(turned, far_right.T, far_right)
     for turn in range(2):
         outs[turn][:, :128] = jnp.where(late == turn, far_left, lefts)
         outs[turn][:, 128:] = jnp.where(late == turn, far_right, rights)
 
 
-def place_kernel(spot, first, second, out):
-    block = jnp.concatenate([first[...], second[...]], 0)
-    swapped = jnp.concatenate([second[...], first[...]], 0)
-    block = jnp.where(spot[TURN] == 0, block, swapped) * (1.0 / 16384)
-    out[...] = jnp.where(spot[MIRROR] == 0, block, block.T)
-
-
 def array(*shape):
     return jax.ShapeDtypeStruct(shape, jnp.float32)
 
 
-def exchange(blocks):
-    return lax.all_to_all(blocks, PLANE, 0, 0, tiled=True)
-
-
 def gathered(blocks):
-    total = call(add_kernel, array(*blocks.shape[1:]), [], [], blocks)
-    return total, lax.ppermute(total, "xl", SWAP)
+    blocks = lax.all_to_all(blocks, PLANE, 0, 0, tiled=True)
+    return call(add_kernel, array(*blocks.shape[1:]), [], [], blocks)
 
 
 def crossed(z, core):
@@ -386,16 +380,17 @@
         1 - core ^ turned(z + 7),
     )
     turn = sum(jnp.where(apart == k, value, 0) for k, value in enumerate(turns))
-    spot = [core, lax.axis_index("xl"), y, x, turn, mirror, core ^ turned(z)]
+    spot = [core, lax.axis_index("xl"), y, x, core ^ turned(z)]
     spot = jnp.stack([jnp.asarray(value).astype(jnp.int32) for value in spot])
     *held, weighted, early = weigh(spot, snapshots, links, mass)
     next_1 = [early[1], lax.ppermute(held[1], ("z", "core"), DOWN_TURNED)]
     last_1 = [early[0], lax.ppermute(held[1], "z", UP)]
     held_other = [lax.ppermute(half, "core", SWAP) for half in held]
     square = call(square_kernel, array(4, 136, 128), [], [spot], *held, *held_other)
-    next_1[1], last_1[1], square = lax.optimization_barrier((next_1[1], last_1[1], square))
-    last_2 = [lax.ppermute(half, "z", UP) for half in last_1]
-    next_other = [lax.ppermute(half, "core", SWAP) for half in next_1]
+    sure = links[0, 0, 0] >= 0
+    next_1[1], last_1[1], square, sure = lax.optimization_barrier(
+        (next_1[1], last_1[1], square, sure)
+    )
     near = call(
         near_kernel,
         array(16, 136, 128),
@@ -407,8 +402,11 @@
         *next_1,
         square,
     )
+    next_1[1], last_1[1], near = lax.optimization_barrier((next_1[1], last_1[1], near))
+    last_2 = [lax.ppermute(half, "z", UP) for half in last_1]
     next_2 = [lax.ppermute(half, "z", DOWN) for half in next_1]
-    near = lax.cond(links[0, 0, 0] >= 0, exchange, lambda blocks: blocks, near)
+    next_other = [lax.ppermute(half, "core", SWAP) for half in next_1]
+    near = lax.cond(sure, gathered, lambda blocks: blocks[0], near)
     far = call(
         far_kernel,
         array(16, 128, 128),
@@ -421,13 +419,18 @@
         *last_1,
         after=(near,),
     )
-    near, near_beside = gathered(near)
-    far, far_beside = gathered(exchange(far))
+    near_beside = lax.ppermute(near, "xl", SWAP)
+    far = gathered(far)
+    far_beside = lax.ppermute(far, "xl", SWAP)
     sent = call(
         send_kernel, [array(128, 256)] * 2, [], [spot], far, far_beside, near, near_beside
     )
     got = [lax.ppermute(sent[k], ALL, routes(k)) for k in range(2)]
-    gram = call(place_kernel, array(256, 256), [], [spot], *got)
+    first = [jnp.where(turn == 0, got[0][:, k : k + 128], got[1][:, k : k + 128]) for k in (0, 128)]
+    second = [jnp.where(turn == 0, got[1][:, k : k + 128], got[0][:, k : k + 128]) for k in (0, 128)]
+    upper = jnp.concatenate([first[0], jnp.where(mirror, second[0], first[1])], 1)
+    lower = jnp.concatenate([jnp.where(mirror, first[1], second[0]), second[1]], 1)
+    gram = jnp.concatenate([upper, lower], 0) * jnp.float32(1.0 / 16384)
     return weighted.reshape(snapshots.shape), gram
 
 

time: 132 us -> 129 us (0.977)
  waiting for transfers between devices: 46.5 us -> 43.6 us
  starting transfers between devices: 34.3 us -> 36.4 us
    ppermute x1, waiting for transfers between devices: 3.59 us -> 1.22 us  [weigh(): lax.ppermute(flat, 'z', UP)]
    ppermute x1, starting transfers between devices: 2.37 us -> 4.73 us  [body(): next_1 = [early[1], lax.ppermute(held[1], ('z', 'core'), DOWN_TURNED)]]
    pallas_call x9 -> x8, Pallas kernels: 15.3 us -> 14.1 us  [call(): pl.pallas_call(ordered, out_shape=shape, in_specs=[SMEM] * len(scalars) +...]
where the time goes in v4:
time: 129 us; the launch traced here: 127 us
  waiting for transfers between devices  43.6 us (34%)
  starting transfers between devices  36.4 us (28%)
  blocking collectives  25.4 us (20%)
  Pallas kernels  14.1 us (11%)
  local copies, waits for them, and re-layouts  3.56 us (3%)
  other arithmetic  2 us (2%)
  between operations  1.48 us (1%)
    all_to_all x1, blocking collectives, gathered(): blocks = lax.all_to_all(blocks, PLANE, 0, 0, tiled=True)  25.4 us
    all_to_all x1, waiting for transfers between devices, gathered(): blocks = lax.all_to_all(blocks, PLANE, 0, 0, tiled=True)  15.6 us
    pallas_call x8, Pallas kernels, call(): pl.pallas_call(ordered, out_shape=shape, in_specs=[SMEM] * len(scalars) +...  14.1 us
    ppermute x2, starting transfers between devices, body(): next_2 = [lax.ppermute(half, 'z', DOWN) for half in next_1]  6.48 us
    ppermute x2, waiting for transfers between devices, body(): got = [lax.ppermute(sent[k], ALL, routes(k)) for k in range(2)]  6.36 us
    ppermute x1, waiting for transfers between devices, body(): next_1 = [early[1], lax.ppermute(held[1], ('z', 'core'), DOWN_TURNED)]  6.35 us
    ppermute x2, starting transfers between devices, body(): got = [lax.ppermute(sent[k], ALL, routes(k)) for k in range(2)]  5.73 us
    all_to_all x1, starting transfers between devices, gathered(): blocks = lax.all_to_all(blocks, PLANE, 0, 0, tiled=True)  4.89 us
  transfers between devices with their start and end apart: 21, of which 10 were waited for; matrix products, arithmetic and copies ran while one was open for 2% of the time, Pallas kernels for 7%

profile of v4, /device:TPU:2, one launch (start us, length us, event | category | flops | bytes accessed | tf_op | source)
XLA Modules:
  0.0 126.5 jit_solution(11983268850499612157)
XLA Ops:
  0.6 0.0 copy-start.2
  0.6 0.0 copy-start.3
  0.7 1.2 fusion
  1.8 2.4 %collective-permute-start = (f32[4,64,256]{2,1,0:T(8,128)S(1)}, f32[4,64,256]{2,1,0:T(8,128)S(1)}, u32[]{:S(2)}, u32[]{:S(2)}) collective-permute-start(f32[4,64,256]{2,1,0:T(8,128)S(1)} %fusion), channel_id=1, source_target_pairs={{0,16},{16,0},{1,17},{17,1},{2,18},{18,2},{3,19},{19,3},{4,20},{20... | collective-permute-start | bytes 786440 | tf_op jit(solution)/shard_map/ppermute | solution.py:169
  4.2 1.1 slice_bitcast_fusion.1
  5.3 2.6 %collective-permute-start.1 = (f32[4,64,256]{2,1,0:T(8,128)S(1)}, f32[4,64,256]{2,1,0:T(8,128)S(1)}, u32[]{:S(2)}, u32[]{:S(2)}) collective-permute-start(f32[4,64,256]{2,1,0:T(8,128)S(1)} %get-tuple-element.46), channel_id=1, source_target_pairs={{0,32},{32,64},{64,96},{96,128},{128,160},{160,192},{192,224},{1,3... | collective-permute-start | bytes 786440 | tf_op jit(solution)/shard_map/ppermute | solution.py:170
  7.9 1.3 %collective-permute-start.2 = (f32[4,64,256]{2,1,0:T(8,128)S(1)}, f32[4,64,256]{2,1,0:T(8,128)S(1)}, u32[]{:S(2)}, u32[]{:S(2)}) collective-permute-start(f32[4,64,256]{2,1,0:T(8,128)S(1)} %get-tuple-element.45), channel_id=1, source_target_pairs={{32,0},{64,32},{96,64},{128,96},{160,128},{192,160},{224,192},{33,... | collective-permute-start | bytes 786440 | tf_op jit(solution)/shard_map/ppermute | solution.py:171
  9.2 0.0 copy-done.3
  9.2 0.1 copy.7
  9.3 0.1 select_reduce_fusion
  9.4 0.1 reshape.25.refs_1_
  9.5 0.1 stack.29.refs_0_
  9.6 0.5 collective-permute-done.refs_3_.refs_5_
  10.1 1.7 %copy-done = f32[4,4,9,4096]{3,1,2,0:T(4,128)S(1)} copy-done((f32[4,4,9,4096]{3,1,2,0:T(4,128)S(1)}, f32[4,4,9,4096]{3,1,2,0:T(4,128)}, u32[]{:S(2)}) %copy-start) | copy-done | bytes 2359320
  11.7 2.0 %shard_map.50 = (f32[8,64,256]{2,1,0:T(8,128)S(1)}, f32[8,64,256]{2,1,0:T(8,128)S(1)}) custom-call(s32[5]{0:T(128)S(1)} %stack.29.refs_0_, s32[144]{0:T(256)S(1)} %reshape.25.refs_1_, f32[16,64,256]{2,1,0:T(8,128)S(1)} %bitcast.33, f32[4,64,256]{2,1,0:T(8,128)S(1)} %collective-permute-done.refs_3_.refs_5_, f32[4,9,4,4096]{3,2,1,0:T(4,128)S(1)} %bitcast.26), custom_call_target="tpu_custom_call" | custom-call | flops 1 | bytes 1 | tf_op jit(solution)/shard_map/pallas_call | solution.py:40
  13.8 2.0 %collective-permute-start.4 = (f32[512,256]{1,0:T(8,128)S(1)}, f32[512,256]{1,0:T(8,128)S(1)}, u32[]{:S(2)}, u32[]{:S(2)}) collective-permute-start(f32[512,256]{1,0:T(8,128)S(1)} %bitcast.28), channel_id=1, source_target_pairs={{0,2},{2,4},{4,6},{6,8},{8,10},{10,12},{12,14},{14,0},{1,3},{3,5},... | collective-permute-start | bytes 1572872 | tf_op jit(solution)/shard_map/ppermute | solution.py:193
  15.8 2.5 %collective-permute-start.5 = (f32[512,256]{1,0:T(8,128)S(1)}, f32[512,256]{1,0:T(8,128)S(1)}, u32[]{:S(2)}, u32[]{:S(2)}) collective-permute-start(f32[512,256]{1,0:T(8,128)S(1)} %bitcast.29), channel_id=1, source_target_pairs={{0,15},{1,14},{2,1},{3,0},{4,2},{5,3},{6,4},{7,5},{8,6},{9,7},{10,... | collective-permute-start | bytes 1572872 | tf_op jit(solution)/shard_map/ppermute | solution.py:193
  18.3 0.0 collective-permute-done.1.refs_3_
  18.3 3.9 %collective-permute-done.2.refs_4_ = f32[4,64,256]{2,1,0:T(8,128)S(1)} collective-permute-done((f32[4,64,256]{2,1,0:T(8,128)S(1)}, f32[4,64,256]{2,1,0:T(8,128)S(1)}, u32[]{:S(2)}, u32[]{:S(2)}) %collective-permute-start.2) | collective-permute-done | bytes 262176 | tf_op jit(solution)/shard_map/ppermute | solution.py:171
  22.2 1.9 %collective-permute-start.3 = (f32[2,64,256]{2,1,0:T(8,128)S(1)}, f32[2,64,256]{2,1,0:T(8,128)S(1)}, u32[]{:S(2)}, u32[]{:S(2)}) collective-permute-start(f32[2,64,256]{2,1,0:T(8,128)S(1)} %maximum_select_fusion), channel_id=1, source_target_pairs={{0,16},{16,0},{1,17},{17,1},{2,18},{18,2},{3,19},{19,3},{4,20},{20... | collective-permute-start | bytes 393224 | tf_op jit(solution)/shard_map/ppermute | solution.py:198
  24.1 0.0 collective-permute-start.9
  24.1 3.2 %collective-permute-done.3.refs_6_ = f32[2,64,256]{2,1,0:T(8,128)S(1)} collective-permute-done((f32[2,64,256]{2,1,0:T(8,128)S(1)}, f32[2,64,256]{2,1,0:T(8,128)S(1)}, u32[]{:S(2)}, u32[]{:S(2)}) %collective-permute-start.3) | collective-permute-done | bytes 131104 | tf_op jit(solution)/shard_map/ppermute | solution.py:198
  27.2 2.2 %shard_map.51 = (f32[8,64,256]{2,1,0:T(8,128)S(1)}, f32[16,64,256]{2,1,0:T(8,128)}) custom-call(s32[5]{0:T(128)S(1)} %stack.29.refs_0_, s32[144]{0:T(256)S(1)} %reshape.25.refs_1_, f32[8,64,256]{2,1,0:T(8,128)S(1)} %get-tuple-element.26.refs_2_, f32[4,64,256]{2,1,0:T(8,128)S(1)} %collective-permute-done.1.refs_3_, ...), custom_call_target="tpu_custom_call" | custom-call | flops 1 | bytes 1 | tf_op jit(solution)/shard_map/pallas_call | solution.py:40
  29.4 1.2 collective-permute-done.4.refs_5_.refs_9_
  30.6 0.0 collective-permute-done.5.refs_7_.refs_3_
  30.7 0.0 collective-permute-start.10
  30.7 4.7 %collective-permute-start.7 = (f32[512,256]{1,0:T(8,128)S(1)}, f32[512,256]{1,0:T(8,128)S(1)}, u32[]{:S(2)}, u32[]{:S(2)}) collective-permute-start(f32[512,256]{1,0:T(8,128)S(1)} %bitcast.35), channel_id=1, source_target_pairs={{0,15},{1,14},{2,1},{3,0},{4,2},{5,3},{6,4},{7,5},{8,6},{9,7},{10,... | collective-permute-start | bytes 1572872 | tf_op jit(solution)/shard_map/ppermute | solution.py:386
  35.4 0.0 collective-permute-start.8
  35.4 0.1 collective-permute-start.12
  35.5 0.5 slice.54
  36.7 0.0 collective-permute-done.9.refs_3_
  36.7 3.2 %collective-permute-start.14 = (f32[512,256]{1,0:T(8,128)S(1)}, f32[512,256]{1,0:T(8,128)S(1)}, u32[]{:S(2)}, u32[]{:S(2)}) collective-permute-start(f32[512,256]{1,0:T(8,128)S(1)} %collective-permute-done.5.refs_7_.refs_3_), channel_id=1, source_target_pairs={{0,14},{2,0},{4,2},{6,4},{8,6},{10,8},{12,10},{14,12},{1,15},{3,1}... | collective-permute-start | bytes 1572872 | tf_op jit(solution)/shard_map/ppermute | solution.py:407
  39.9 0.0 collective-permute-done.10.refs_4_
  39.9 0.0 collective-permute-start.6
  39.9 1.4 %shard_map.52.refs_9_ = f32[4,136,128]{2,1,0:T(8,128)S(1)} custom-call(s32[5]{0:T(128)S(1)} %stack.29.refs_0_, f32[512,256]{1,0:T(8,128)S(1)} %bitcast.31, f32[512,256]{1,0:T(8,128)S(1)} %bitcast.37, f32[512,256]{1,0:T(8,128)S(1)} %collective-permute-done.9.refs_3_, f32[512,256]{1,0:T(8,128)S(1)} %collective-permute-done.10.refs_4_), custom_call_target="tpu_custom_call" | custom-call | flops 1 | bytes 1 | tf_op jit(solution)/shard_map/pallas_call | solution.py:40
  41.3 6.3 %collective-permute-done.7.refs_8_.refs_4_ = f32[512,256]{1,0:T(8,128)S(1)} collective-permute-done((f32[512,256]{1,0:T(8,128)S(1)}, f32[512,256]{1,0:T(8,128)S(1)}, u32[]{:S(2)}, u32[]{:S(2)}) %collective-permute-start.7) | collective-permute-done | bytes 524320 | tf_op jit(solution)/shard_map/ppermute | solution.py:386
  47.7 3.7 %collective-permute-done.8.refs_6_.refs_10_ = f32[512,256]{1,0:T(8,128)S(1)} collective-permute-done((f32[512,256]{1,0:T(8,128)S(1)}, f32[512,256]{1,0:T(8,128)S(1)}, u32[]{:S(2)}, u32[]{:S(2)}) %collective-permute-start.8) | collective-permute-done | bytes 524320 | tf_op jit(solution)/shard_map/ppermute | solution.py:387
  51.4 3.1 %shard_map.53 = f32[16,136,128]{2,1,0:T(8,128)} custom-call(s32[5]{0:T(128)S(1)} %stack.29.refs_0_, f32[512,256]{1,0:T(8,128)S(1)} %bitcast.32, f32[512,256]{1,0:T(8,128)S(1)} %bitcast.38, f32[512,256]{1,0:T(8,128)S(1)} %collective-permute-done.9.refs_3_, f32[512,256]{1,0:T(8,128)S(1)} %collective-permute-done.10.refs_4_, ...), custom_call_target="tpu_custom_call" | custom-call | flops 1 | bytes 1 | tf_op jit(solution)/shard_map/pallas_call | solution.py:40
  54.5 0.0 collective-permute-start.11
  54.5 0.0 collective-permute-start.13
  54.5 0.0 collective-permute-done.12.refs_5_
  54.5 3.2 %collective-permute-start.15 = (f32[512,256]{1,0:T(8,128)S(1)}, f32[512,256]{1,0:T(8,128)}, u32[]{:S(2)}, u32[]{:S(2)}) collective-permute-start(f32[512,256]{1,0:T(8,128)S(1)} %collective-permute-done.7.refs_8_.refs_4_), channel_id=1, source_target_pairs={{0,14},{2,0},{4,2},{6,4},{8,6},{10,8},{12,10},{14,12},{1,15},{3,1}... | collective-permute-start | bytes 1572872 | tf_op jit(solution)/shard_map/ppermute | solution.py:407
  57.7 25.4 %conditional.1 = (f32[136,128]{1,0:T(8,128)S(1)}) conditional(s32[]{:T(128)} %convert_element_type.3, f32[16,136,128]{2,1,0:T(8,128)} %shard_map.53, f32[16,136,128]{2,1,0:T(8,128)} %shard_map.53), branch_computations={%region_1.2_spmd, %region_2.3_spmd} | conditional | flops 1 | bytes 2228233 | solution.py:409
  57.7 25.4 %all_to_all.9.refs_0_ = f32[16,136,128]{2,1,0:T(8,128)S(1)} all-to-all(f32[16,136,128]{2,1,0:T(8,128)} %param.1), channel_id=1, replica_groups=mesh['y'=4,'xh'=2,'xl'=2,'z'=8,'core'=2] {'y','xh','xl'}, dimensions={0} | all-to-all | bytes 2228224 | tf_op jit(solution)/shard_map/cond/branch_1_fun/all_to_all | solution.py:321
  83.1 0.1 branch_1_fun.1
  83.2 0.0 collective-permute-done.14.refs_7_
  83.2 0.0 collective-permute-done.6.refs_1_
  83.2 0.0 collective-permute-done.11.refs_2_
  83.2 0.0 collective-permute-done.13.refs_6_
  83.2 0.0 collective-permute-done.15.refs_8_
  83.2 4.5 %shard_map.54 = f32[16,128,128]{2,1,0:T(8,128)} custom-call(s32[5]{0:T(128)S(1)} %stack.29.refs_0_, f32[512,256]{1,0:T(8,128)} %collective-permute-done.6.refs_1_, f32[512,256]{1,0:T(8,128)} %collective-permute-done.11.refs_2_, f32[512,256]{1,0:T(8,128)S(1)} %collective-permute-done.5.refs_7_.refs_3_, f32[512,256]{1,0:T(8,128)S(1)} %collective-permute-done.7.refs_8_.refs_4_, ...), custom_call_target="tpu_custom_call" | custom-call | flops 1 | bytes 1 | tf_op jit(solution)/shard_map/pallas_call | solution.py:40
  87.7 4.9 %all-to-all-start.1 = ((f32[16,128,128]{2,1,0:T(8,128)}), f32[16,128,128]{2,1,0:T(8,128)S(1)}, u32[]{:S(2)}, u32[]{:S(2)}) async-start(f32[16,128,128]{2,1,0:T(8,128)} %shard_map.54), calls=%async_computation.1 | async-start | bytes 2097152 | tf_op jit(solution)/shard_map/all_to_all | solution.py:321
  92.6 0.3 collective-permute-start.17
  92.9 15.6 %all-to-all-done.1.refs_0_ = f32[16,128,128]{2,1,0:T(8,128)S(1)} async-done(((f32[16,128,128]{2,1,0:T(8,128)}), f32[16,128,128]{2,1,0:T(8,128)S(1)}, u32[]{:S(2)}, u32[]{:S(2)}) %all-to-all-start.1) | async-done | bytes 1048608 | tf_op jit(solution)/shard_map/all_to_all | solution.py:321
  108.5 0.1 shard_map.55.refs_1_
  108.5 1.5 %collective-permute-start.16 = (f32[128,128]{1,0:T(8,128)S(1)}, f32[128,128]{1,0:T(8,128)S(1)}, u32[]{:S(2)}, u32[]{:S(2)}) collective-permute-start(f32[128,128]{1,0:T(8,128)S(1)} %shard_map.55.refs_1_), channel_id=1, source_target_pairs={{0,16},{16,0},{1,17},{17,1},{2,18},{18,2},{3,19},{19,3},{4,20},{20... | collective-permute-start | bytes 196616 | tf_op jit(solution)/shard_map/ppermute | solution.py:424
  110.1 0.0 collective-permute-done.17.refs_4_
  110.1 2.8 %collective-permute-done.16.refs_2_ = f32[128,128]{1,0:T(8,128)S(1)} collective-permute-done((f32[128,128]{1,0:T(8,128)S(1)}, f32[128,128]{1,0:T(8,128)S(1)}, u32[]{:S(2)}, u32[]{:S(2)}) %collective-permute-start.16) | collective-permute-done | bytes 65568 | tf_op jit(solution)/shard_map/ppermute | solution.py:424
  112.9 0.8 shard_map.56
  113.7 1.9 %collective-permute-start.18 = (f32[128,256]{1,0:T(8,128)S(1)}, f32[128,256]{1,0:T(8,128)S(1)}, u32[]{:S(2)}, u32[]{:S(2)}) collective-permute-start(f32[128,256]{1,0:T(8,128)S(1)} %get-tuple-element.43), channel_id=1, source_target_pairs={{0,44},{1,2},{2,78},{3,37},{4,96},{5,71},{6,130},{7,105},{8,164},{... | collective-permute-start | bytes 393224 | tf_op jit(solution)/shard_map/ppermute | solution.py:428
  115.6 3.8 %collective-permute-start.19 = (f32[128,256]{1,0:T(8,128)S(1)}, f32[128,256]{1,0:T(8,128)S(1)}, u32[]{:S(2)}, u32[]{:S(2)}) collective-permute-start(f32[128,256]{1,0:T(8,128)S(1)} %get-tuple-element.44), channel_id=1, source_target_pairs={{0,3},{1,45},{2,36},{3,79},{4,70},{5,97},{6,104},{7,131},{8,138},{... | collective-permute-start | bytes 393224 | tf_op jit(solution)/shard_map/ppermute | solution.py:428
  119.4 6.3 %collective-permute-done.18 = f32[128,256]{1,0:T(8,128)S(1)} collective-permute-done((f32[128,256]{1,0:T(8,128)S(1)}, f32[128,256]{1,0:T(8,128)S(1)}, u32[]{:S(2)}, u32[]{:S(2)}) %collective-permute-start.18) | collective-permute-done | bytes 131104 | tf_op jit(solution)/shard_map/ppermute | solution.py:428
  125.7 0.1 collective-permute-done.19
  125.8 0.7 maximum_multiply_fusion
  (7 shorter events, 0.1 us)
Async XLA Ops:
  0.6 9.4 %copy-start.2 = (f32[4,4,64,256]{3,2,1,0:T(8,128)S(1)}, f32[4,4,64,256]{3,2,1,0:T(8,128)}, u32[]{:S(2)}) copy-start(f32[4,4,64,256]{3,2,1,0:T(8,128)} %param.5) | copy-start | bytes 3145732
  0.6 8.6 %copy-start.3 = (s32[4,4,9]{2,1,0:T(4,128)S(1)}, s32[4,4,9]{2,1,0:T(4,128)}, u32[]{:S(2)}) copy-start(s32[4,4,9]{2,1,0:T(4,128)} %param.6) | copy-start | bytes 1732
  1.8 8.3 %collective-permute-start = (f32[4,64,256]{2,1,0:T(8,128)S(1)}, f32[4,64,256]{2,1,0:T(8,128)S(1)}, u32[]{:S(2)}, u32[]{:S(2)}) collective-permute-start(f32[4,64,256]{2,1,0:T(8,128)S(1)} %fusion), channel_id=1, source_target_pairs={{0,16},{16,0},{1,17},{17,1},{2,18},{18,2},{3,19},{19,3},{4,20},{20... | collective-permute-start | bytes 786440 | tf_op jit(solution)/shard_map/ppermute | solution.py:169
  5.3 13.0 %collective-permute-start.1 = (f32[4,64,256]{2,1,0:T(8,128)S(1)}, f32[4,64,256]{2,1,0:T(8,128)S(1)}, u32[]{:S(2)}, u32[]{:S(2)}) collective-permute-start(f32[4,64,256]{2,1,0:T(8,128)S(1)} %get-tuple-element.46), channel_id=1, source_target_pairs={{0,32},{32,64},{64,96},{96,128},{128,160},{160,192},{192,224},{1,3... | collective-permute-start | bytes 786440 | tf_op jit(solution)/shard_map/ppermute | solution.py:170
  7.9 14.2 %collective-permute-start.2 = (f32[4,64,256]{2,1,0:T(8,128)S(1)}, f32[4,64,256]{2,1,0:T(8,128)S(1)}, u32[]{:S(2)}, u32[]{:S(2)}) collective-permute-start(f32[4,64,256]{2,1,0:T(8,128)S(1)} %get-tuple-element.45), channel_id=1, source_target_pairs={{32,0},{64,32},{96,64},{128,96},{160,128},{192,160},{224,192},{33,... | collective-permute-start | bytes 786440 | tf_op jit(solution)/shard_map/ppermute | solution.py:171
  10.1 1.7 %copy-start = (f32[4,4,9,4096]{3,1,2,0:T(4,128)S(1)}, f32[4,4,9,4096]{3,1,2,0:T(4,128)}, u32[]{:S(2)}) copy-start(f32[4,4,9,4096]{3,1,2,0:T(4,128)} %param.7) | copy-start | bytes 7077892
  11.7 15.5 %copy-start.1 = (f32[4,4,9,4096]{3,1,2,0:T(4,128)S(1)}, f32[4,4,9,4096]{3,1,2,0:T(4,128)}, u32[]{:S(2)}) copy-start(f32[4,4,9,4096]{3,1,2,0:T(4,128)} %param.7) | copy-start | bytes 7077892
  13.8 16.9 %collective-permute-start.4 = (f32[512,256]{1,0:T(8,128)S(1)}, f32[512,256]{1,0:T(8,128)S(1)}, u32[]{:S(2)}, u32[]{:S(2)}) collective-permute-start(f32[512,256]{1,0:T(8,128)S(1)} %bitcast.28), channel_id=1, source_target_pairs={{0,2},{2,4},{4,6},{6,8},{8,10},{10,12},{12,14},{14,0},{1,3},{3,5},... | collective-permute-start | bytes 1572872 | tf_op jit(solution)/shard_map/ppermute | solution.py:193
  15.8 14.9 %collective-permute-start.5 = (f32[512,256]{1,0:T(8,128)S(1)}, f32[512,256]{1,0:T(8,128)S(1)}, u32[]{:S(2)}, u32[]{:S(2)}) collective-permute-start(f32[512,256]{1,0:T(8,128)S(1)} %bitcast.29), channel_id=1, source_target_pairs={{0,15},{1,14},{2,1},{3,0},{4,2},{5,3},{6,4},{7,5},{8,6},{9,7},{10,... | collective-permute-start | bytes 1572872 | tf_op jit(solution)/shard_map/ppermute | solution.py:193
  22.2 5.1 %collective-permute-start.3 = (f32[2,64,256]{2,1,0:T(8,128)S(1)}, f32[2,64,256]{2,1,0:T(8,128)S(1)}, u32[]{:S(2)}, u32[]{:S(2)}) collective-permute-start(f32[2,64,256]{2,1,0:T(8,128)S(1)} %maximum_select_fusion), channel_id=1, source_target_pairs={{0,16},{16,0},{1,17},{17,1},{2,18},{18,2},{3,19},{19,3},{4,20},{20... | collective-permute-start | bytes 393224 | tf_op jit(solution)/shard_map/ppermute | solution.py:198
  24.1 12.6 %collective-permute-start.9 = (f32[512,256]{1,0:T(8,128)S(1)}, f32[512,256]{1,0:T(8,128)S(1)}, u32[]{:S(2)}, u32[]{:S(2)}) collective-permute-start(f32[512,256]{1,0:T(8,128)S(1)} %bitcast.30), channel_id=1, source_target_pairs={{0,1},{1,0},{2,3},{3,2},{4,5},{5,4},{6,7},{7,6},{8,9},{9,8},{10,11... | collective-permute-start | bytes 1572872 | tf_op jit(solution)/shard_map/ppermute | solution.py:388
  30.7 9.3 %collective-permute-start.10 = (f32[512,256]{1,0:T(8,128)S(1)}, f32[512,256]{1,0:T(8,128)S(1)}, u32[]{:S(2)}, u32[]{:S(2)}) collective-permute-start(f32[512,256]{1,0:T(8,128)S(1)} %bitcast.34), channel_id=1, source_target_pairs={{0,1},{1,0},{2,3},{3,2},{4,5},{5,4},{6,7},{7,6},{8,9},{9,8},{10,11... | collective-permute-start | bytes 1572872 | tf_op jit(solution)/shard_map/ppermute | solution.py:388
  30.7 17.0 %collective-permute-start.7 = (f32[512,256]{1,0:T(8,128)S(1)}, f32[512,256]{1,0:T(8,128)S(1)}, u32[]{:S(2)}, u32[]{:S(2)}) collective-permute-start(f32[512,256]{1,0:T(8,128)S(1)} %bitcast.35), channel_id=1, source_target_pairs={{0,15},{1,14},{2,1},{3,0},{4,2},{5,3},{6,4},{7,5},{8,6},{9,7},{10,... | collective-permute-start | bytes 1572872 | tf_op jit(solution)/shard_map/ppermute | solution.py:386
  35.4 16.0 %collective-permute-start.8 = (f32[512,256]{1,0:T(8,128)S(1)}, f32[512,256]{1,0:T(8,128)S(1)}, u32[]{:S(2)}, u32[]{:S(2)}) collective-permute-start(f32[512,256]{1,0:T(8,128)S(1)} %bitcast.36), channel_id=1, source_target_pairs={{0,2},{2,4},{4,6},{6,8},{8,10},{10,12},{12,14},{14,0},{1,3},{3,5},... | collective-permute-start | bytes 1572872 | tf_op jit(solution)/shard_map/ppermute | solution.py:387
  35.4 19.1 %collective-permute-start.12 = (f32[512,256]{1,0:T(8,128)S(1)}, f32[512,256]{1,0:T(8,128)S(1)}, u32[]{:S(2)}, u32[]{:S(2)}) collective-permute-start(f32[512,256]{1,0:T(8,128)S(1)} %collective-permute-done.5.refs_7_.refs_3_), channel_id=1, source_target_pairs={{0,1},{1,0},{2,3},{3,2},{4,5},{5,4},{6,7},{7,6},{8,9},{9,8},{10,11... | collective-permute-start | bytes 1572872 | tf_op jit(solution)/shard_map/ppermute | solution.py:408
  36.7 46.5 %collective-permute-start.14 = (f32[512,256]{1,0:T(8,128)S(1)}, f32[512,256]{1,0:T(8,128)S(1)}, u32[]{:S(2)}, u32[]{:S(2)}) collective-permute-start(f32[512,256]{1,0:T(8,128)S(1)} %collective-permute-done.5.refs_7_.refs_3_), channel_id=1, source_target_pairs={{0,14},{2,0},{4,2},{6,4},{8,6},{10,8},{12,10},{14,12},{1,15},{3,1}... | collective-permute-start | bytes 1572872 | tf_op jit(solution)/shard_map/ppermute | solution.py:407
  39.9 43.3 %collective-permute-start.6 = (f32[512,256]{1,0:T(8,128)S(1)}, f32[512,256]{1,0:T(8,128)}, u32[]{:S(2)}, u32[]{:S(2)}) collective-permute-start(f32[512,256]{1,0:T(8,128)S(1)} %collective-permute-done.4.refs_5_.refs_9_), channel_id=1, source_target_pairs={{0,2},{2,4},{4,6},{6,8},{8,10},{10,12},{12,14},{14,0},{1,3},{3,5},... | collective-permute-start | bytes 1572872 | tf_op jit(solution)/shard_map/ppermute | solution.py:406
  54.5 28.7 %collective-permute-start.11 = (f32[512,256]{1,0:T(8,128)S(1)}, f32[512,256]{1,0:T(8,128)}, u32[]{:S(2)}, u32[]{:S(2)}) collective-permute-start(f32[512,256]{1,0:T(8,128)S(1)} %collective-permute-done.8.refs_6_.refs_10_), channel_id=1, source_target_pairs={{0,2},{2,4},{4,6},{6,8},{8,10},{10,12},{12,14},{14,0},{1,3},{3,5},... | collective-permute-start | bytes 1572872 | tf_op jit(solution)/shard_map/ppermute | solution.py:406
  54.5 28.7 %collective-permute-start.13 = (f32[512,256]{1,0:T(8,128)S(1)}, f32[512,256]{1,0:T(8,128)}, u32[]{:S(2)}, u32[]{:S(2)}) collective-permute-start(f32[512,256]{1,0:T(8,128)S(1)} %collective-permute-done.7.refs_8_.refs_4_), channel_id=1, source_target_pairs={{0,1},{1,0},{2,3},{3,2},{4,5},{5,4},{6,7},{7,6},{8,9},{9,8},{10,11... | collective-permute-start | bytes 1572872 | tf_op jit(solution)/shard_map/ppermute | solution.py:408
  54.5 28.7 %collective-permute-start.15 = (f32[512,256]{1,0:T(8,128)S(1)}, f32[512,256]{1,0:T(8,128)}, u32[]{:S(2)}, u32[]{:S(2)}) collective-permute-start(f32[512,256]{1,0:T(8,128)S(1)} %collective-permute-done.7.refs_8_.refs_4_), channel_id=1, source_target_pairs={{0,14},{2,0},{4,2},{6,4},{8,6},{10,8},{12,10},{14,12},{1,15},{3,1}... | collective-permute-start | bytes 1572872 | tf_op jit(solution)/shard_map/ppermute | solution.py:407
  87.7 20.8 %all-to-all-start.1 = ((f32[16,128,128]{2,1,0:T(8,128)}), f32[16,128,128]{2,1,0:T(8,128)S(1)}, u32[]{:S(2)}, u32[]{:S(2)}) async-start(f32[16,128,128]{2,1,0:T(8,128)} %shard_map.54), calls=%async_computation.1 | async-start | bytes 2097152 | tf_op jit(solution)/shard_map/all_to_all | solution.py:321
  92.6 17.5 %collective-permute-start.17 = (f32[136,128]{1,0:T(8,128)S(1)}, f32[136,128]{1,0:T(8,128)S(1)}, u32[]{:S(2)}, u32[]{:S(2)}) collective-permute-start(f32[136,128]{1,0:T(8,128)S(1)} %get-tuple-element.57.refs_11_.refs_3_), channel_id=1, source_target_pairs={{0,16},{16,0},{1,17},{17,1},{2,18},{18,2},{3,19},{19,3},{4,20},{20... | collective-permute-start | bytes 208904 | tf_op jit(solution)/shard_map/ppermute | solution.py:422
  108.5 4.4 %collective-permute-start.16 = (f32[128,128]{1,0:T(8,128)S(1)}, f32[128,128]{1,0:T(8,128)S(1)}, u32[]{:S(2)}, u32[]{:S(2)}) collective-permute-start(f32[128,128]{1,0:T(8,128)S(1)} %shard_map.55.refs_1_), channel_id=1, source_target_pairs={{0,16},{16,0},{1,17},{17,1},{2,18},{18,2},{3,19},{19,3},{4,20},{20... | collective-permute-start | bytes 196616 | tf_op jit(solution)/shard_map/ppermute | solution.py:424
  113.7 12.0 %collective-permute-start.18 = (f32[128,256]{1,0:T(8,128)S(1)}, f32[128,256]{1,0:T(8,128)S(1)}, u32[]{:S(2)}, u32[]{:S(2)}) collective-permute-start(f32[128,256]{1,0:T(8,128)S(1)} %get-tuple-element.43), channel_id=1, source_target_pairs={{0,44},{1,2},{2,78},{3,37},{4,96},{5,71},{6,130},{7,105},{8,164},{... | collective-permute-start | bytes 393224 | tf_op jit(solution)/shard_map/ppermute | solution.py:428
  115.6 10.1 %collective-permute-start.19 = (f32[128,256]{1,0:T(8,128)S(1)}, f32[128,256]{1,0:T(8,128)S(1)}, u32[]{:S(2)}, u32[]{:S(2)}) collective-permute-start(f32[128,256]{1,0:T(8,128)S(1)} %get-tuple-element.44), channel_id=1, source_target_pairs={{0,3},{1,45},{2,36},{3,79},{4,70},{5,97},{6,104},{7,131},{8,138},{... | collective-permute-start | bytes 393224 | tf_op jit(solution)/shard_map/ppermute | solution.py:428

commit v5 on v4

--- a/solution.py
+++ b/solution.py
@@ -388,8 +388,10 @@
     held_other = [lax.ppermute(half, "core", SWAP) for half in held]
     square = call(square_kernel, array(4, 136, 128), [], [spot], *held, *held_other)
     sure = links[0, 0, 0] >= 0
-    next_1[1], last_1[1], square, sure = lax.optimization_barrier(
-        (next_1[1], last_1[1], square, sure)
+    next_1[1], square, sure = lax.optimization_barrier((next_1[1], square, sure))
+    next_other = [lax.ppermute(half, "core", SWAP) for half in next_1]
+    next_1[1], last_1[1], square, next_other[1] = lax.optimization_barrier(
+        (next_1[1], last_1[1], square, next_other[1])
     )
     near = call(
         near_kernel,
@@ -405,7 +407,6 @@
     next_1[1], last_1[1], near = lax.optimization_barrier((next_1[1], last_1[1], near))
     last_2 = [lax.ppermute(half, "z", UP) for half in last_1]
     next_2 = [lax.ppermute(half, "z", DOWN) for half in next_1]
-    next_other = [lax.ppermute(half, "core", SWAP) for half in next_1]
     near = lax.cond(sure, gathered, lambda blocks: blocks[0], near)
     far = call(
         far_kernel,

time: 129 us -> 127 us (0.984)
  blocking collectives: 25.4 us -> 24 us
    ppermute x1, waiting for transfers between devices: 3.73 us -> 0.99 us  [body(): last_1 = [early[0], lax.ppermute(held[1], 'z', UP)]]
    ppermute x1, waiting for transfers between devices: 6.35 us -> 9 us  [body(): next_1 = [early[1], lax.ppermute(held[1], ('z', 'core'), DOWN_TURNED)]]
    all_to_all x1, blocking collectives: 25.4 us -> 24 us  [gathered(): blocks = lax.all_to_all(blocks, PLANE, 0, 0, tiled=True)]
where the time goes in v5:
time: 127 us; the launch traced here: 125 us
  waiting for transfers between devices  43.7 us (34%)
  starting transfers between devices  35.8 us (28%)
  blocking collectives  24 us (19%)
  Pallas kernels  14.1 us (11%)
  local copies, waits for them, and re-layouts  3.56 us (3%)
  other arithmetic  2 us (2%)
  between operations  1.5 us (1%)
    all_to_all x1, blocking collectives, gathered(): blocks = lax.all_to_all(blocks, PLANE, 0, 0, tiled=True)  24 us
    all_to_all x1, waiting for transfers between devices, gathered(): blocks = lax.all_to_all(blocks, PLANE, 0, 0, tiled=True)  15.4 us
    pallas_call x8, Pallas kernels, call(): pl.pallas_call(ordered, out_shape=shape, in_specs=[SMEM] * len(scalars) +...  14.1 us
    ppermute x1, waiting for transfers between devices, body(): next_1 = [early[1], lax.ppermute(held[1], ('z', 'core'), DOWN_TURNED)]  9 us
    ppermute x2, waiting for transfers between devices, body(): got = [lax.ppermute(sent[k], ALL, routes(k)) for k in range(2)]  6.53 us
    ppermute x2, starting transfers between devices, body(): next_2 = [lax.ppermute(half, 'z', DOWN) for half in next_1]  6.38 us
    all_to_all x1, starting transfers between devices, gathered(): blocks = lax.all_to_all(blocks, PLANE, 0, 0, tiled=True)  4.96 us
    ppermute x2, starting transfers between devices, body(): got = [lax.ppermute(sent[k], ALL, routes(k)) for k in range(2)]  4.8 us
  transfers between devices with their start and end apart: 21, of which 10 were waited for; matrix products, arithmetic and copies ran while one was open for 2% of the time, Pallas kernels for 7%

profile of v5, /device:TPU:2, one launch (start us, length us, event | category | flops | bytes accessed | tf_op | source)
XLA Modules:
  0.0 124.6 jit_solution(3720877918537032890)
XLA Ops:
  0.6 0.0 copy-start.2
  0.6 0.0 copy-start.3
  0.7 1.2 fusion
  1.8 2.4 %collective-permute-start = (f32[4,64,256]{2,1,0:T(8,128)S(1)}, f32[4,64,256]{2,1,0:T(8,128)S(1)}, u32[]{:S(2)}, u32[]{:S(2)}) collective-permute-start(f32[4,64,256]{2,1,0:T(8,128)S(1)} %fusion), channel_id=1, source_target_pairs={{0,16},{16,0},{1,17},{17,1},{2,18},{18,2},{3,19},{19,3},{4,20},{20... | collective-permute-start | bytes 786440 | tf_op jit(solution)/shard_map/ppermute | solution.py:169
  4.2 1.1 slice_bitcast_fusion.1
  5.3 2.6 %collective-permute-start.1 = (f32[4,64,256]{2,1,0:T(8,128)S(1)}, f32[4,64,256]{2,1,0:T(8,128)S(1)}, u32[]{:S(2)}, u32[]{:S(2)}) collective-permute-start(f32[4,64,256]{2,1,0:T(8,128)S(1)} %get-tuple-element.52), channel_id=1, source_target_pairs={{0,32},{32,64},{64,96},{96,128},{128,160},{160,192},{192,224},{1,3... | collective-permute-start | bytes 786440 | tf_op jit(solution)/shard_map/ppermute | solution.py:170
  7.9 1.3 %collective-permute-start.2 = (f32[4,64,256]{2,1,0:T(8,128)S(1)}, f32[4,64,256]{2,1,0:T(8,128)S(1)}, u32[]{:S(2)}, u32[]{:S(2)}) collective-permute-start(f32[4,64,256]{2,1,0:T(8,128)S(1)} %get-tuple-element.51), channel_id=1, source_target_pairs={{32,0},{64,32},{96,64},{128,96},{160,128},{192,160},{224,192},{33,... | collective-permute-start | bytes 786440 | tf_op jit(solution)/shard_map/ppermute | solution.py:171
  9.2 0.0 copy-done.3
  9.2 0.1 copy.7
  9.3 0.1 select_reduce_fusion
  9.4 0.1 reshape.25.refs_1_
  9.5 0.1 stack.29.refs_0_
  9.6 0.5 collective-permute-done.refs_3_.refs_5_
  10.1 1.7 %copy-done = f32[4,4,9,4096]{3,1,2,0:T(4,128)S(1)} copy-done((f32[4,4,9,4096]{3,1,2,0:T(4,128)S(1)}, f32[4,4,9,4096]{3,1,2,0:T(4,128)}, u32[]{:S(2)}) %copy-start) | copy-done | bytes 2359320
  11.7 2.0 %shard_map.50 = (f32[8,64,256]{2,1,0:T(8,128)S(1)}, f32[8,64,256]{2,1,0:T(8,128)S(1)}) custom-call(s32[5]{0:T(128)S(1)} %stack.29.refs_0_, s32[144]{0:T(256)S(1)} %reshape.25.refs_1_, f32[16,64,256]{2,1,0:T(8,128)S(1)} %bitcast.33, f32[4,64,256]{2,1,0:T(8,128)S(1)} %collective-permute-done.refs_3_.refs_5_, f32[4,9,4,4096]{3,2,1,0:T(4,128)S(1)} %bitcast.26), custom_call_target="tpu_custom_call" | custom-call | flops 1 | bytes 1 | tf_op jit(solution)/shard_map/pallas_call | solution.py:40
  13.8 2.0 %collective-permute-start.4 = (f32[512,256]{1,0:T(8,128)S(1)}, f32[512,256]{1,0:T(8,128)S(1)}, u32[]{:S(2)}, u32[]{:S(2)}) collective-permute-start(f32[512,256]{1,0:T(8,128)S(1)} %bitcast.28), channel_id=1, source_target_pairs={{0,2},{2,4},{4,6},{6,8},{8,10},{10,12},{12,14},{14,0},{1,3},{3,5},... | collective-permute-start | bytes 1572872 | tf_op jit(solution)/shard_map/ppermute | solution.py:193
  15.8 2.5 %collective-permute-start.5 = (f32[512,256]{1,0:T(8,128)S(1)}, f32[512,256]{1,0:T(8,128)S(1)}, u32[]{:S(2)}, u32[]{:S(2)}) collective-permute-start(f32[512,256]{1,0:T(8,128)S(1)} %bitcast.29), channel_id=1, source_target_pairs={{0,15},{1,14},{2,1},{3,0},{4,2},{5,3},{6,4},{7,5},{8,6},{9,7},{10,... | collective-permute-start | bytes 1572872 | tf_op jit(solution)/shard_map/ppermute | solution.py:193
  18.3 0.0 collective-permute-done.1.refs_3_
  18.3 3.9 %collective-permute-done.2.refs_4_ = f32[4,64,256]{2,1,0:T(8,128)S(1)} collective-permute-done((f32[4,64,256]{2,1,0:T(8,128)S(1)}, f32[4,64,256]{2,1,0:T(8,128)S(1)}, u32[]{:S(2)}, u32[]{:S(2)}) %collective-permute-start.2) | collective-permute-done | bytes 262176 | tf_op jit(solution)/shard_map/ppermute | solution.py:171
  22.2 1.9 %collective-permute-start.3 = (f32[2,64,256]{2,1,0:T(8,128)S(1)}, f32[2,64,256]{2,1,0:T(8,128)S(1)}, u32[]{:S(2)}, u32[]{:S(2)}) collective-permute-start(f32[2,64,256]{2,1,0:T(8,128)S(1)} %maximum_select_fusion), channel_id=1, source_target_pairs={{0,16},{16,0},{1,17},{17,1},{2,18},{18,2},{3,19},{19,3},{4,20},{20... | collective-permute-start | bytes 393224 | tf_op jit(solution)/shard_map/ppermute | solution.py:198
  24.1 0.0 collective-permute-start.8
  24.1 3.2 %collective-permute-done.3.refs_6_ = f32[2,64,256]{2,1,0:T(8,128)S(1)} collective-permute-done((f32[2,64,256]{2,1,0:T(8,128)S(1)}, f32[2,64,256]{2,1,0:T(8,128)S(1)}, u32[]{:S(2)}, u32[]{:S(2)}) %collective-permute-start.3) | collective-permute-done | bytes 131104 | tf_op jit(solution)/shard_map/ppermute | solution.py:198
  27.2 2.2 %shard_map.51 = (f32[8,64,256]{2,1,0:T(8,128)S(1)}, f32[16,64,256]{2,1,0:T(8,128)}) custom-call(s32[5]{0:T(128)S(1)} %stack.29.refs_0_, s32[144]{0:T(256)S(1)} %reshape.25.refs_1_, f32[8,64,256]{2,1,0:T(8,128)S(1)} %get-tuple-element.29.refs_2_, f32[4,64,256]{2,1,0:T(8,128)S(1)} %collective-permute-done.1.refs_3_, ...), custom_call_target="tpu_custom_call" | custom-call | flops 1 | bytes 1 | tf_op jit(solution)/shard_map/pallas_call | solution.py:40
  29.4 1.2 collective-permute-done.4.refs_5_.refs_9_
  30.6 0.0 collective-permute-done.5.refs_7_.refs_3_
  30.7 0.0 collective-permute-start.9
  30.7 4.7 %collective-permute-start.7 = (f32[512,256]{1,0:T(8,128)S(1)}, f32[512,256]{1,0:T(8,128)S(1)}, u32[]{:S(2)}, u32[]{:S(2)}) collective-permute-start(f32[512,256]{1,0:T(8,128)S(1)} %bitcast.35), channel_id=1, source_target_pairs={{0,15},{1,14},{2,1},{3,0},{4,2},{5,3},{6,4},{7,5},{8,6},{9,7},{10,... | collective-permute-start | bytes 1572872 | tf_op jit(solution)/shard_map/ppermute | solution.py:386
  35.4 0.5 slice.54
  36.6 0.1 collective-permute-start.10
  36.7 0.0 collective-permute-done.8.refs_3_
  36.7 0.0 collective-permute-done.9.refs_4_
  36.7 1.4 %shard_map.52.refs_9_ = f32[4,136,128]{2,1,0:T(8,128)S(1)} custom-call(s32[5]{0:T(128)S(1)} %stack.29.refs_0_, f32[512,256]{1,0:T(8,128)S(1)} %bitcast.31, f32[512,256]{1,0:T(8,128)S(1)} %bitcast.37, f32[512,256]{1,0:T(8,128)S(1)} %collective-permute-done.8.refs_3_, f32[512,256]{1,0:T(8,128)S(1)} %collective-permute-done.9.refs_4_), custom_call_target="tpu_custom_call" | custom-call | flops 1 | bytes 1 | tf_op jit(solution)/shard_map/pallas_call | solution.py:40
  38.1 9.0 %collective-permute-done.7.refs_8_.refs_4_ = f32[512,256]{1,0:T(8,128)S(1)} collective-permute-done((f32[512,256]{1,0:T(8,128)S(1)}, f32[512,256]{1,0:T(8,128)S(1)}, u32[]{:S(2)}, u32[]{:S(2)}) %collective-permute-start.7) | collective-permute-done | bytes 524320 | tf_op jit(solution)/shard_map/ppermute | solution.py:386
  47.1 0.0 collective-permute-start.11
  47.1 0.5 collective-permute-start.13
  47.6 3.2 %collective-permute-start.14 = (f32[512,256]{1,0:T(8,128)S(1)}, f32[512,256]{1,0:T(8,128)}, u32[]{:S(2)}, u32[]{:S(2)}) collective-permute-start(f32[512,256]{1,0:T(8,128)S(1)} %collective-permute-done.5.refs_7_.refs_3_), channel_id=1, source_target_pairs={{0,14},{2,0},{4,2},{6,4},{8,6},{10,8},{12,10},{14,12},{1,15},{3,1}... | collective-permute-start | bytes 1572872 | tf_op jit(solution)/shard_map/ppermute | solution.py:409
  50.8 0.0 collective-permute-start.6
  50.8 1.0 collective-permute-done.10.refs_6_.refs_10_
  51.8 0.0 collective-permute-done.11.refs_6_
  51.8 3.1 %shard_map.53 = f32[16,136,128]{2,1,0:T(8,128)} custom-call(s32[5]{0:T(128)S(1)} %stack.29.refs_0_, f32[512,256]{1,0:T(8,128)S(1)} %bitcast.32, f32[512,256]{1,0:T(8,128)S(1)} %bitcast.38, f32[512,256]{1,0:T(8,128)S(1)} %collective-permute-done.8.refs_3_, f32[512,256]{1,0:T(8,128)S(1)} %collective-permute-done.9.refs_4_, ...), custom_call_target="tpu_custom_call" | custom-call | flops 1 | bytes 1 | tf_op jit(solution)/shard_map/pallas_call | solution.py:40
  54.8 0.0 collective-permute-start.12
  54.8 3.2 %collective-permute-start.15 = (f32[512,256]{1,0:T(8,128)S(1)}, f32[512,256]{1,0:T(8,128)}, u32[]{:S(2)}, u32[]{:S(2)}) collective-permute-start(f32[512,256]{1,0:T(8,128)S(1)} %collective-permute-done.7.refs_8_.refs_4_), channel_id=1, source_target_pairs={{0,14},{2,0},{4,2},{6,4},{8,6},{10,8},{12,10},{14,12},{1,15},{3,1}... | collective-permute-start | bytes 1572872 | tf_op jit(solution)/shard_map/ppermute | solution.py:409
  58.1 24.0 %conditional.1 = (f32[136,128]{1,0:T(8,128)S(1)}) conditional(s32[]{:T(128)} %convert_element_type.3, f32[16,136,128]{2,1,0:T(8,128)} %shard_map.53, f32[16,136,128]{2,1,0:T(8,128)} %shard_map.53), branch_computations={%region_1.2_spmd, %region_2.3_spmd} | conditional | flops 1 | bytes 2228233 | solution.py:410
  58.1 24.0 %all_to_all.9.refs_0_ = f32[16,136,128]{2,1,0:T(8,128)S(1)} all-to-all(f32[16,136,128]{2,1,0:T(8,128)} %param.1), channel_id=1, replica_groups=mesh['y'=4,'xh'=2,'xl'=2,'z'=8,'core'=2] {'y','xh','xl'}, dimensions={0} | all-to-all | bytes 2228224 | tf_op jit(solution)/shard_map/cond/branch_1_fun/all_to_all | solution.py:321
  82.1 0.1 branch_1_fun.1
  82.1 0.0 collective-permute-done.13.refs_5_
  82.1 0.0 collective-permute-done.14.refs_7_
  82.1 0.0 collective-permute-done.6.refs_1_
  82.1 0.0 collective-permute-done.12.refs_2_
  82.2 0.0 collective-permute-done.15.refs_8_
  82.2 4.5 %shard_map.54 = f32[16,128,128]{2,1,0:T(8,128)} custom-call(s32[5]{0:T(128)S(1)} %stack.29.refs_0_, f32[512,256]{1,0:T(8,128)} %collective-permute-done.6.refs_1_, f32[512,256]{1,0:T(8,128)} %collective-permute-done.12.refs_2_, f32[512,256]{1,0:T(8,128)S(1)} %collective-permute-done.5.refs_7_.refs_3_, f32[512,256]{1,0:T(8,128)S(1)} %collective-permute-done.7.refs_8_.refs_4_, ...), custom_call_target="tpu_custom_call" | custom-call | flops 1 | bytes 1 | tf_op jit(solution)/shard_map/pallas_call | solution.py:40
  86.6 5.0 %all-to-all-start.1 = ((f32[16,128,128]{2,1,0:T(8,128)}), f32[16,128,128]{2,1,0:T(8,128)S(1)}, u32[]{:S(2)}, u32[]{:S(2)}) async-start(f32[16,128,128]{2,1,0:T(8,128)} %shard_map.54), calls=%async_computation.1 | async-start | bytes 2097152 | tf_op jit(solution)/shard_map/all_to_all | solution.py:321
  91.6 0.3 collective-permute-start.17
  91.9 15.4 %all-to-all-done.1.refs_0_ = f32[16,128,128]{2,1,0:T(8,128)S(1)} async-done(((f32[16,128,128]{2,1,0:T(8,128)}), f32[16,128,128]{2,1,0:T(8,128)S(1)}, u32[]{:S(2)}, u32[]{:S(2)}) %all-to-all-start.1) | async-done | bytes 1048608 | tf_op jit(solution)/shard_map/all_to_all | solution.py:321
  107.3 0.1 shard_map.55.refs_1_
  107.4 1.4 %collective-permute-start.16 = (f32[128,128]{1,0:T(8,128)S(1)}, f32[128,128]{1,0:T(8,128)S(1)}, u32[]{:S(2)}, u32[]{:S(2)}) collective-permute-start(f32[128,128]{1,0:T(8,128)S(1)} %shard_map.55.refs_1_), channel_id=1, source_target_pairs={{0,16},{16,0},{1,17},{17,1},{2,18},{18,2},{3,19},{19,3},{4,20},{20... | collective-permute-start | bytes 196616 | tf_op jit(solution)/shard_map/ppermute | solution.py:425
  108.7 0.0 collective-permute-done.17.refs_4_
  108.7 3.0 %collective-permute-done.16.refs_2_ = f32[128,128]{1,0:T(8,128)S(1)} collective-permute-done((f32[128,128]{1,0:T(8,128)S(1)}, f32[128,128]{1,0:T(8,128)S(1)}, u32[]{:S(2)}, u32[]{:S(2)}) %collective-permute-start.16) | collective-permute-done | bytes 65568 | tf_op jit(solution)/shard_map/ppermute | solution.py:425
  111.7 0.8 shard_map.56
  112.5 1.9 %collective-permute-start.18 = (f32[128,256]{1,0:T(8,128)S(1)}, f32[128,256]{1,0:T(8,128)S(1)}, u32[]{:S(2)}, u32[]{:S(2)}) collective-permute-start(f32[128,256]{1,0:T(8,128)S(1)} %get-tuple-element.49), channel_id=1, source_target_pairs={{0,44},{1,2},{2,78},{3,37},{4,96},{5,71},{6,130},{7,105},{8,164},{... | collective-permute-start | bytes 393224 | tf_op jit(solution)/shard_map/ppermute | solution.py:429
  114.4 2.9 %collective-permute-start.19 = (f32[128,256]{1,0:T(8,128)S(1)}, f32[128,256]{1,0:T(8,128)S(1)}, u32[]{:S(2)}, u32[]{:S(2)}) collective-permute-start(f32[128,256]{1,0:T(8,128)S(1)} %get-tuple-element.50), channel_id=1, source_target_pairs={{0,3},{1,45},{2,36},{3,79},{4,70},{5,97},{6,104},{7,131},{8,138},{... | collective-permute-start | bytes 393224 | tf_op jit(solution)/shard_map/ppermute | solution.py:429
  117.3 6.3 %collective-permute-done.18 = f32[128,256]{1,0:T(8,128)S(1)} collective-permute-done((f32[128,256]{1,0:T(8,128)S(1)}, f32[128,256]{1,0:T(8,128)S(1)}, u32[]{:S(2)}, u32[]{:S(2)}) %collective-permute-start.18) | collective-permute-done | bytes 131104 | tf_op jit(solution)/shard_map/ppermute | solution.py:429
  123.7 0.2 collective-permute-done.19
  123.9 0.7 maximum_multiply_fusion
  (7 shorter events, 0.1 us)
Async XLA Ops:
  0.6 9.4 %copy-start.2 = (f32[4,4,64,256]{3,2,1,0:T(8,128)S(1)}, f32[4,4,64,256]{3,2,1,0:T(8,128)}, u32[]{:S(2)}) copy-start(f32[4,4,64,256]{3,2,1,0:T(8,128)} %param.5) | copy-start | bytes 3145732
  0.6 8.6 %copy-start.3 = (s32[4,4,9]{2,1,0:T(4,128)S(1)}, s32[4,4,9]{2,1,0:T(4,128)}, u32[]{:S(2)}) copy-start(s32[4,4,9]{2,1,0:T(4,128)} %param.6) | copy-start | bytes 1732
  1.8 8.3 %collective-permute-start = (f32[4,64,256]{2,1,0:T(8,128)S(1)}, f32[4,64,256]{2,1,0:T(8,128)S(1)}, u32[]{:S(2)}, u32[]{:S(2)}) collective-permute-start(f32[4,64,256]{2,1,0:T(8,128)S(1)} %fusion), channel_id=1, source_target_pairs={{0,16},{16,0},{1,17},{17,1},{2,18},{18,2},{3,19},{19,3},{4,20},{20... | collective-permute-start | bytes 786440 | tf_op jit(solution)/shard_map/ppermute | solution.py:169
  5.3 13.0 %collective-permute-start.1 = (f32[4,64,256]{2,1,0:T(8,128)S(1)}, f32[4,64,256]{2,1,0:T(8,128)S(1)}, u32[]{:S(2)}, u32[]{:S(2)}) collective-permute-start(f32[4,64,256]{2,1,0:T(8,128)S(1)} %get-tuple-element.52), channel_id=1, source_target_pairs={{0,32},{32,64},{64,96},{96,128},{128,160},{160,192},{192,224},{1,3... | collective-permute-start | bytes 786440 | tf_op jit(solution)/shard_map/ppermute | solution.py:170
  7.9 14.2 %collective-permute-start.2 = (f32[4,64,256]{2,1,0:T(8,128)S(1)}, f32[4,64,256]{2,1,0:T(8,128)S(1)}, u32[]{:S(2)}, u32[]{:S(2)}) collective-permute-start(f32[4,64,256]{2,1,0:T(8,128)S(1)} %get-tuple-element.51), channel_id=1, source_target_pairs={{32,0},{64,32},{96,64},{128,96},{160,128},{192,160},{224,192},{33,... | collective-permute-start | bytes 786440 | tf_op jit(solution)/shard_map/ppermute | solution.py:171
  10.1 1.7 %copy-start = (f32[4,4,9,4096]{3,1,2,0:T(4,128)S(1)}, f32[4,4,9,4096]{3,1,2,0:T(4,128)}, u32[]{:S(2)}) copy-start(f32[4,4,9,4096]{3,1,2,0:T(4,128)} %param.7) | copy-start | bytes 7077892
  11.7 15.5 %copy-start.1 = (f32[4,4,9,4096]{3,1,2,0:T(4,128)S(1)}, f32[4,4,9,4096]{3,1,2,0:T(4,128)}, u32[]{:S(2)}) copy-start(f32[4,4,9,4096]{3,1,2,0:T(4,128)} %param.7) | copy-start | bytes 7077892
  13.8 16.9 %collective-permute-start.4 = (f32[512,256]{1,0:T(8,128)S(1)}, f32[512,256]{1,0:T(8,128)S(1)}, u32[]{:S(2)}, u32[]{:S(2)}) collective-permute-start(f32[512,256]{1,0:T(8,128)S(1)} %bitcast.28), channel_id=1, source_target_pairs={{0,2},{2,4},{4,6},{6,8},{8,10},{10,12},{12,14},{14,0},{1,3},{3,5},... | collective-permute-start | bytes 1572872 | tf_op jit(solution)/shard_map/ppermute | solution.py:193
  15.8 14.9 %collective-permute-start.5 = (f32[512,256]{1,0:T(8,128)S(1)}, f32[512,256]{1,0:T(8,128)S(1)}, u32[]{:S(2)}, u32[]{:S(2)}) collective-permute-start(f32[512,256]{1,0:T(8,128)S(1)} %bitcast.29), channel_id=1, source_target_pairs={{0,15},{1,14},{2,1},{3,0},{4,2},{5,3},{6,4},{7,5},{8,6},{9,7},{10,... | collective-permute-start | bytes 1572872 | tf_op jit(solution)/shard_map/ppermute | solution.py:193
  22.2 5.1 %collective-permute-start.3 = (f32[2,64,256]{2,1,0:T(8,128)S(1)}, f32[2,64,256]{2,1,0:T(8,128)S(1)}, u32[]{:S(2)}, u32[]{:S(2)}) collective-permute-start(f32[2,64,256]{2,1,0:T(8,128)S(1)} %maximum_select_fusion), channel_id=1, source_target_pairs={{0,16},{16,0},{1,17},{17,1},{2,18},{18,2},{3,19},{19,3},{4,20},{20... | collective-permute-start | bytes 393224 | tf_op jit(solution)/shard_map/ppermute | solution.py:198
  24.1 12.6 %collective-permute-start.8 = (f32[512,256]{1,0:T(8,128)S(1)}, f32[512,256]{1,0:T(8,128)S(1)}, u32[]{:S(2)}, u32[]{:S(2)}) collective-permute-start(f32[512,256]{1,0:T(8,128)S(1)} %bitcast.30), channel_id=1, source_target_pairs={{0,1},{1,0},{2,3},{3,2},{4,5},{5,4},{6,7},{7,6},{8,9},{9,8},{10,11... | collective-permute-start | bytes 1572872 | tf_op jit(solution)/shard_map/ppermute | solution.py:388
  30.7 6.0 %collective-permute-start.9 = (f32[512,256]{1,0:T(8,128)S(1)}, f32[512,256]{1,0:T(8,128)S(1)}, u32[]{:S(2)}, u32[]{:S(2)}) collective-permute-start(f32[512,256]{1,0:T(8,128)S(1)} %bitcast.34), channel_id=1, source_target_pairs={{0,1},{1,0},{2,3},{3,2},{4,5},{5,4},{6,7},{7,6},{8,9},{9,8},{10,11... | collective-permute-start | bytes 1572872 | tf_op jit(solution)/shard_map/ppermute | solution.py:388
  30.7 16.4 %collective-permute-start.7 = (f32[512,256]{1,0:T(8,128)S(1)}, f32[512,256]{1,0:T(8,128)S(1)}, u32[]{:S(2)}, u32[]{:S(2)}) collective-permute-start(f32[512,256]{1,0:T(8,128)S(1)} %bitcast.35), channel_id=1, source_target_pairs={{0,15},{1,14},{2,1},{3,0},{4,2},{5,3},{6,4},{7,5},{8,6},{9,7},{10,... | collective-permute-start | bytes 1572872 | tf_op jit(solution)/shard_map/ppermute | solution.py:386
  36.6 15.2 %collective-permute-start.10 = (f32[512,256]{1,0:T(8,128)S(1)}, f32[512,256]{1,0:T(8,128)S(1)}, u32[]{:S(2)}, u32[]{:S(2)}) collective-permute-start(f32[512,256]{1,0:T(8,128)S(1)} %bitcast.36), channel_id=1, source_target_pairs={{0,2},{2,4},{4,6},{6,8},{8,10},{10,12},{12,14},{14,0},{1,3},{3,5},... | collective-permute-start | bytes 1572872 | tf_op jit(solution)/shard_map/ppermute | solution.py:387
  47.1 4.7 %collective-permute-start.11 = (f32[512,256]{1,0:T(8,128)S(1)}, f32[512,256]{1,0:T(8,128)S(1)}, u32[]{:S(2)}, u32[]{:S(2)}) collective-permute-start(f32[512,256]{1,0:T(8,128)S(1)} %collective-permute-done.7.refs_8_.refs_4_), channel_id=1, source_target_pairs={{0,1},{1,0},{2,3},{3,2},{4,5},{5,4},{6,7},{7,6},{8,9},{9,8},{10,11... | collective-permute-start | bytes 1572872 | tf_op jit(solution)/shard_map/ppermute | solution.py:392
  47.1 35.0 %collective-permute-start.13 = (f32[512,256]{1,0:T(8,128)S(1)}, f32[512,256]{1,0:T(8,128)S(1)}, u32[]{:S(2)}, u32[]{:S(2)}) collective-permute-start(f32[512,256]{1,0:T(8,128)S(1)} %collective-permute-done.5.refs_7_.refs_3_), channel_id=1, source_target_pairs={{0,1},{1,0},{2,3},{3,2},{4,5},{5,4},{6,7},{7,6},{8,9},{9,8},{10,11... | collective-permute-start | bytes 1572872 | tf_op jit(solution)/shard_map/ppermute | solution.py:392
  47.6 34.5 %collective-permute-start.14 = (f32[512,256]{1,0:T(8,128)S(1)}, f32[512,256]{1,0:T(8,128)}, u32[]{:S(2)}, u32[]{:S(2)}) collective-permute-start(f32[512,256]{1,0:T(8,128)S(1)} %collective-permute-done.5.refs_7_.refs_3_), channel_id=1, source_target_pairs={{0,14},{2,0},{4,2},{6,4},{8,6},{10,8},{12,10},{14,12},{1,15},{3,1}... | collective-permute-start | bytes 1572872 | tf_op jit(solution)/shard_map/ppermute | solution.py:409
  50.8 31.4 %collective-permute-start.6 = (f32[512,256]{1,0:T(8,128)S(1)}, f32[512,256]{1,0:T(8,128)}, u32[]{:S(2)}, u32[]{:S(2)}) collective-permute-start(f32[512,256]{1,0:T(8,128)S(1)} %collective-permute-done.4.refs_5_.refs_9_), channel_id=1, source_target_pairs={{0,2},{2,4},{4,6},{6,8},{8,10},{10,12},{12,14},{14,0},{1,3},{3,5},... | collective-permute-start | bytes 1572872 | tf_op jit(solution)/shard_map/ppermute | solution.py:408
  54.8 27.3 %collective-permute-start.12 = (f32[512,256]{1,0:T(8,128)S(1)}, f32[512,256]{1,0:T(8,128)}, u32[]{:S(2)}, u32[]{:S(2)}) collective-permute-start(f32[512,256]{1,0:T(8,128)S(1)} %collective-permute-done.10.refs_6_.refs_10_), channel_id=1, source_target_pairs={{0,2},{2,4},{4,6},{6,8},{8,10},{10,12},{12,14},{14,0},{1,3},{3,5},... | collective-permute-start | bytes 1572872 | tf_op jit(solution)/shard_map/ppermute | solution.py:408
  54.8 27.3 %collective-permute-start.15 = (f32[512,256]{1,0:T(8,128)S(1)}, f32[512,256]{1,0:T(8,128)}, u32[]{:S(2)}, u32[]{:S(2)}) collective-permute-start(f32[512,256]{1,0:T(8,128)S(1)} %collective-permute-done.7.refs_8_.refs_4_), channel_id=1, source_target_pairs={{0,14},{2,0},{4,2},{6,4},{8,6},{10,8},{12,10},{14,12},{1,15},{3,1}... | collective-permute-start | bytes 1572872 | tf_op jit(solution)/shard_map/ppermute | solution.py:409
  86.6 20.7 %all-to-all-start.1 = ((f32[16,128,128]{2,1,0:T(8,128)}), f32[16,128,128]{2,1,0:T(8,128)S(1)}, u32[]{:S(2)}, u32[]{:S(2)}) async-start(f32[16,128,128]{2,1,0:T(8,128)} %shard_map.54), calls=%async_computation.1 | async-start | bytes 2097152 | tf_op jit(solution)/shard_map/all_to_all | solution.py:321
  91.6 17.1 %collective-permute-start.17 = (f32[136,128]{1,0:T(8,128)S(1)}, f32[136,128]{1,0:T(8,128)S(1)}, u32[]{:S(2)}, u32[]{:S(2)}) collective-permute-start(f32[136,128]{1,0:T(8,128)S(1)} %get-tuple-element.63.refs_11_.refs_3_), channel_id=1, source_target_pairs={{0,16},{16,0},{1,17},{17,1},{2,18},{18,2},{3,19},{19,3},{4,20},{20... | collective-permute-start | bytes 208904 | tf_op jit(solution)/shard_map/ppermute | solution.py:423
  107.4 4.4 %collective-permute-start.16 = (f32[128,128]{1,0:T(8,128)S(1)}, f32[128,128]{1,0:T(8,128)S(1)}, u32[]{:S(2)}, u32[]{:S(2)}) collective-permute-start(f32[128,128]{1,0:T(8,128)S(1)} %shard_map.55.refs_1_), channel_id=1, source_target_pairs={{0,16},{16,0},{1,17},{17,1},{2,18},{18,2},{3,19},{19,3},{4,20},{20... | collective-permute-start | bytes 196616 | tf_op jit(solution)/shard_map/ppermute | solution.py:425
  112.5 11.1 %collective-permute-start.18 = (f32[128,256]{1,0:T(8,128)S(1)}, f32[128,256]{1,0:T(8,128)S(1)}, u32[]{:S(2)}, u32[]{:S(2)}) collective-permute-start(f32[128,256]{1,0:T(8,128)S(1)} %get-tuple-element.49), channel_id=1, source_target_pairs={{0,44},{1,2},{2,78},{3,37},{4,96},{5,71},{6,130},{7,105},{8,164},{... | collective-permute-start | bytes 393224 | tf_op jit(solution)/shard_map/ppermute | solution.py:429
  114.4 9.4 %collective-permute-start.19 = (f32[128,256]{1,0:T(8,128)S(1)}, f32[128,256]{1,0:T(8,128)S(1)}, u32[]{:S(2)}, u32[]{:S(2)}) collective-permute-start(f32[128,256]{1,0:T(8,128)S(1)} %get-tuple-element.50), channel_id=1, source_target_pairs={{0,3},{1,45},{2,36},{3,79},{4,70},{5,97},{6,104},{7,131},{8,138},{... | collective-permute-start | bytes 393224 | tf_op jit(solution)/shard_map/ppermute | solution.py:429

commit v6 on v4

--- a/solution.py
+++ b/solution.py
@@ -256,16 +256,29 @@
     square[3, :128, :] = diagonal[:128, 128:]
 
 
+def near_products(mine, refs):
+    held, beside, last, own = [split(ref[...]) for ref in refs]
+    return (2 * mine, dot(own, held)), (2 * (1 - mine), dot(own, beside)), (8, dot(last, own))
+
+
 def near_kernel(spot, *refs):
     *arrays, square, out = refs
-    mine = spot[CORE]
-    held, beside, last, own = [whole(arrays[k : k + 2]) for k in range(0, 8, 2)]
     out[:, 128:, :] = jnp.zeros((16, 8, 128), jnp.float32)
-    lay(out, 2 * mine, dot(own, held))
-    lay(out, 2 * (1 - mine), dot(own, beside))
-    lay(out, 8, dot(last, own))
+    for at, block in near_products(spot[CORE], arrays):
+        lay(out, at, block)
     out[10:12] = square[:2]
     out[14:16] = square[2:]
+
+
+def more_kernel(spot, *refs):
+    *arrays, part, out = refs
+    out[...] = part[...]
+    for at, block in near_products(spot[CORE], arrays):
+        for i in range(2):
+            for j in range(2):
+                place = at + 4 * i + j
+                piece = block[i * 128 : i * 128 + 128, j * 128 : j * 128 + 128]
+                out[place, :128, :] = part[place, :128, :] + piece
 
 
 def far_kernel(spot, *refs):
@@ -388,24 +401,36 @@
     held_other = [lax.ppermute(half, "core", SWAP) for half in held]
     square = call(square_kernel, array(4, 136, 128), [], [spot], *held, *held_other)
     sure = links[0, 0, 0] >= 0
-    next_1[1], last_1[1], square, sure = lax.optimization_barrier(
-        (next_1[1], last_1[1], square, sure)
-    )
-    near = call(
+    part = call(
         near_kernel,
         array(16, 136, 128),
         [],
         [spot],
-        *held,
-        *held_other,
-        *last_1,
-        *next_1,
+        held[0],
+        held_other[0],
+        last_1[0],
+        next_1[0],
         square,
+    )
+    next_1[1], part, sure = lax.optimization_barrier((next_1[1], part, sure))
+    next_other = [lax.ppermute(half, "core", SWAP) for half in next_1]
+    next_1[1], last_1[1], part, next_other[1] = lax.optimization_barrier(
+        (next_1[1], last_1[1], part, next_other[1])
+    )
+    near = call(
+        more_kernel,
+        array(16, 136, 128),
+        [],
+        [spot],
+        held[1],
+        held_other[1],
+        last_1[1],
+        next_1[1],
+        part,
     )
     next_1[1], last_1[1], near = lax.optimization_barrier((next_1[1], last_1[1], near))
     last_2 = [lax.ppermute(half, "z", UP) for half in last_1]
     next_2 = [lax.ppermute(half, "z", DOWN) for half in next_1]
-    next_other = [lax.ppermute(half, "core", SWAP) for half in next_1]
     near = lax.cond(sure, gathered, lambda blocks: blocks[0], near)
     far = call(
         far_kernel,

time: 129 us -> 127 us (0.984)
  waiting for transfers between devices: 43.6 us -> 41.6 us
  blocking collectives: 25.4 us -> 24 us
    ppermute x1, waiting for transfers between devices: 3.73 us -> 0.99 us  [body(): last_1 = [early[0], lax.ppermute(held[1], 'z', UP)]]
    all_to_all x1, blocking collectives: 25.4 us -> 24 us  [gathered(): blocks = lax.all_to_all(blocks, PLANE, 0, 0, tiled=True)]
    pallas_call x8 -> x9, Pallas kernels: 14.1 us -> 14.9 us  [call(): pl.pallas_call(ordered, out_shape=shape, in_specs=[SMEM] * len(scalars) +...]
  transfers between devices with their start and end apart: 21 -> 21, of which waited for: 10 -> 10; matrix products, arithmetic and copies ran while one was open for 2% -> 2% of each run, Pallas kernels for 7% -> 8%
where the time goes in v6:
time: 127 us; the launch traced here: 124 us
  waiting for transfers between devices  41.6 us (33%)
  starting transfers between devices  36.7 us (29%)
  blocking collectives  24 us (19%)
  Pallas kernels  14.9 us (12%)
  local copies, waits for them, and re-layouts  3.56 us (3%)
  other arithmetic  2 us (2%)
  between operations  1.5 us (1%)
    all_to_all x1, blocking collectives, gathered(): blocks = lax.all_to_all(blocks, PLANE, 0, 0, tiled=True)  24 us
    all_to_all x1, waiting for transfers between devices, gathered(): blocks = lax.all_to_all(blocks, PLANE, 0, 0, tiled=True)  15.4 us
    pallas_call x9, Pallas kernels, call(): pl.pallas_call(ordered, out_shape=shape, in_specs=[SMEM] * len(scalars) +...  14.9 us
    ppermute x1, waiting for transfers between devices, body(): next_1 = [early[1], lax.ppermute(held[1], ('z', 'core'), DOWN_TURNED)]  7.59 us
    ppermute x2, starting transfers between devices, body(): next_2 = [lax.ppermute(half, 'z', DOWN) for half in next_1]  6.38 us
    ppermute x2, waiting for transfers between devices, body(): got = [lax.ppermute(sent[k], ALL, routes(k)) for k in range(2)]  6.19 us
    ppermute x2, starting transfers between devices, body(): got = [lax.ppermute(sent[k], ALL, routes(k)) for k in range(2)]  5.36 us
    all_to_all x1, starting transfers between devices, gathered(): blocks = lax.all_to_all(blocks, PLANE, 0, 0, tiled=True)  4.97 us
  transfers between devices with their start and end apart: 21, of which 10 were waited for; matrix products, arithmetic and copies ran while one was open for 2% of the time, Pallas kernels for 8%

profile of v6, /device:TPU:2, one launch (start us, length us, event | category | flops | bytes accessed | tf_op | source)
XLA Modules:
  0.0 124.1 jit_solution(10164481409742209972)
XLA Ops:
  0.6 0.0 copy-start.2
  0.6 0.0 copy-start.3
  0.7 1.2 fusion
  1.8 2.4 %collective-permute-start = (f32[4,64,256]{2,1,0:T(8,128)S(1)}, f32[4,64,256]{2,1,0:T(8,128)S(1)}, u32[]{:S(2)}, u32[]{:S(2)}) collective-permute-start(f32[4,64,256]{2,1,0:T(8,128)S(1)} %fusion), channel_id=1, source_target_pairs={{0,16},{16,0},{1,17},{17,1},{2,18},{18,2},{3,19},{19,3},{4,20},{20... | collective-permute-start | bytes 786440 | tf_op jit(solution)/shard_map/ppermute | solution.py:169
  4.2 1.1 slice_bitcast_fusion.1
  5.3 2.6 %collective-permute-start.1 = (f32[4,64,256]{2,1,0:T(8,128)S(1)}, f32[4,64,256]{2,1,0:T(8,128)S(1)}, u32[]{:S(2)}, u32[]{:S(2)}) collective-permute-start(f32[4,64,256]{2,1,0:T(8,128)S(1)} %get-tuple-element.52), channel_id=1, source_target_pairs={{0,32},{32,64},{64,96},{96,128},{128,160},{160,192},{192,224},{1,3... | collective-permute-start | bytes 786440 | tf_op jit(solution)/shard_map/ppermute | solution.py:170
  7.9 1.3 %collective-permute-start.2 = (f32[4,64,256]{2,1,0:T(8,128)S(1)}, f32[4,64,256]{2,1,0:T(8,128)S(1)}, u32[]{:S(2)}, u32[]{:S(2)}) collective-permute-start(f32[4,64,256]{2,1,0:T(8,128)S(1)} %get-tuple-element.51), channel_id=1, source_target_pairs={{32,0},{64,32},{96,64},{128,96},{160,128},{192,160},{224,192},{33,... | collective-permute-start | bytes 786440 | tf_op jit(solution)/shard_map/ppermute | solution.py:171
  9.2 0.1 copy.7
  9.3 0.1 select_reduce_fusion
  9.4 0.1 reshape.25.refs_1_
  9.5 0.1 stack.29.refs_0_
  9.6 0.5 collective-permute-done.refs_3_.refs_5_
  10.1 1.7 %copy-done = f32[4,4,9,4096]{3,1,2,0:T(4,128)S(1)} copy-done((f32[4,4,9,4096]{3,1,2,0:T(4,128)S(1)}, f32[4,4,9,4096]{3,1,2,0:T(4,128)}, u32[]{:S(2)}) %copy-start) | copy-done | bytes 2359320
  11.7 2.0 %shard_map.50 = (f32[8,64,256]{2,1,0:T(8,128)S(1)}, f32[8,64,256]{2,1,0:T(8,128)S(1)}) custom-call(s32[5]{0:T(128)S(1)} %stack.29.refs_0_, s32[144]{0:T(256)S(1)} %reshape.25.refs_1_, f32[16,64,256]{2,1,0:T(8,128)S(1)} %bitcast.33, f32[4,64,256]{2,1,0:T(8,128)S(1)} %collective-permute-done.refs_3_.refs_5_, f32[4,9,4,4096]{3,2,1,0:T(4,128)S(1)} %bitcast.26), custom_call_target="tpu_custom_call" | custom-call | flops 1 | bytes 1 | tf_op jit(solution)/shard_map/pallas_call | solution.py:40
  13.8 2.0 %collective-permute-start.4 = (f32[512,256]{1,0:T(8,128)S(1)}, f32[512,256]{1,0:T(8,128)S(1)}, u32[]{:S(2)}, u32[]{:S(2)}) collective-permute-start(f32[512,256]{1,0:T(8,128)S(1)} %bitcast.28), channel_id=1, source_target_pairs={{0,2},{2,4},{4,6},{6,8},{8,10},{10,12},{12,14},{14,0},{1,3},{3,5},... | collective-permute-start | bytes 1572872 | tf_op jit(solution)/shard_map/ppermute | solution.py:193
  15.8 2.5 %collective-permute-start.5 = (f32[512,256]{1,0:T(8,128)S(1)}, f32[512,256]{1,0:T(8,128)S(1)}, u32[]{:S(2)}, u32[]{:S(2)}) collective-permute-start(f32[512,256]{1,0:T(8,128)S(1)} %bitcast.29), channel_id=1, source_target_pairs={{0,15},{1,14},{2,1},{3,0},{4,2},{5,3},{6,4},{7,5},{8,6},{9,7},{10,... | collective-permute-start | bytes 1572872 | tf_op jit(solution)/shard_map/ppermute | solution.py:193
  18.3 0.0 collective-permute-done.1.refs_3_
  18.3 3.9 %collective-permute-done.2.refs_4_ = f32[4,64,256]{2,1,0:T(8,128)S(1)} collective-permute-done((f32[4,64,256]{2,1,0:T(8,128)S(1)}, f32[4,64,256]{2,1,0:T(8,128)S(1)}, u32[]{:S(2)}, u32[]{:S(2)}) %collective-permute-start.2) | collective-permute-done | bytes 262176 | tf_op jit(solution)/shard_map/ppermute | solution.py:171
  22.2 1.9 %collective-permute-start.3 = (f32[2,64,256]{2,1,0:T(8,128)S(1)}, f32[2,64,256]{2,1,0:T(8,128)S(1)}, u32[]{:S(2)}, u32[]{:S(2)}) collective-permute-start(f32[2,64,256]{2,1,0:T(8,128)S(1)} %maximum_select_fusion), channel_id=1, source_target_pairs={{0,16},{16,0},{1,17},{17,1},{2,18},{18,2},{3,19},{19,3},{4,20},{20... | collective-permute-start | bytes 393224 | tf_op jit(solution)/shard_map/ppermute | solution.py:198
  24.1 0.0 collective-permute-start.8
  24.1 3.2 %collective-permute-done.3.refs_6_ = f32[2,64,256]{2,1,0:T(8,128)S(1)} collective-permute-done((f32[2,64,256]{2,1,0:T(8,128)S(1)}, f32[2,64,256]{2,1,0:T(8,128)S(1)}, u32[]{:S(2)}, u32[]{:S(2)}) %collective-permute-start.3) | collective-permute-done | bytes 131104 | tf_op jit(solution)/shard_map/ppermute | solution.py:198
  27.2 2.2 %shard_map.51 = (f32[8,64,256]{2,1,0:T(8,128)S(1)}, f32[16,64,256]{2,1,0:T(8,128)}) custom-call(s32[5]{0:T(128)S(1)} %stack.29.refs_0_, s32[144]{0:T(256)S(1)} %reshape.25.refs_1_, f32[8,64,256]{2,1,0:T(8,128)S(1)} %get-tuple-element.29.refs_2_, f32[4,64,256]{2,1,0:T(8,128)S(1)} %collective-permute-done.1.refs_3_, ...), custom_call_target="tpu_custom_call" | custom-call | flops 1 | bytes 1 | tf_op jit(solution)/shard_map/pallas_call | solution.py:40
  29.4 1.2 collective-permute-done.4.refs_3_.refs_9_
  30.6 0.0 collective-permute-done.5.refs_4_.refs_3_
  30.7 0.0 collective-permute-start.9
  30.7 4.7 %collective-permute-start.7 = (f32[512,256]{1,0:T(8,128)S(1)}, f32[512,256]{1,0:T(8,128)S(1)}, u32[]{:S(2)}, u32[]{:S(2)}) collective-permute-start(f32[512,256]{1,0:T(8,128)S(1)} %bitcast.35), channel_id=1, source_target_pairs={{0,15},{1,14},{2,1},{3,0},{4,2},{5,3},{6,4},{7,5},{8,6},{9,7},{10,... | collective-permute-start | bytes 1572872 | tf_op jit(solution)/shard_map/ppermute | solution.py:399
  35.4 0.5 slice.54
  36.6 0.1 collective-permute-start.10
  36.7 0.0 collective-permute-done.8.refs_3_.refs_2_
  36.7 0.0 collective-permute-done.9.refs_4_.refs_2_
  36.7 1.4 %shard_map.52.refs_5_ = f32[4,136,128]{2,1,0:T(8,128)S(1)} custom-call(s32[5]{0:T(128)S(1)} %stack.29.refs_0_, f32[512,256]{1,0:T(8,128)S(1)} %bitcast.31, f32[512,256]{1,0:T(8,128)S(1)} %bitcast.37, f32[512,256]{1,0:T(8,128)S(1)} %collective-permute-done.8.refs_3_.refs_2_, f32[512,256]{1,0:T(8,128)S(1)} %collective-permute-done.9.refs_4_.refs_2_), custom_call_target="tpu_custom_call" | custom-call | flops 1 | bytes 1 | tf_op jit(solution)/shard_map/pallas_call | solution.py:40
  38.1 1.4 %shard_map.53.refs_5_ = f32[16,136,128]{2,1,0:T(8,128)S(1)} custom-call(s32[5]{0:T(128)S(1)} %stack.29.refs_0_, f32[512,256]{1,0:T(8,128)S(1)} %bitcast.32, f32[512,256]{1,0:T(8,128)S(1)} %collective-permute-done.8.refs_3_.refs_2_, f32[512,256]{1,0:T(8,128)S(1)} %collective-permute-done.4.refs_3_.refs_9_, ...), custom_call_target="tpu_custom_call" | custom-call | flops 1 | bytes 1 | tf_op jit(solution)/shard_map/pallas_call | solution.py:40
  39.5 7.6 %collective-permute-done.7.refs_4_ = f32[512,256]{1,0:T(8,128)S(1)} collective-permute-done((f32[512,256]{1,0:T(8,128)S(1)}, f32[512,256]{1,0:T(8,128)S(1)}, u32[]{:S(2)}, u32[]{:S(2)}) %collective-permute-start.7) | collective-permute-done | bytes 524320 | tf_op jit(solution)/shard_map/ppermute | solution.py:399
  47.1 0.0 collective-permute-start.11
  47.1 0.5 collective-permute-start.13
  47.6 3.2 %collective-permute-start.14 = (f32[512,256]{1,0:T(8,128)S(1)}, f32[512,256]{1,0:T(8,128)}, u32[]{:S(2)}, u32[]{:S(2)}) collective-permute-start(f32[512,256]{1,0:T(8,128)S(1)} %collective-permute-done.5.refs_4_.refs_3_), channel_id=1, source_target_pairs={{0,14},{2,0},{4,2},{6,4},{8,6},{10,8},{12,10},{14,12},{1,15},{3,1}... | collective-permute-start | bytes 1572872 | tf_op jit(solution)/shard_map/ppermute | solution.py:433
  50.8 0.0 collective-permute-start.6
  50.8 1.0 collective-permute-done.10.refs_3_.refs_10_
  51.8 0.0 collective-permute-done.11.refs_6_
  51.8 2.4 %shard_map.54 = f32[16,136,128]{2,1,0:T(8,128)} custom-call(s32[5]{0:T(128)S(1)} %stack.29.refs_0_, f32[512,256]{1,0:T(8,128)S(1)} %bitcast.38, f32[512,256]{1,0:T(8,128)S(1)} %collective-permute-done.9.refs_4_.refs_2_, f32[512,256]{1,0:T(8,128)S(1)} %collective-permute-done.10.refs_3_.refs_10_, f32[512,256]{1,0:T(8,128)S(1)} %collective-permute-done.7.refs_4_, ...), custom_call_target="tpu_custom_call" | custom-call | flops 1 | bytes 1 | tf_op jit(solution)/shard_map/pallas_call | solution.py:40
  54.2 0.0 collective-permute-start.12
  54.2 3.2 %collective-permute-start.15 = (f32[512,256]{1,0:T(8,128)S(1)}, f32[512,256]{1,0:T(8,128)}, u32[]{:S(2)}, u32[]{:S(2)}) collective-permute-start(f32[512,256]{1,0:T(8,128)S(1)} %collective-permute-done.7.refs_4_), channel_id=1, source_target_pairs={{0,14},{2,0},{4,2},{6,4},{8,6},{10,8},{12,10},{14,12},{1,15},{3,1}... | collective-permute-start | bytes 1572872 | tf_op jit(solution)/shard_map/ppermute | solution.py:433
  57.4 24.0 %conditional.1 = (f32[136,128]{1,0:T(8,128)S(1)}) conditional(s32[]{:T(128)} %convert_element_type.3, f32[16,136,128]{2,1,0:T(8,128)} %shard_map.54, f32[16,136,128]{2,1,0:T(8,128)} %shard_map.54), branch_computations={%region_1.2_spmd, %region_2.3_spmd} | conditional | flops 1 | bytes 2228233 | solution.py:434
  57.4 24.0 %all_to_all.9.refs_0_ = f32[16,136,128]{2,1,0:T(8,128)S(1)} all-to-all(f32[16,136,128]{2,1,0:T(8,128)} %param.1), channel_id=1, replica_groups=mesh['y'=4,'xh'=2,'xl'=2,'z'=8,'core'=2] {'y','xh','xl'}, dimensions={0} | all-to-all | bytes 2228224 | tf_op jit(solution)/shard_map/cond/branch_1_fun/all_to_all | solution.py:334
  81.4 0.1 branch_1_fun.1
  81.5 0.0 collective-permute-done.13.refs_5_
  81.5 0.0 collective-permute-done.14.refs_7_
  81.5 0.0 collective-permute-done.6.refs_1_
  81.5 0.0 collective-permute-done.12.refs_2_
  81.5 0.0 collective-permute-done.15.refs_8_
  81.5 4.5 %shard_map.55 = f32[16,128,128]{2,1,0:T(8,128)} custom-call(s32[5]{0:T(128)S(1)} %stack.29.refs_0_, f32[512,256]{1,0:T(8,128)} %collective-permute-done.6.refs_1_, f32[512,256]{1,0:T(8,128)} %collective-permute-done.12.refs_2_, f32[512,256]{1,0:T(8,128)S(1)} %collective-permute-done.5.refs_4_.refs_3_, f32[512,256]{1,0:T(8,128)S(1)} %collective-permute-done.7.refs_4_, ...), custom_call_target="tpu_custom_call" | custom-call | flops 1 | bytes 1 | tf_op jit(solution)/shard_map/pallas_call | solution.py:40
  86.0 5.0 %all-to-all-start.1 = ((f32[16,128,128]{2,1,0:T(8,128)}), f32[16,128,128]{2,1,0:T(8,128)S(1)}, u32[]{:S(2)}, u32[]{:S(2)}) async-start(f32[16,128,128]{2,1,0:T(8,128)} %shard_map.55), calls=%async_computation.1 | async-start | bytes 2097152 | tf_op jit(solution)/shard_map/all_to_all | solution.py:334
  91.0 0.3 collective-permute-start.17
  91.3 15.4 %all-to-all-done.1.refs_0_ = f32[16,128,128]{2,1,0:T(8,128)S(1)} async-done(((f32[16,128,128]{2,1,0:T(8,128)}), f32[16,128,128]{2,1,0:T(8,128)S(1)}, u32[]{:S(2)}, u32[]{:S(2)}) %all-to-all-start.1) | async-done | bytes 1048608 | tf_op jit(solution)/shard_map/all_to_all | solution.py:334
  106.6 0.1 shard_map.56.refs_1_
  106.7 1.7 %collective-permute-start.16 = (f32[128,128]{1,0:T(8,128)S(1)}, f32[128,128]{1,0:T(8,128)S(1)}, u32[]{:S(2)}, u32[]{:S(2)}) collective-permute-start(f32[128,128]{1,0:T(8,128)S(1)} %shard_map.56.refs_1_), channel_id=1, source_target_pairs={{0,16},{16,0},{1,17},{17,1},{2,18},{18,2},{3,19},{19,3},{4,20},{20... | collective-permute-start | bytes 196616 | tf_op jit(solution)/shard_map/ppermute | solution.py:449
  108.4 0.0 collective-permute-done.17.refs_4_
  108.4 2.7 %collective-permute-done.16.refs_2_ = f32[128,128]{1,0:T(8,128)S(1)} collective-permute-done((f32[128,128]{1,0:T(8,128)S(1)}, f32[128,128]{1,0:T(8,128)S(1)}, u32[]{:S(2)}, u32[]{:S(2)}) %collective-permute-start.16) | collective-permute-done | bytes 65568 | tf_op jit(solution)/shard_map/ppermute | solution.py:449
  111.0 0.8 shard_map.57
  111.8 1.9 %collective-permute-start.18 = (f32[128,256]{1,0:T(8,128)S(1)}, f32[128,256]{1,0:T(8,128)S(1)}, u32[]{:S(2)}, u32[]{:S(2)}) collective-permute-start(f32[128,256]{1,0:T(8,128)S(1)} %get-tuple-element.49), channel_id=1, source_target_pairs={{0,44},{1,2},{2,78},{3,37},{4,96},{5,71},{6,130},{7,105},{8,164},{... | collective-permute-start | bytes 393224 | tf_op jit(solution)/shard_map/ppermute | solution.py:453
  113.8 3.4 %collective-permute-start.19 = (f32[128,256]{1,0:T(8,128)S(1)}, f32[128,256]{1,0:T(8,128)S(1)}, u32[]{:S(2)}, u32[]{:S(2)}) collective-permute-start(f32[128,256]{1,0:T(8,128)S(1)} %get-tuple-element.50), channel_id=1, source_target_pairs={{0,3},{1,45},{2,36},{3,79},{4,70},{5,97},{6,104},{7,131},{8,138},{... | collective-permute-start | bytes 393224 | tf_op jit(solution)/shard_map/ppermute | solution.py:453
  117.2 5.8 %collective-permute-done.18 = f32[128,256]{1,0:T(8,128)S(1)} collective-permute-done((f32[128,256]{1,0:T(8,128)S(1)}, f32[128,256]{1,0:T(8,128)S(1)}, u32[]{:S(2)}, u32[]{:S(2)}) %collective-permute-start.18) | collective-permute-done | bytes 131104 | tf_op jit(solution)/shard_map/ppermute | solution.py:453
  123.0 0.4 collective-permute-done.19
  123.4 0.7 maximum_multiply_fusion
  (8 shorter events, 0.1 us)
Async XLA Ops:
  0.6 9.4 %copy-start.2 = (f32[4,4,64,256]{3,2,1,0:T(8,128)S(1)}, f32[4,4,64,256]{3,2,1,0:T(8,128)}, u32[]{:S(2)}) copy-start(f32[4,4,64,256]{3,2,1,0:T(8,128)} %param.5) | copy-start | bytes 3145732
  0.6 8.6 %copy-start.3 = (s32[4,4,9]{2,1,0:T(4,128)S(1)}, s32[4,4,9]{2,1,0:T(4,128)}, u32[]{:S(2)}) copy-start(s32[4,4,9]{2,1,0:T(4,128)} %param.6) | copy-start | bytes 1732
  1.8 8.3 %collective-permute-start = (f32[4,64,256]{2,1,0:T(8,128)S(1)}, f32[4,64,256]{2,1,0:T(8,128)S(1)}, u32[]{:S(2)}, u32[]{:S(2)}) collective-permute-start(f32[4,64,256]{2,1,0:T(8,128)S(1)} %fusion), channel_id=1, source_target_pairs={{0,16},{16,0},{1,17},{17,1},{2,18},{18,2},{3,19},{19,3},{4,20},{20... | collective-permute-start | bytes 786440 | tf_op jit(solution)/shard_map/ppermute | solution.py:169
  5.3 13.0 %collective-permute-start.1 = (f32[4,64,256]{2,1,0:T(8,128)S(1)}, f32[4,64,256]{2,1,0:T(8,128)S(1)}, u32[]{:S(2)}, u32[]{:S(2)}) collective-permute-start(f32[4,64,256]{2,1,0:T(8,128)S(1)} %get-tuple-element.52), channel_id=1, source_target_pairs={{0,32},{32,64},{64,96},{96,128},{128,160},{160,192},{192,224},{1,3... | collective-permute-start | bytes 786440 | tf_op jit(solution)/shard_map/ppermute | solution.py:170
  7.9 14.2 %collective-permute-start.2 = (f32[4,64,256]{2,1,0:T(8,128)S(1)}, f32[4,64,256]{2,1,0:T(8,128)S(1)}, u32[]{:S(2)}, u32[]{:S(2)}) collective-permute-start(f32[4,64,256]{2,1,0:T(8,128)S(1)} %get-tuple-element.51), channel_id=1, source_target_pairs={{32,0},{64,32},{96,64},{128,96},{160,128},{192,160},{224,192},{33,... | collective-permute-start | bytes 786440 | tf_op jit(solution)/shard_map/ppermute | solution.py:171
  10.1 1.7 %copy-start = (f32[4,4,9,4096]{3,1,2,0:T(4,128)S(1)}, f32[4,4,9,4096]{3,1,2,0:T(4,128)}, u32[]{:S(2)}) copy-start(f32[4,4,9,4096]{3,1,2,0:T(4,128)} %param.7) | copy-start | bytes 7077892
  11.7 15.5 %copy-start.1 = (f32[4,4,9,4096]{3,1,2,0:T(4,128)S(1)}, f32[4,4,9,4096]{3,1,2,0:T(4,128)}, u32[]{:S(2)}) copy-start(f32[4,4,9,4096]{3,1,2,0:T(4,128)} %param.7) | copy-start | bytes 7077892
  13.8 16.9 %collective-permute-start.4 = (f32[512,256]{1,0:T(8,128)S(1)}, f32[512,256]{1,0:T(8,128)S(1)}, u32[]{:S(2)}, u32[]{:S(2)}) collective-permute-start(f32[512,256]{1,0:T(8,128)S(1)} %bitcast.28), channel_id=1, source_target_pairs={{0,2},{2,4},{4,6},{6,8},{8,10},{10,12},{12,14},{14,0},{1,3},{3,5},... | collective-permute-start | bytes 1572872 | tf_op jit(solution)/shard_map/ppermute | solution.py:193
  15.8 14.9 %collective-permute-start.5 = (f32[512,256]{1,0:T(8,128)S(1)}, f32[512,256]{1,0:T(8,128)S(1)}, u32[]{:S(2)}, u32[]{:S(2)}) collective-permute-start(f32[512,256]{1,0:T(8,128)S(1)} %bitcast.29), channel_id=1, source_target_pairs={{0,15},{1,14},{2,1},{3,0},{4,2},{5,3},{6,4},{7,5},{8,6},{9,7},{10,... | collective-permute-start | bytes 1572872 | tf_op jit(solution)/shard_map/ppermute | solution.py:193
  22.2 5.1 %collective-permute-start.3 = (f32[2,64,256]{2,1,0:T(8,128)S(1)}, f32[2,64,256]{2,1,0:T(8,128)S(1)}, u32[]{:S(2)}, u32[]{:S(2)}) collective-permute-start(f32[2,64,256]{2,1,0:T(8,128)S(1)} %maximum_select_fusion), channel_id=1, source_target_pairs={{0,16},{16,0},{1,17},{17,1},{2,18},{18,2},{3,19},{19,3},{4,20},{20... | collective-permute-start | bytes 393224 | tf_op jit(solution)/shard_map/ppermute | solution.py:198
  24.1 12.6 %collective-permute-start.8 = (f32[512,256]{1,0:T(8,128)S(1)}, f32[512,256]{1,0:T(8,128)S(1)}, u32[]{:S(2)}, u32[]{:S(2)}) collective-permute-start(f32[512,256]{1,0:T(8,128)S(1)} %bitcast.30), channel_id=1, source_target_pairs={{0,1},{1,0},{2,3},{3,2},{4,5},{5,4},{6,7},{7,6},{8,9},{9,8},{10,11... | collective-permute-start | bytes 1572872 | tf_op jit(solution)/shard_map/ppermute | solution.py:401
  30.7 6.0 %collective-permute-start.9 = (f32[512,256]{1,0:T(8,128)S(1)}, f32[512,256]{1,0:T(8,128)S(1)}, u32[]{:S(2)}, u32[]{:S(2)}) collective-permute-start(f32[512,256]{1,0:T(8,128)S(1)} %bitcast.34), channel_id=1, source_target_pairs={{0,1},{1,0},{2,3},{3,2},{4,5},{5,4},{6,7},{7,6},{8,9},{9,8},{10,11... | collective-permute-start | bytes 1572872 | tf_op jit(solution)/shard_map/ppermute | solution.py:401
  30.7 16.4 %collective-permute-start.7 = (f32[512,256]{1,0:T(8,128)S(1)}, f32[512,256]{1,0:T(8,128)S(1)}, u32[]{:S(2)}, u32[]{:S(2)}) collective-permute-start(f32[512,256]{1,0:T(8,128)S(1)} %bitcast.35), channel_id=1, source_target_pairs={{0,15},{1,14},{2,1},{3,0},{4,2},{5,3},{6,4},{7,5},{8,6},{9,7},{10,... | collective-permute-start | bytes 1572872 | tf_op jit(solution)/shard_map/ppermute | solution.py:399
  36.6 15.2 %collective-permute-start.10 = (f32[512,256]{1,0:T(8,128)S(1)}, f32[512,256]{1,0:T(8,128)S(1)}, u32[]{:S(2)}, u32[]{:S(2)}) collective-permute-start(f32[512,256]{1,0:T(8,128)S(1)} %bitcast.36), channel_id=1, source_target_pairs={{0,2},{2,4},{4,6},{6,8},{8,10},{10,12},{12,14},{14,0},{1,3},{3,5},... | collective-permute-start | bytes 1572872 | tf_op jit(solution)/shard_map/ppermute | solution.py:400
  47.1 4.7 %collective-permute-start.11 = (f32[512,256]{1,0:T(8,128)S(1)}, f32[512,256]{1,0:T(8,128)S(1)}, u32[]{:S(2)}, u32[]{:S(2)}) collective-permute-start(f32[512,256]{1,0:T(8,128)S(1)} %collective-permute-done.7.refs_4_), channel_id=1, source_target_pairs={{0,1},{1,0},{2,3},{3,2},{4,5},{5,4},{6,7},{7,6},{8,9},{9,8},{10,11... | collective-permute-start | bytes 1572872 | tf_op jit(solution)/shard_map/ppermute | solution.py:416
  47.1 34.4 %collective-permute-start.13 = (f32[512,256]{1,0:T(8,128)S(1)}, f32[512,256]{1,0:T(8,128)S(1)}, u32[]{:S(2)}, u32[]{:S(2)}) collective-permute-start(f32[512,256]{1,0:T(8,128)S(1)} %collective-permute-done.5.refs_4_.refs_3_), channel_id=1, source_target_pairs={{0,1},{1,0},{2,3},{3,2},{4,5},{5,4},{6,7},{7,6},{8,9},{9,8},{10,11... | collective-permute-start | bytes 1572872 | tf_op jit(solution)/shard_map/ppermute | solution.py:416
  47.6 33.9 %collective-permute-start.14 = (f32[512,256]{1,0:T(8,128)S(1)}, f32[512,256]{1,0:T(8,128)}, u32[]{:S(2)}, u32[]{:S(2)}) collective-permute-start(f32[512,256]{1,0:T(8,128)S(1)} %collective-permute-done.5.refs_4_.refs_3_), channel_id=1, source_target_pairs={{0,14},{2,0},{4,2},{6,4},{8,6},{10,8},{12,10},{14,12},{1,15},{3,1}... | collective-permute-start | bytes 1572872 | tf_op jit(solution)/shard_map/ppermute | solution.py:433
  50.8 30.7 %collective-permute-start.6 = (f32[512,256]{1,0:T(8,128)S(1)}, f32[512,256]{1,0:T(8,128)}, u32[]{:S(2)}, u32[]{:S(2)}) collective-permute-start(f32[512,256]{1,0:T(8,128)S(1)} %collective-permute-done.4.refs_3_.refs_9_), channel_id=1, source_target_pairs={{0,2},{2,4},{4,6},{6,8},{8,10},{10,12},{12,14},{14,0},{1,3},{3,5},... | collective-permute-start | bytes 1572872 | tf_op jit(solution)/shard_map/ppermute | solution.py:432
  54.2 27.3 %collective-permute-start.12 = (f32[512,256]{1,0:T(8,128)S(1)}, f32[512,256]{1,0:T(8,128)}, u32[]{:S(2)}, u32[]{:S(2)}) collective-permute-start(f32[512,256]{1,0:T(8,128)S(1)} %collective-permute-done.10.refs_3_.refs_10_), channel_id=1, source_target_pairs={{0,2},{2,4},{4,6},{6,8},{8,10},{10,12},{12,14},{14,0},{1,3},{3,5},... | collective-permute-start | bytes 1572872 | tf_op jit(solution)/shard_map/ppermute | solution.py:432
  54.2 27.3 %collective-permute-start.15 = (f32[512,256]{1,0:T(8,128)S(1)}, f32[512,256]{1,0:T(8,128)}, u32[]{:S(2)}, u32[]{:S(2)}) collective-permute-start(f32[512,256]{1,0:T(8,128)S(1)} %collective-permute-done.7.refs_4_), channel_id=1, source_target_pairs={{0,14},{2,0},{4,2},{6,4},{8,6},{10,8},{12,10},{14,12},{1,15},{3,1}... | collective-permute-start | bytes 1572872 | tf_op jit(solution)/shard_map/ppermute | solution.py:433
  86.0 20.6 %all-to-all-start.1 = ((f32[16,128,128]{2,1,0:T(8,128)}), f32[16,128,128]{2,1,0:T(8,128)S(1)}, u32[]{:S(2)}, u32[]{:S(2)}) async-start(f32[16,128,128]{2,1,0:T(8,128)} %shard_map.55), calls=%async_computation.1 | async-start | bytes 2097152 | tf_op jit(solution)/shard_map/all_to_all | solution.py:334
  91.0 17.4 %collective-permute-start.17 = (f32[136,128]{1,0:T(8,128)S(1)}, f32[136,128]{1,0:T(8,128)S(1)}, u32[]{:S(2)}, u32[]{:S(2)}) collective-permute-start(f32[136,128]{1,0:T(8,128)S(1)} %get-tuple-element.63.refs_11_.refs_3_), channel_id=1, source_target_pairs={{0,16},{16,0},{1,17},{17,1},{2,18},{18,2},{3,19},{19,3},{4,20},{20... | collective-permute-start | bytes 208904 | tf_op jit(solution)/shard_map/ppermute | solution.py:447
  106.7 4.4 %collective-permute-start.16 = (f32[128,128]{1,0:T(8,128)S(1)}, f32[128,128]{1,0:T(8,128)S(1)}, u32[]{:S(2)}, u32[]{:S(2)}) collective-permute-start(f32[128,128]{1,0:T(8,128)S(1)} %shard_map.56.refs_1_), channel_id=1, source_target_pairs={{0,16},{16,0},{1,17},{17,1},{2,18},{18,2},{3,19},{19,3},{4,20},{20... | collective-permute-start | bytes 196616 | tf_op jit(solution)/shard_map/ppermute | solution.py:449
  111.8 11.2 %collective-permute-start.18 = (f32[128,256]{1,0:T(8,128)S(1)}, f32[128,256]{1,0:T(8,128)S(1)}, u32[]{:S(2)}, u32[]{:S(2)}) collective-permute-start(f32[128,256]{1,0:T(8,128)S(1)} %get-tuple-element.49), channel_id=1, source_target_pairs={{0,44},{1,2},{2,78},{3,37},{4,96},{5,71},{6,130},{7,105},{8,164},{... | collective-permute-start | bytes 393224 | tf_op jit(solution)/shard_map/ppermute | solution.py:453
  113.8 9.6 %collective-permute-start.19 = (f32[128,256]{1,0:T(8,128)S(1)}, f32[128,256]{1,0:T(8,128)S(1)}, u32[]{:S(2)}, u32[]{:S(2)}) collective-permute-start(f32[128,256]{1,0:T(8,128)S(1)} %get-tuple-element.50), channel_id=1, source_target_pairs={{0,3},{1,45},{2,36},{3,79},{4,70},{5,97},{6,104},{7,131},{8,138},{... | collective-permute-start | bytes 393224 | tf_op jit(solution)/shard_map/ppermute | solution.py:453

commit v7 on v5

--- a/solution.py
+++ b/solution.py
@@ -220,6 +220,11 @@
     return one(left[0], right[0]) + (one(left[0], right[1]) + one(left[1], right[0]))
 
 
+def dots(left, *rights):
+    total = dot(left, tuple(jnp.concatenate(parts, 1) for parts in zip(*rights)))
+    return [total[:, k * 256 : k * 256 + 256] for k in range(len(rights))]
+
+
 def whole(pair):
     parts = [split(ref[...]) for ref in pair]
     return tuple(jnp.concatenate([parts[0][k], parts[1][k]], 0) for k in range(2))
@@ -261,8 +266,9 @@
     mine = spot[CORE]
     held, beside, last, own = [whole(arrays[k : k + 2]) for k in range(0, 8, 2)]
     out[:, 128:, :] = jnp.zeros((16, 8, 128), jnp.float32)
-    lay(out, 2 * mine, dot(own, held))
-    lay(out, 2 * (1 - mine), dot(own, beside))
+    same, cross = dots(own, held, beside)
+    lay(out, 2 * mine, same)
+    lay(out, 2 * (1 - mine), cross)
     lay(out, 8, dot(last, own))
     out[10:12] = square[:2]
     out[14:16] = square[2:]
@@ -272,9 +278,10 @@
     *arrays, out = refs
     mine = spot[OWN]
     last_2, own, other, opposite, last_1 = [whole(arrays[k : k + 2]) for k in range(0, 10, 2)]
-    lay(out, 2 * mine, dot(last_2, own))
-    lay(out, 2 * (1 - mine), dot(last_2, other))
-    lay(out, 8, dot(last_2, opposite))
+    same, cross, across = dots(last_2, own, other, opposite)
+    lay(out, 2 * mine, same)
+    lay(out, 2 * (1 - mine), cross)
+    lay(out, 8, across)
     lay(out, 10, dot(last_1, other))
 
 

time: 127 us -> 127 us (level)
  no operation moved by 1% of the time
where the time goes in v7:
time: 127 us; the launch traced here: 125 us
  waiting for transfers between devices  43.7 us (34%)
  starting transfers between devices  35.8 us (28%)
  blocking collectives  24 us (19%)
  Pallas kernels  14.1 us (11%)
  local copies, waits for them, and re-layouts  3.56 us (3%)
  other arithmetic  2 us (2%)
  between operations  1.5 us (1%)
    all_to_all x1, blocking collectives, gathered(): blocks = lax.all_to_all(blocks, PLANE, 0, 0, tiled=True)  24 us
    all_to_all x1, waiting for transfers between devices, gathered(): blocks = lax.all_to_all(blocks, PLANE, 0, 0, tiled=True)  15.4 us
    pallas_call x8, Pallas kernels, call(): pl.pallas_call(ordered, out_shape=shape, in_specs=[SMEM] * len(scalars) +...  14.1 us
    ppermute x1, waiting for transfers between devices, body(): next_1 = [early[1], lax.ppermute(held[1], ('z', 'core'), DOWN_TURNED)]  9 us
    ppermute x2, waiting for transfers between devices, body(): got = [lax.ppermute(sent[k], ALL, routes(k)) for k in range(2)]  6.53 us
    ppermute x2, starting transfers between devices, body(): next_2 = [lax.ppermute(half, 'z', DOWN) for half in next_1]  6.38 us
    all_to_all x1, starting transfers between devices, gathered(): blocks = lax.all_to_all(blocks, PLANE, 0, 0, tiled=True)  4.96 us
    ppermute x2, starting transfers between devices, body(): got = [lax.ppermute(sent[k], ALL, routes(k)) for k in range(2)]  4.8 us
  transfers between devices with their start and end apart: 21, of which 10 were waited for; matrix products, arithmetic and copies ran while one was open for 2% of the time, Pallas kernels for 7%

profile of v7, /device:TPU:2, one launch (start us, length us, event | category | flops | bytes accessed | tf_op | source)
XLA Modules:
  0.0 124.6 jit_solution(10913168434399084072)
XLA Ops:
  0.6 0.0 copy-start.2
  0.6 0.0 copy-start.3
  0.7 1.2 fusion
  1.8 2.4 %collective-permute-start = (f32[4,64,256]{2,1,0:T(8,128)S(1)}, f32[4,64,256]{2,1,0:T(8,128)S(1)}, u32[]{:S(2)}, u32[]{:S(2)}) collective-permute-start(f32[4,64,256]{2,1,0:T(8,128)S(1)} %fusion), channel_id=1, source_target_pairs={{0,16},{16,0},{1,17},{17,1},{2,18},{18,2},{3,19},{19,3},{4,20},{20... | collective-permute-start | bytes 786440 | tf_op jit(solution)/shard_map/ppermute | solution.py:169
  4.2 1.1 slice_bitcast_fusion.1
  5.3 2.6 %collective-permute-start.1 = (f32[4,64,256]{2,1,0:T(8,128)S(1)}, f32[4,64,256]{2,1,0:T(8,128)S(1)}, u32[]{:S(2)}, u32[]{:S(2)}) collective-permute-start(f32[4,64,256]{2,1,0:T(8,128)S(1)} %get-tuple-element.52), channel_id=1, source_target_pairs={{0,32},{32,64},{64,96},{96,128},{128,160},{160,192},{192,224},{1,3... | collective-permute-start | bytes 786440 | tf_op jit(solution)/shard_map/ppermute | solution.py:170
  7.9 1.3 %collective-permute-start.2 = (f32[4,64,256]{2,1,0:T(8,128)S(1)}, f32[4,64,256]{2,1,0:T(8,128)S(1)}, u32[]{:S(2)}, u32[]{:S(2)}) collective-permute-start(f32[4,64,256]{2,1,0:T(8,128)S(1)} %get-tuple-element.51), channel_id=1, source_target_pairs={{32,0},{64,32},{96,64},{128,96},{160,128},{192,160},{224,192},{33,... | collective-permute-start | bytes 786440 | tf_op jit(solution)/shard_map/ppermute | solution.py:171
  9.2 0.1 copy.7
  9.3 0.1 select_reduce_fusion
  9.4 0.1 reshape.25.refs_1_
  9.5 0.1 stack.29.refs_0_
  9.6 0.5 collective-permute-done.refs_3_.refs_5_
  10.1 0.0 copy-done.2
  10.1 1.7 %copy-done = f32[4,4,9,4096]{3,1,2,0:T(4,128)S(1)} copy-done((f32[4,4,9,4096]{3,1,2,0:T(4,128)S(1)}, f32[4,4,9,4096]{3,1,2,0:T(4,128)}, u32[]{:S(2)}) %copy-start) | copy-done | bytes 2359320
  11.7 2.0 %shard_map.50 = (f32[8,64,256]{2,1,0:T(8,128)S(1)}, f32[8,64,256]{2,1,0:T(8,128)S(1)}) custom-call(s32[5]{0:T(128)S(1)} %stack.29.refs_0_, s32[144]{0:T(256)S(1)} %reshape.25.refs_1_, f32[16,64,256]{2,1,0:T(8,128)S(1)} %bitcast.33, f32[4,64,256]{2,1,0:T(8,128)S(1)} %collective-permute-done.refs_3_.refs_5_, f32[4,9,4,4096]{3,2,1,0:T(4,128)S(1)} %bitcast.26), custom_call_target="tpu_custom_call" | custom-call | flops 1 | bytes 1 | tf_op jit(solution)/shard_map/pallas_call | solution.py:40
  13.8 2.0 %collective-permute-start.4 = (f32[512,256]{1,0:T(8,128)S(1)}, f32[512,256]{1,0:T(8,128)S(1)}, u32[]{:S(2)}, u32[]{:S(2)}) collective-permute-start(f32[512,256]{1,0:T(8,128)S(1)} %bitcast.28), channel_id=1, source_target_pairs={{0,2},{2,4},{4,6},{6,8},{8,10},{10,12},{12,14},{14,0},{1,3},{3,5},... | collective-permute-start | bytes 1572872 | tf_op jit(solution)/shard_map/ppermute | solution.py:193
  15.8 2.5 %collective-permute-start.5 = (f32[512,256]{1,0:T(8,128)S(1)}, f32[512,256]{1,0:T(8,128)S(1)}, u32[]{:S(2)}, u32[]{:S(2)}) collective-permute-start(f32[512,256]{1,0:T(8,128)S(1)} %bitcast.29), channel_id=1, source_target_pairs={{0,15},{1,14},{2,1},{3,0},{4,2},{5,3},{6,4},{7,5},{8,6},{9,7},{10,... | collective-permute-start | bytes 1572872 | tf_op jit(solution)/shard_map/ppermute | solution.py:193
  18.3 0.0 collective-permute-done.1.refs_3_
  18.3 3.9 %collective-permute-done.2.refs_4_ = f32[4,64,256]{2,1,0:T(8,128)S(1)} collective-permute-done((f32[4,64,256]{2,1,0:T(8,128)S(1)}, f32[4,64,256]{2,1,0:T(8,128)S(1)}, u32[]{:S(2)}, u32[]{:S(2)}) %collective-permute-start.2) | collective-permute-done | bytes 262176 | tf_op jit(solution)/shard_map/ppermute | solution.py:171
  22.2 1.9 %collective-permute-start.3 = (f32[2,64,256]{2,1,0:T(8,128)S(1)}, f32[2,64,256]{2,1,0:T(8,128)S(1)}, u32[]{:S(2)}, u32[]{:S(2)}) collective-permute-start(f32[2,64,256]{2,1,0:T(8,128)S(1)} %maximum_select_fusion), channel_id=1, source_target_pairs={{0,16},{16,0},{1,17},{17,1},{2,18},{18,2},{3,19},{19,3},{4,20},{20... | collective-permute-start | bytes 393224 | tf_op jit(solution)/shard_map/ppermute | solution.py:198
  24.1 0.0 collective-permute-start.8
  24.1 3.2 %collective-permute-done.3.refs_6_ = f32[2,64,256]{2,1,0:T(8,128)S(1)} collective-permute-done((f32[2,64,256]{2,1,0:T(8,128)S(1)}, f32[2,64,256]{2,1,0:T(8,128)S(1)}, u32[]{:S(2)}, u32[]{:S(2)}) %collective-permute-start.3) | collective-permute-done | bytes 131104 | tf_op jit(solution)/shard_map/ppermute | solution.py:198
  27.2 2.2 %shard_map.51 = (f32[8,64,256]{2,1,0:T(8,128)S(1)}, f32[16,64,256]{2,1,0:T(8,128)}) custom-call(s32[5]{0:T(128)S(1)} %stack.29.refs_0_, s32[144]{0:T(256)S(1)} %reshape.25.refs_1_, f32[8,64,256]{2,1,0:T(8,128)S(1)} %get-tuple-element.29.refs_2_, f32[4,64,256]{2,1,0:T(8,128)S(1)} %collective-permute-done.1.refs_3_, ...), custom_call_target="tpu_custom_call" | custom-call | flops 1 | bytes 1 | tf_op jit(solution)/shard_map/pallas_call | solution.py:40
  29.4 1.2 collective-permute-done.4.refs_5_.refs_9_
  30.6 0.0 collective-permute-done.5.refs_7_.refs_3_
  30.7 0.0 collective-permute-start.9
  30.7 4.7 %collective-permute-start.7 = (f32[512,256]{1,0:T(8,128)S(1)}, f32[512,256]{1,0:T(8,128)S(1)}, u32[]{:S(2)}, u32[]{:S(2)}) collective-permute-start(f32[512,256]{1,0:T(8,128)S(1)} %bitcast.35), channel_id=1, source_target_pairs={{0,15},{1,14},{2,1},{3,0},{4,2},{5,3},{6,4},{7,5},{8,6},{9,7},{10,... | collective-permute-start | bytes 1572872 | tf_op jit(solution)/shard_map/ppermute | solution.py:393
  35.4 0.5 slice.54
  36.6 0.1 collective-permute-start.10
  36.7 0.0 collective-permute-done.8.refs_3_
  36.7 0.0 collective-permute-done.9.refs_4_
  36.7 1.4 %shard_map.52.refs_9_ = f32[4,136,128]{2,1,0:T(8,128)S(1)} custom-call(s32[5]{0:T(128)S(1)} %stack.29.refs_0_, f32[512,256]{1,0:T(8,128)S(1)} %bitcast.31, f32[512,256]{1,0:T(8,128)S(1)} %bitcast.37, f32[512,256]{1,0:T(8,128)S(1)} %collective-permute-done.8.refs_3_, f32[512,256]{1,0:T(8,128)S(1)} %collective-permute-done.9.refs_4_), custom_call_target="tpu_custom_call" | custom-call | flops 1 | bytes 1 | tf_op jit(solution)/shard_map/pallas_call | solution.py:40
  38.1 9.0 %collective-permute-done.7.refs_8_.refs_4_ = f32[512,256]{1,0:T(8,128)S(1)} collective-permute-done((f32[512,256]{1,0:T(8,128)S(1)}, f32[512,256]{1,0:T(8,128)S(1)}, u32[]{:S(2)}, u32[]{:S(2)}) %collective-permute-start.7) | collective-permute-done | bytes 524320 | tf_op jit(solution)/shard_map/ppermute | solution.py:393
  47.1 0.0 collective-permute-start.11
  47.1 0.5 collective-permute-start.13
  47.6 3.2 %collective-permute-start.14 = (f32[512,256]{1,0:T(8,128)S(1)}, f32[512,256]{1,0:T(8,128)}, u32[]{:S(2)}, u32[]{:S(2)}) collective-permute-start(f32[512,256]{1,0:T(8,128)S(1)} %collective-permute-done.5.refs_7_.refs_3_), channel_id=1, source_target_pairs={{0,14},{2,0},{4,2},{6,4},{8,6},{10,8},{12,10},{14,12},{1,15},{3,1}... | collective-permute-start | bytes 1572872 | tf_op jit(solution)/shard_map/ppermute | solution.py:416
  50.8 0.0 collective-permute-start.6
  50.8 1.0 collective-permute-done.10.refs_6_.refs_10_
  51.8 0.0 collective-permute-done.11.refs_6_
  51.8 3.0 %shard_map.53 = f32[16,136,128]{2,1,0:T(8,128)} custom-call(s32[5]{0:T(128)S(1)} %stack.29.refs_0_, f32[512,256]{1,0:T(8,128)S(1)} %bitcast.32, f32[512,256]{1,0:T(8,128)S(1)} %bitcast.38, f32[512,256]{1,0:T(8,128)S(1)} %collective-permute-done.8.refs_3_, f32[512,256]{1,0:T(8,128)S(1)} %collective-permute-done.9.refs_4_, ...), custom_call_target="tpu_custom_call" | custom-call | flops 1 | bytes 1 | tf_op jit(solution)/shard_map/pallas_call | solution.py:40
  54.8 0.0 collective-permute-start.12
  54.8 3.2 %collective-permute-start.15 = (f32[512,256]{1,0:T(8,128)S(1)}, f32[512,256]{1,0:T(8,128)}, u32[]{:S(2)}, u32[]{:S(2)}) collective-permute-start(f32[512,256]{1,0:T(8,128)S(1)} %collective-permute-done.7.refs_8_.refs_4_), channel_id=1, source_target_pairs={{0,14},{2,0},{4,2},{6,4},{8,6},{10,8},{12,10},{14,12},{1,15},{3,1}... | collective-permute-start | bytes 1572872 | tf_op jit(solution)/shard_map/ppermute | solution.py:416
  58.1 24.0 %conditional.1 = (f32[136,128]{1,0:T(8,128)S(1)}) conditional(s32[]{:T(128)} %convert_element_type.3, f32[16,136,128]{2,1,0:T(8,128)} %shard_map.53, f32[16,136,128]{2,1,0:T(8,128)} %shard_map.53), branch_computations={%region_1.2_spmd, %region_2.3_spmd} | conditional | flops 1 | bytes 2228233 | solution.py:417
  58.1 24.0 %all_to_all.9.refs_0_ = f32[16,136,128]{2,1,0:T(8,128)S(1)} all-to-all(f32[16,136,128]{2,1,0:T(8,128)} %param.1), channel_id=1, replica_groups=mesh['y'=4,'xh'=2,'xl'=2,'z'=8,'core'=2] {'y','xh','xl'}, dimensions={0} | all-to-all | bytes 2228224 | tf_op jit(solution)/shard_map/cond/branch_1_fun/all_to_all | solution.py:328
  82.1 0.1 branch_1_fun.1
  82.1 0.0 collective-permute-done.13.refs_5_
  82.1 0.0 collective-permute-done.14.refs_7_
  82.1 0.0 collective-permute-done.6.refs_1_
  82.1 0.0 collective-permute-done.12.refs_2_
  82.2 0.0 collective-permute-done.15.refs_8_
  82.2 4.5 %shard_map.54 = f32[16,128,128]{2,1,0:T(8,128)} custom-call(s32[5]{0:T(128)S(1)} %stack.29.refs_0_, f32[512,256]{1,0:T(8,128)} %collective-permute-done.6.refs_1_, f32[512,256]{1,0:T(8,128)} %collective-permute-done.12.refs_2_, f32[512,256]{1,0:T(8,128)S(1)} %collective-permute-done.5.refs_7_.refs_3_, f32[512,256]{1,0:T(8,128)S(1)} %collective-permute-done.7.refs_8_.refs_4_, ...), custom_call_target="tpu_custom_call" | custom-call | flops 1 | bytes 1 | tf_op jit(solution)/shard_map/pallas_call | solution.py:40
  86.6 5.0 %all-to-all-start.1 = ((f32[16,128,128]{2,1,0:T(8,128)}), f32[16,128,128]{2,1,0:T(8,128)S(1)}, u32[]{:S(2)}, u32[]{:S(2)}) async-start(f32[16,128,128]{2,1,0:T(8,128)} %shard_map.54), calls=%async_computation.1 | async-start | bytes 2097152 | tf_op jit(solution)/shard_map/all_to_all | solution.py:328
  91.6 0.3 collective-permute-start.17
  91.9 15.4 %all-to-all-done.1.refs_0_ = f32[16,128,128]{2,1,0:T(8,128)S(1)} async-done(((f32[16,128,128]{2,1,0:T(8,128)}), f32[16,128,128]{2,1,0:T(8,128)S(1)}, u32[]{:S(2)}, u32[]{:S(2)}) %all-to-all-start.1) | async-done | bytes 1048608 | tf_op jit(solution)/shard_map/all_to_all | solution.py:328
  107.3 0.1 shard_map.55.refs_1_
  107.4 1.4 %collective-permute-start.16 = (f32[128,128]{1,0:T(8,128)S(1)}, f32[128,128]{1,0:T(8,128)S(1)}, u32[]{:S(2)}, u32[]{:S(2)}) collective-permute-start(f32[128,128]{1,0:T(8,128)S(1)} %shard_map.55.refs_1_), channel_id=1, source_target_pairs={{0,16},{16,0},{1,17},{17,1},{2,18},{18,2},{3,19},{19,3},{4,20},{20... | collective-permute-start | bytes 196616 | tf_op jit(solution)/shard_map/ppermute | solution.py:432
  108.7 0.0 collective-permute-done.17.refs_4_
  108.7 3.0 %collective-permute-done.16.refs_2_ = f32[128,128]{1,0:T(8,128)S(1)} collective-permute-done((f32[128,128]{1,0:T(8,128)S(1)}, f32[128,128]{1,0:T(8,128)S(1)}, u32[]{:S(2)}, u32[]{:S(2)}) %collective-permute-start.16) | collective-permute-done | bytes 65568 | tf_op jit(solution)/shard_map/ppermute | solution.py:432
  111.7 0.8 shard_map.56
  112.5 1.9 %collective-permute-start.18 = (f32[128,256]{1,0:T(8,128)S(1)}, f32[128,256]{1,0:T(8,128)S(1)}, u32[]{:S(2)}, u32[]{:S(2)}) collective-permute-start(f32[128,256]{1,0:T(8,128)S(1)} %get-tuple-element.49), channel_id=1, source_target_pairs={{0,44},{1,2},{2,78},{3,37},{4,96},{5,71},{6,130},{7,105},{8,164},{... | collective-permute-start | bytes 393224 | tf_op jit(solution)/shard_map/ppermute | solution.py:436
  114.4 2.9 %collective-permute-start.19 = (f32[128,256]{1,0:T(8,128)S(1)}, f32[128,256]{1,0:T(8,128)S(1)}, u32[]{:S(2)}, u32[]{:S(2)}) collective-permute-start(f32[128,256]{1,0:T(8,128)S(1)} %get-tuple-element.50), channel_id=1, source_target_pairs={{0,3},{1,45},{2,36},{3,79},{4,70},{5,97},{6,104},{7,131},{8,138},{... | collective-permute-start | bytes 393224 | tf_op jit(solution)/shard_map/ppermute | solution.py:436
  117.3 6.3 %collective-permute-done.18 = f32[128,256]{1,0:T(8,128)S(1)} collective-permute-done((f32[128,256]{1,0:T(8,128)S(1)}, f32[128,256]{1,0:T(8,128)S(1)}, u32[]{:S(2)}, u32[]{:S(2)}) %collective-permute-start.18) | collective-permute-done | bytes 131104 | tf_op jit(solution)/shard_map/ppermute | solution.py:436
  123.6 0.2 collective-permute-done.19
  123.9 0.7 maximum_multiply_fusion
  (7 shorter events, 0.1 us)
Async XLA Ops:
  0.6 9.4 %copy-start.2 = (f32[4,4,64,256]{3,2,1,0:T(8,128)S(1)}, f32[4,4,64,256]{3,2,1,0:T(8,128)}, u32[]{:S(2)}) copy-start(f32[4,4,64,256]{3,2,1,0:T(8,128)} %param.5) | copy-start | bytes 3145732
  0.6 8.6 %copy-start.3 = (s32[4,4,9]{2,1,0:T(4,128)S(1)}, s32[4,4,9]{2,1,0:T(4,128)}, u32[]{:S(2)}) copy-start(s32[4,4,9]{2,1,0:T(4,128)} %param.6) | copy-start | bytes 1732
  1.8 8.3 %collective-permute-start = (f32[4,64,256]{2,1,0:T(8,128)S(1)}, f32[4,64,256]{2,1,0:T(8,128)S(1)}, u32[]{:S(2)}, u32[]{:S(2)}) collective-permute-start(f32[4,64,256]{2,1,0:T(8,128)S(1)} %fusion), channel_id=1, source_target_pairs={{0,16},{16,0},{1,17},{17,1},{2,18},{18,2},{3,19},{19,3},{4,20},{20... | collective-permute-start | bytes 786440 | tf_op jit(solution)/shard_map/ppermute | solution.py:169
  5.3 13.0 %collective-permute-start.1 = (f32[4,64,256]{2,1,0:T(8,128)S(1)}, f32[4,64,256]{2,1,0:T(8,128)S(1)}, u32[]{:S(2)}, u32[]{:S(2)}) collective-permute-start(f32[4,64,256]{2,1,0:T(8,128)S(1)} %get-tuple-element.52), channel_id=1, source_target_pairs={{0,32},{32,64},{64,96},{96,128},{128,160},{160,192},{192,224},{1,3... | collective-permute-start | bytes 786440 | tf_op jit(solution)/shard_map/ppermute | solution.py:170
  7.9 14.2 %collective-permute-start.2 = (f32[4,64,256]{2,1,0:T(8,128)S(1)}, f32[4,64,256]{2,1,0:T(8,128)S(1)}, u32[]{:S(2)}, u32[]{:S(2)}) collective-permute-start(f32[4,64,256]{2,1,0:T(8,128)S(1)} %get-tuple-element.51), channel_id=1, source_target_pairs={{32,0},{64,32},{96,64},{128,96},{160,128},{192,160},{224,192},{33,... | collective-permute-start | bytes 786440 | tf_op jit(solution)/shard_map/ppermute | solution.py:171
  10.1 1.7 %copy-start = (f32[4,4,9,4096]{3,1,2,0:T(4,128)S(1)}, f32[4,4,9,4096]{3,1,2,0:T(4,128)}, u32[]{:S(2)}) copy-start(f32[4,4,9,4096]{3,1,2,0:T(4,128)} %param.7) | copy-start | bytes 7077892
  11.7 15.5 %copy-start.1 = (f32[4,4,9,4096]{3,1,2,0:T(4,128)S(1)}, f32[4,4,9,4096]{3,1,2,0:T(4,128)}, u32[]{:S(2)}) copy-start(f32[4,4,9,4096]{3,1,2,0:T(4,128)} %param.7) | copy-start | bytes 7077892
  13.8 16.9 %collective-permute-start.4 = (f32[512,256]{1,0:T(8,128)S(1)}, f32[512,256]{1,0:T(8,128)S(1)}, u32[]{:S(2)}, u32[]{:S(2)}) collective-permute-start(f32[512,256]{1,0:T(8,128)S(1)} %bitcast.28), channel_id=1, source_target_pairs={{0,2},{2,4},{4,6},{6,8},{8,10},{10,12},{12,14},{14,0},{1,3},{3,5},... | collective-permute-start | bytes 1572872 | tf_op jit(solution)/shard_map/ppermute | solution.py:193
  15.8 14.9 %collective-permute-start.5 = (f32[512,256]{1,0:T(8,128)S(1)}, f32[512,256]{1,0:T(8,128)S(1)}, u32[]{:S(2)}, u32[]{:S(2)}) collective-permute-start(f32[512,256]{1,0:T(8,128)S(1)} %bitcast.29), channel_id=1, source_target_pairs={{0,15},{1,14},{2,1},{3,0},{4,2},{5,3},{6,4},{7,5},{8,6},{9,7},{10,... | collective-permute-start | bytes 1572872 | tf_op jit(solution)/shard_map/ppermute | solution.py:193
  22.2 5.1 %collective-permute-start.3 = (f32[2,64,256]{2,1,0:T(8,128)S(1)}, f32[2,64,256]{2,1,0:T(8,128)S(1)}, u32[]{:S(2)}, u32[]{:S(2)}) collective-permute-start(f32[2,64,256]{2,1,0:T(8,128)S(1)} %maximum_select_fusion), channel_id=1, source_target_pairs={{0,16},{16,0},{1,17},{17,1},{2,18},{18,2},{3,19},{19,3},{4,20},{20... | collective-permute-start | bytes 393224 | tf_op jit(solution)/shard_map/ppermute | solution.py:198
  24.1 12.6 %collective-permute-start.8 = (f32[512,256]{1,0:T(8,128)S(1)}, f32[512,256]{1,0:T(8,128)S(1)}, u32[]{:S(2)}, u32[]{:S(2)}) collective-permute-start(f32[512,256]{1,0:T(8,128)S(1)} %bitcast.30), channel_id=1, source_target_pairs={{0,1},{1,0},{2,3},{3,2},{4,5},{5,4},{6,7},{7,6},{8,9},{9,8},{10,11... | collective-permute-start | bytes 1572872 | tf_op jit(solution)/shard_map/ppermute | solution.py:395
  30.7 6.0 %collective-permute-start.9 = (f32[512,256]{1,0:T(8,128)S(1)}, f32[512,256]{1,0:T(8,128)S(1)}, u32[]{:S(2)}, u32[]{:S(2)}) collective-permute-start(f32[512,256]{1,0:T(8,128)S(1)} %bitcast.34), channel_id=1, source_target_pairs={{0,1},{1,0},{2,3},{3,2},{4,5},{5,4},{6,7},{7,6},{8,9},{9,8},{10,11... | collective-permute-start | bytes 1572872 | tf_op jit(solution)/shard_map/ppermute | solution.py:395
  30.7 16.4 %collective-permute-start.7 = (f32[512,256]{1,0:T(8,128)S(1)}, f32[512,256]{1,0:T(8,128)S(1)}, u32[]{:S(2)}, u32[]{:S(2)}) collective-permute-start(f32[512,256]{1,0:T(8,128)S(1)} %bitcast.35), channel_id=1, source_target_pairs={{0,15},{1,14},{2,1},{3,0},{4,2},{5,3},{6,4},{7,5},{8,6},{9,7},{10,... | collective-permute-start | bytes 1572872 | tf_op jit(solution)/shard_map/ppermute | solution.py:393
  36.6 15.2 %collective-permute-start.10 = (f32[512,256]{1,0:T(8,128)S(1)}, f32[512,256]{1,0:T(8,128)S(1)}, u32[]{:S(2)}, u32[]{:S(2)}) collective-permute-start(f32[512,256]{1,0:T(8,128)S(1)} %bitcast.36), channel_id=1, source_target_pairs={{0,2},{2,4},{4,6},{6,8},{8,10},{10,12},{12,14},{14,0},{1,3},{3,5},... | collective-permute-start | bytes 1572872 | tf_op jit(solution)/shard_map/ppermute | solution.py:394
  47.1 4.7 %collective-permute-start.11 = (f32[512,256]{1,0:T(8,128)S(1)}, f32[512,256]{1,0:T(8,128)S(1)}, u32[]{:S(2)}, u32[]{:S(2)}) collective-permute-start(f32[512,256]{1,0:T(8,128)S(1)} %collective-permute-done.7.refs_8_.refs_4_), channel_id=1, source_target_pairs={{0,1},{1,0},{2,3},{3,2},{4,5},{5,4},{6,7},{7,6},{8,9},{9,8},{10,11... | collective-permute-start | bytes 1572872 | tf_op jit(solution)/shard_map/ppermute | solution.py:399
  47.1 35.0 %collective-permute-start.13 = (f32[512,256]{1,0:T(8,128)S(1)}, f32[512,256]{1,0:T(8,128)S(1)}, u32[]{:S(2)}, u32[]{:S(2)}) collective-permute-start(f32[512,256]{1,0:T(8,128)S(1)} %collective-permute-done.5.refs_7_.refs_3_), channel_id=1, source_target_pairs={{0,1},{1,0},{2,3},{3,2},{4,5},{5,4},{6,7},{7,6},{8,9},{9,8},{10,11... | collective-permute-start | bytes 1572872 | tf_op jit(solution)/shard_map/ppermute | solution.py:399
  47.6 34.5 %collective-permute-start.14 = (f32[512,256]{1,0:T(8,128)S(1)}, f32[512,256]{1,0:T(8,128)}, u32[]{:S(2)}, u32[]{:S(2)}) collective-permute-start(f32[512,256]{1,0:T(8,128)S(1)} %collective-permute-done.5.refs_7_.refs_3_), channel_id=1, source_target_pairs={{0,14},{2,0},{4,2},{6,4},{8,6},{10,8},{12,10},{14,12},{1,15},{3,1}... | collective-permute-start | bytes 1572872 | tf_op jit(solution)/shard_map/ppermute | solution.py:416
  50.8 31.3 %collective-permute-start.6 = (f32[512,256]{1,0:T(8,128)S(1)}, f32[512,256]{1,0:T(8,128)}, u32[]{:S(2)}, u32[]{:S(2)}) collective-permute-start(f32[512,256]{1,0:T(8,128)S(1)} %collective-permute-done.4.refs_5_.refs_9_), channel_id=1, source_target_pairs={{0,2},{2,4},{4,6},{6,8},{8,10},{10,12},{12,14},{14,0},{1,3},{3,5},... | collective-permute-start | bytes 1572872 | tf_op jit(solution)/shard_map/ppermute | solution.py:415
  54.8 27.3 %collective-permute-start.12 = (f32[512,256]{1,0:T(8,128)S(1)}, f32[512,256]{1,0:T(8,128)}, u32[]{:S(2)}, u32[]{:S(2)}) collective-permute-start(f32[512,256]{1,0:T(8,128)S(1)} %collective-permute-done.10.refs_6_.refs_10_), channel_id=1, source_target_pairs={{0,2},{2,4},{4,6},{6,8},{8,10},{10,12},{12,14},{14,0},{1,3},{3,5},... | collective-permute-start | bytes 1572872 | tf_op jit(solution)/shard_map/ppermute | solution.py:415
  54.8 27.3 %collective-permute-start.15 = (f32[512,256]{1,0:T(8,128)S(1)}, f32[512,256]{1,0:T(8,128)}, u32[]{:S(2)}, u32[]{:S(2)}) collective-permute-start(f32[512,256]{1,0:T(8,128)S(1)} %collective-permute-done.7.refs_8_.refs_4_), channel_id=1, source_target_pairs={{0,14},{2,0},{4,2},{6,4},{8,6},{10,8},{12,10},{14,12},{1,15},{3,1}... | collective-permute-start | bytes 1572872 | tf_op jit(solution)/shard_map/ppermute | solution.py:416
  86.6 20.7 %all-to-all-start.1 = ((f32[16,128,128]{2,1,0:T(8,128)}), f32[16,128,128]{2,1,0:T(8,128)S(1)}, u32[]{:S(2)}, u32[]{:S(2)}) async-start(f32[16,128,128]{2,1,0:T(8,128)} %shard_map.54), calls=%async_computation.1 | async-start | bytes 2097152 | tf_op jit(solution)/shard_map/all_to_all | solution.py:328
  91.6 17.1 %collective-permute-start.17 = (f32[136,128]{1,0:T(8,128)S(1)}, f32[136,128]{1,0:T(8,128)S(1)}, u32[]{:S(2)}, u32[]{:S(2)}) collective-permute-start(f32[136,128]{1,0:T(8,128)S(1)} %get-tuple-element.63.refs_11_.refs_3_), channel_id=1, source_target_pairs={{0,16},{16,0},{1,17},{17,1},{2,18},{18,2},{3,19},{19,3},{4,20},{20... | collective-permute-start | bytes 208904 | tf_op jit(solution)/shard_map/ppermute | solution.py:430
  107.4 4.4 %collective-permute-start.16 = (f32[128,128]{1,0:T(8,128)S(1)}, f32[128,128]{1,0:T(8,128)S(1)}, u32[]{:S(2)}, u32[]{:S(2)}) collective-permute-start(f32[128,128]{1,0:T(8,128)S(1)} %shard_map.55.refs_1_), channel_id=1, source_target_pairs={{0,16},{16,0},{1,17},{17,1},{2,18},{18,2},{3,19},{19,3},{4,20},{20... | collective-permute-start | bytes 196616 | tf_op jit(solution)/shard_map/ppermute | solution.py:432
  112.5 11.1 %collective-permute-start.18 = (f32[128,256]{1,0:T(8,128)S(1)}, f32[128,256]{1,0:T(8,128)S(1)}, u32[]{:S(2)}, u32[]{:S(2)}) collective-permute-start(f32[128,256]{1,0:T(8,128)S(1)} %get-tuple-element.49), channel_id=1, source_target_pairs={{0,44},{1,2},{2,78},{3,37},{4,96},{5,71},{6,130},{7,105},{8,164},{... | collective-permute-start | bytes 393224 | tf_op jit(solution)/shard_map/ppermute | solution.py:436
  114.4 9.4 %collective-permute-start.19 = (f32[128,256]{1,0:T(8,128)S(1)}, f32[128,256]{1,0:T(8,128)S(1)}, u32[]{:S(2)}, u32[]{:S(2)}) collective-permute-start(f32[128,256]{1,0:T(8,128)S(1)} %get-tuple-element.50), channel_id=1, source_target_pairs={{0,3},{1,45},{2,36},{3,79},{4,70},{5,97},{6,104},{7,131},{8,138},{... | collective-permute-start | bytes 393224 | tf_op jit(solution)/shard_map/ppermute | solution.py:436
